TPU v7x, 256 devices: a whole 4x4x8 slice. The times are simulated.
256 devices in a mesh: row: 32 (over z, x_lo, core), col: 8 (over x_hi, y).
Axes of the slice: x: 4 (x_hi: 2, x_lo: 2; x = x_hi * 2 + x_lo), y: 4, z: 8, core: 2. Of those that a mesh axis runs over, the one named last changes fastest.
Arguments:
- queries: bfloat16 [1, 128, 128, 1536], P(None, 'row', 'col'), may hold values from -180 to 180
- key_tokens: bfloat16 [1, 128, 128, 1536], P(None, 'row', 'col'), may hold values from -4 to 4
- values: bfloat16 [1, 128, 128, 1536], P(None, 'row', 'col'), may hold values from -6 to 6
- position_bias: float32 [24, 49], replicated, may hold values from -4 to 4
- out_weight: bfloat16 [1536, 1536], P('col', 'row'), may hold values from -0.15625 to 0.15625
Outputs:
- projected: bfloat16 [1, 128, 128, 1536], P(None, 'row', 'col')
All inputs are finite; a program needn't handle non-finite values.
Results may differ from a plain program's by a relative error of at most 0.0057.
Values may be sent and summed in bfloat16 or wider, within the bound.
No kernel may reach another device: no remote copies, remote signals or barrier semaphores. Data moves between devices by JAX's collectives and lax.ppermute only.
A program may use at most 64 MiB of HBM per device.

v0:
```python
import math

import jax
import jax.numpy as jnp
from jax import lax
from jax.sharding import PartitionSpec as P


def extended_2(block, sides, width):
    for axis, dim in sides:
        count = lax.axis_size(axis)
        forward = [(i, i + 1) for i in range(count - 1)]
        backward = [(target, source) for source, target in forward]
        low = lax.ppermute(
            lax.slice_in_dim(block, block.shape[dim] - width, None, axis=dim), axis, forward
        )
        high = lax.ppermute(lax.slice_in_dim(block, 0, width, axis=dim), axis, backward)
        block = jnp.concatenate([low, block, high], axis=dim)
    return block


def shards(queries, key_tokens, values, position_bias, out_weight):
    images = queries.shape[0]
    band_rows = queries.shape[1]
    strip_cols = queries.shape[2]
    model_width = queries.shape[3]
    head_count = position_bias.shape[0]
    head_size = model_width // head_count
    height = band_rows * lax.axis_size("row")
    breadth = strip_cols * lax.axis_size("col")
    stacked = jnp.stack([key_tokens, values], 0)
    extended = extended_2(stacked, (("row", 2), ("col", 3)), 3)
    key_ext = extended[0]
    value_ext = extended[1]
    query_heads = queries.reshape(images, band_rows, strip_cols, head_count, head_size)
    global_rows = lax.axis_index("row") * band_rows + jnp.arange(band_rows)
    global_cols = lax.axis_index("col") * strip_cols + jnp.arange(strip_cols)
    offsets = jnp.arange(7) - 3
    rows_inside = (global_rows[None, :] + offsets[:, None] >= 0) & (
        global_rows[None, :] + offsets[:, None] < height
    )
    cols_inside = (global_cols[None, :] + offsets[:, None] >= 0) & (
        global_cols[None, :] + offsets[:, None] < breadth
    )
    inside = (rows_inside[:, None, :, None] & cols_inside[None, :, None, :]).reshape(
        49, 1, band_rows, strip_cols, 1
    )
    score_scale = 1.0 / math.sqrt(head_size)
    row_steps = jnp.arange(7, dtype=jnp.int32)

    def score_step(carry, row_off):
        band_keys = lax.dynamic_slice_in_dim(key_ext, row_off, band_rows, 1)
        row_scores = []
        for col_off in range(7):
            window = band_keys[:, :, col_off : col_off + strip_cols].reshape(
                images, band_rows, strip_cols, head_count, head_size
            )
            row_scores.append(
                jnp.einsum(
                    "ibshd,ibshd->ibsh", query_heads, window, preferred_element_type=jnp.float32
                )
            )
        return (carry, jnp.stack(row_scores, 0))

    unused, score_grid = lax.scan(score_step, jnp.zeros((), jnp.float32), row_steps)
    scores = score_grid.reshape(49, images, band_rows, strip_cols, head_count) * score_scale
    scores = scores + jnp.transpose(position_bias)[:, None, None, None, :]
    scores = jnp.where(inside, scores, -jnp.inf)
    attention = jax.nn.softmax(scores, axis=0).astype(jnp.bfloat16)
    attention_grid = attention.reshape(7, 7, images, band_rows, strip_cols, head_count)

    def value_step(summed, items):
        row_off, weights = items
        band_values = lax.dynamic_slice_in_dim(value_ext, row_off, band_rows, 1)
        row_total = None
        for col_off in range(7):
            window = band_values[:, :, col_off : col_off + strip_cols].reshape(
                images, band_rows, strip_cols, head_count, head_size
            )
            term = weights[col_off].astype(jnp.float32)[..., None] * window.astype(jnp.float32)
            row_total = term if row_total is None else row_total + term
        return (summed + row_total, None)

    initial_sum = jnp.zeros((images, band_rows, strip_cols, head_count, head_size), jnp.float32)
    summed, unused_out = lax.scan(value_step, initial_sum, (row_steps, attention_grid))
    mixed_heads = summed.astype(jnp.bfloat16).reshape(images * band_rows * strip_cols, model_width)
    tall_weight = lax.all_gather(out_weight, "col", axis=0, tiled=True)
    result = jnp.dot(
        mixed_heads,
        lax.all_gather(tall_weight, "row", axis=1, tiled=True),
        preferred_element_type=jnp.float32,
    )
    return result.astype(jnp.bfloat16).reshape(images, band_rows, strip_cols, model_width)


def solution(mesh):
    in_specs = (
        P(None, "row", "col", None),
        P(None, "row", "col", None),
        P(None, "row", "col", None),
        P(),
        P("col", "row"),
    )
    out_specs = P(None, "row", "col", None)
    return jax.shard_map(shards, mesh=mesh, in_specs=in_specs, out_specs=out_specs, check_vma=False)
```

profile of v0, /device:TPU:248, one launch (start us, length us, event | category | flops | bytes accessed | tf_op | source)
XLA Modules:
  0.0 312.8 jit_solution(8154622619189542940)
XLA Ops:
  9.8 4.5 %collective-permute-start.1 = (bf16[2,1,3,16,1536]{4,3,2,1,0:T(8,128)(2,1)S(1)}, bf16[2,1,3,16,1536]{4,3,2,1,0:T(8,128)(2,1)S(1)}, u32[]{:S(2)}, u32[]{:S(2)}) collective-permute-start(bf16[2,1,3,16,1536]{4,3,2,1,0:T(8,128)(2,1)S(1)} %get-tuple-element.132), channel_id=1, source_target_pairs={{8,0},{16,8},{24,16},{32,24},{40,32},{48,40},{56,48},{64,56},{72,6... | collective-permute-start | bytes 884744 | tf_op jit(solution)/shard_map/ppermute | solution.py:17
  14.3 34.5 %all-gather = bf16[8,192,48]{1,2,0:T(8,128)(2,1)S(1)} all-gather(bf16[1,192,48]{1,2,0:T(8,128)(2,1)} %bitcast.136), channel_id=1, replica_groups=mesh['row'=32,'col'=8] {'col'}, dimensions={0}, use_global_device_ids=true | all-gather | bytes 165888 | tf_op jit(solution)/shard_map/all_gather | solution.py:87
  51.3 4.6 %collective-permute-start.2 = (bf16[2,1,10,3,1536]{4,3,2,1,0:T(4,128)(2,1)S(1)}, bf16[2,1,10,3,1536]{4,3,2,1,0:T(4,128)(2,1)S(1)}, u32[]{:S(2)}, u32[]{:S(2)}) collective-permute-start(bf16[2,1,10,3,1536]{4,3,2,1,0:T(4,128)(2,1)S(1)} %get-tuple-element.129), channel_id=1, source_target_pairs={{0,1},{1,2},{2,3},{3,4},{4,5},{5,6},{6,7},{8,9},{9,10},{10,11},{11... | collective-permute-start | bytes 552968 | tf_op jit(solution)/shard_map/ppermute | solution.py:14
  59.7 9.8 %collective-permute-done.3 = bf16[2,1,10,3,1536]{4,3,2,1,0:T(4,128)(2,1)S(1)} collective-permute-done((bf16[2,1,10,3,1536]{4,3,2,1,0:T(4,128)(2,1)S(1)}, bf16[2,1,10,3,1536]{4,3,2,1,0:T(4,128)(2,1)S(1)}, u32[]{:S(2)}, u32[]{:S(2)}) %collective-permute-start.3) | collective-permute-done | bytes 184352 | tf_op jit(solution)/shard_map/ppermute | solution.py:17
  70.3 93.0 %while.21 = (s32[]{:T(128)}, f32[7,7,1,4,16,24]{5,4,3,2,1,0:T(8,128)}, s32[7]{0:T(128)S(1)}, bf16[1,10,22,1536]{3,2,1,0:T(8,128)(2,1)S(1)}, bf16[1,4,16,24,64]{4...) while((s32[]{:T(128)}, ...), condition=%wide.region_1.2_spmd, body=%wide.region_0.1_spmd.sunk | while | flops 2151947 | bytes 7826199 | solution.py:65
  76.1 2.0 reshape.511
  80.0 2.7 fusion.23
  89.4 2.0 reshape.511
  93.3 2.7 fusion.23
  102.7 2.0 reshape.511
  106.6 2.8 fusion.23
  116.0 2.0 reshape.511
  119.9 2.7 fusion.23
  129.3 2.0 reshape.511
  133.2 2.7 fusion.23
  146.5 2.7 fusion.23
  159.8 2.7 fusion.23
  166.8 2.6 divide_convert_fusion
  169.4 130.5 %while.22 = (s32[]{:T(128)}, f32[1,4,16,24,64]{4,3,2,1,0:T(8,128)}, bf16[7,7,1,4,16,24]{5,4,3,2,1,0:T(8,128)(2,1)}, s32[7]{0:T(128)S(1)}, bf16[1,10,22,1536]{3,2...) while((s32[]{:T(128)}, f32[1,4,16,24,64]{4,3,2,1,0:T(8,128)}, ...), condition=%wide.region_5.6_spmd.clone, body=%wide.region_4.5_spmd.clone.sunk | while | flops 2173452 | bytes 13280573 | solution.py:85
  175.0 2.1 reshape.516
  177.1 2.1 reshape.517
  179.2 2.1 reshape.518
  183.3 4.7 %select_add_fusion.2 = f32[1,4,16,24,64]{4,3,2,1,0:T(8,128)} fusion(f32[1,4,16,24,64]{4,3,2,1,0:T(8,128)} %get-tuple-element.308, f32[1,4,16,24,64]{4,3,2,1,0:T(8,128)S(1)} %reshape.513, f32[1,4,16,24,64]{4,3,2,1,0:T(8,128)S(1)} %reshape.514, f32[1,4,16,24,64]{4,3,2,1,0:T(8,128)S(1)} %reshape.515, f32[1,4,16,24,64]{4,3,2,1,0:T(8,128)} %reshape.516, ...), kind=kLoop, calls=%fused_computation.clone.1 | loop fusion | flops 1474560 | bytes 3581953 | tf_op jit(solution)/shard_map/while/body/eval_jaxpr/add | solution.py:82
  193.5 2.1 reshape.516
  195.6 2.1 reshape.517
  197.7 2.1 reshape.518
  201.8 4.8 %select_add_fusion.2 = f32[1,4,16,24,64]{4,3,2,1,0:T(8,128)} fusion(f32[1,4,16,24,64]{4,3,2,1,0:T(8,128)} %get-tuple-element.308, f32[1,4,16,24,64]{4,3,2,1,0:T(8,128)S(1)} %reshape.513, f32[1,4,16,24,64]{4,3,2,1,0:T(8,128)S(1)} %reshape.514, f32[1,4,16,24,64]{4,3,2,1,0:T(8,128)S(1)} %reshape.515, f32[1,4,16,24,64]{4,3,2,1,0:T(8,128)} %reshape.516, ...), kind=kLoop, calls=%fused_computation.clone.1 | loop fusion | flops 1474560 | bytes 3581953 | tf_op jit(solution)/shard_map/while/body/eval_jaxpr/add | solution.py:82
  212.2 2.1 reshape.516
  214.2 2.1 reshape.517
  216.4 2.1 reshape.518
  220.5 4.8 %select_add_fusion.2 = f32[1,4,16,24,64]{4,3,2,1,0:T(8,128)} fusion(f32[1,4,16,24,64]{4,3,2,1,0:T(8,128)} %get-tuple-element.308, f32[1,4,16,24,64]{4,3,2,1,0:T(8,128)S(1)} %reshape.513, f32[1,4,16,24,64]{4,3,2,1,0:T(8,128)S(1)} %reshape.514, f32[1,4,16,24,64]{4,3,2,1,0:T(8,128)S(1)} %reshape.515, f32[1,4,16,24,64]{4,3,2,1,0:T(8,128)} %reshape.516, ...), kind=kLoop, calls=%fused_computation.clone.1 | loop fusion | flops 1474560 | bytes 3581953 | tf_op jit(solution)/shard_map/while/body/eval_jaxpr/add | solution.py:82
  230.8 2.1 reshape.516
  232.9 2.1 reshape.517
  235.0 2.1 reshape.518
  239.1 4.8 %select_add_fusion.2 = f32[1,4,16,24,64]{4,3,2,1,0:T(8,128)} fusion(f32[1,4,16,24,64]{4,3,2,1,0:T(8,128)} %get-tuple-element.308, f32[1,4,16,24,64]{4,3,2,1,0:T(8,128)S(1)} %reshape.513, f32[1,4,16,24,64]{4,3,2,1,0:T(8,128)S(1)} %reshape.514, f32[1,4,16,24,64]{4,3,2,1,0:T(8,128)S(1)} %reshape.515, f32[1,4,16,24,64]{4,3,2,1,0:T(8,128)} %reshape.516, ...), kind=kLoop, calls=%fused_computation.clone.1 | loop fusion | flops 1474560 | bytes 3581953 | tf_op jit(solution)/shard_map/while/body/eval_jaxpr/add | solution.py:82
  249.5 2.1 reshape.516
  251.5 2.1 reshape.517
  253.7 2.1 reshape.518
  257.8 4.8 %select_add_fusion.2 = f32[1,4,16,24,64]{4,3,2,1,0:T(8,128)} fusion(f32[1,4,16,24,64]{4,3,2,1,0:T(8,128)} %get-tuple-element.308, f32[1,4,16,24,64]{4,3,2,1,0:T(8,128)S(1)} %reshape.513, f32[1,4,16,24,64]{4,3,2,1,0:T(8,128)S(1)} %reshape.514, f32[1,4,16,24,64]{4,3,2,1,0:T(8,128)S(1)} %reshape.515, f32[1,4,16,24,64]{4,3,2,1,0:T(8,128)} %reshape.516, ...), kind=kLoop, calls=%fused_computation.clone.1 | loop fusion | flops 1474560 | bytes 3581953 | tf_op jit(solution)/shard_map/while/body/eval_jaxpr/add | solution.py:82
  268.1 2.1 reshape.516
  270.2 2.1 reshape.517
  272.3 2.1 reshape.518
  276.4 4.8 %select_add_fusion.2 = f32[1,4,16,24,64]{4,3,2,1,0:T(8,128)} fusion(f32[1,4,16,24,64]{4,3,2,1,0:T(8,128)} %get-tuple-element.308, f32[1,4,16,24,64]{4,3,2,1,0:T(8,128)S(1)} %reshape.513, f32[1,4,16,24,64]{4,3,2,1,0:T(8,128)S(1)} %reshape.514, f32[1,4,16,24,64]{4,3,2,1,0:T(8,128)S(1)} %reshape.515, f32[1,4,16,24,64]{4,3,2,1,0:T(8,128)} %reshape.516, ...), kind=kLoop, calls=%fused_computation.clone.1 | loop fusion | flops 1474560 | bytes 3581953 | tf_op jit(solution)/shard_map/while/body/eval_jaxpr/add | solution.py:82
  286.8 2.1 reshape.516
  288.9 2.1 reshape.517
  291.0 2.1 reshape.518
  295.1 4.8 %select_add_fusion.2 = f32[1,4,16,24,64]{4,3,2,1,0:T(8,128)} fusion(f32[1,4,16,24,64]{4,3,2,1,0:T(8,128)} %get-tuple-element.308, f32[1,4,16,24,64]{4,3,2,1,0:T(8,128)S(1)} %reshape.513, f32[1,4,16,24,64]{4,3,2,1,0:T(8,128)S(1)} %reshape.514, f32[1,4,16,24,64]{4,3,2,1,0:T(8,128)S(1)} %reshape.515, f32[1,4,16,24,64]{4,3,2,1,0:T(8,128)} %reshape.516, ...), kind=kLoop, calls=%fused_computation.clone.1 | loop fusion | flops 1474560 | bytes 3581953 | tf_op jit(solution)/shard_map/while/body/eval_jaxpr/add | solution.py:82
  301.4 4.5 %convolution_convert_fusion = bf16[64,1536]{1,0:T(8,128)(2,1)} fusion(bf16[64,1536]{1,0:T(8,128)(2,1)S(1)} %reshape.439, bf16[1536,1536]{0,1:T(8,128)(2,1)} %all-gather.3.cloned.1.call-done), kind=kOutput, calls=%fused_computation.51 | convolution fusion | flops 302088192 | bytes 5111808 | tf_op jit(solution)/shard_map/dot_general | solution.py:88
  (202 shorter events, 103.9 us)
Async XLA Ops:
  6.5 44.6 %copy-start = (bf16[1,4,16,1536]{3,2,1,0:T(8,128)(2,1)S(1)}, bf16[1,4,16,1536]{3,2,1,0:T(8,128)(2,1)}, u32[]{:S(2)}) copy-start(bf16[1,4,16,1536]{3,2,1,0:T(8,128)(2,1)} %param.10) | copy-start | bytes 589828
  6.5 44.6 %copy-start.1 = (bf16[1,4,16,1536]{3,2,1,0:T(8,128)(2,1)S(1)}, bf16[1,4,16,1536]{3,2,1,0:T(8,128)(2,1)}, u32[]{:S(2)}) copy-start(bf16[1,4,16,1536]{3,2,1,0:T(8,128)(2,1)} %param.11) | copy-start | bytes 589828
  6.5 43.3 %copy-start.2 = (bf16[1,4,16,1536]{3,2,1,0:T(8,128)(2,1)S(1)}, bf16[1,4,16,1536]{3,2,1,0:T(8,128)(2,1)}, u32[]{:S(2)}) copy-start(bf16[1,4,16,1536]{3,2,1,0:T(8,128)(2,1)} %param.9) | copy-start | bytes 589828
  6.5 44.3 %copy-start.3 = (f32[24,49]{1,0:T(8,128)S(1)}, f32[24,49]{1,0:T(8,128)}, u32[]{:S(2)}) copy-start(f32[24,49]{1,0:T(8,128)} %param.12) | copy-start | bytes 14116
  6.5 294.8 %all-gather.3.cloned.1.call-start = ((), (), s32[]{:S(2)}) async-start(), calls=%async_computation | async-start | bytes 4866048 | tf_op jit(solution)/shard_map/all_gather | solution.py:90
  7.8 43.2 %collective-permute-start = (bf16[2,1,3,16,1536]{4,3,2,1,0:T(8,128)(2,1)S(1)}, bf16[2,1,3,16,1536]{4,3,2,1,0:T(8,128)(2,1)S(1)}, u32[]{:S(2)}, u32[]{:S(2)}) collective-permute-start(bf16[2,1,3,16,1536]{4,3,2,1,0:T(8,128)(2,1)S(1)} %get-tuple-element.131), channel_id=1, source_target_pairs={{0,8},{8,16},{16,24},{24,32},{32,40},{40,48},{48,56},{56,64},{64,7... | collective-permute-start | bytes 884744 | tf_op jit(solution)/shard_map/ppermute | solution.py:14
  9.8 41.3 %collective-permute-start.1 = (bf16[2,1,3,16,1536]{4,3,2,1,0:T(8,128)(2,1)S(1)}, bf16[2,1,3,16,1536]{4,3,2,1,0:T(8,128)(2,1)S(1)}, u32[]{:S(2)}, u32[]{:S(2)}) collective-permute-start(bf16[2,1,3,16,1536]{4,3,2,1,0:T(8,128)(2,1)S(1)} %get-tuple-element.132), channel_id=1, source_target_pairs={{8,0},{16,8},{24,16},{32,24},{40,32},{48,40},{56,48},{64,56},{72,6... | collective-permute-start | bytes 884744 | tf_op jit(solution)/shard_map/ppermute | solution.py:17
  51.3 8.3 %collective-permute-start.2 = (bf16[2,1,10,3,1536]{4,3,2,1,0:T(4,128)(2,1)S(1)}, bf16[2,1,10,3,1536]{4,3,2,1,0:T(4,128)(2,1)S(1)}, u32[]{:S(2)}, u32[]{:S(2)}) collective-permute-start(bf16[2,1,10,3,1536]{4,3,2,1,0:T(4,128)(2,1)S(1)} %get-tuple-element.129), channel_id=1, source_target_pairs={{0,1},{1,2},{2,3},{3,4},{4,5},{5,6},{6,7},{8,9},{9,10},{10,11},{11... | collective-permute-start | bytes 552968 | tf_op jit(solution)/shard_map/ppermute | solution.py:14
  56.0 13.5 %collective-permute-start.3 = (bf16[2,1,10,3,1536]{4,3,2,1,0:T(4,128)(2,1)S(1)}, bf16[2,1,10,3,1536]{4,3,2,1,0:T(4,128)(2,1)S(1)}, u32[]{:S(2)}, u32[]{:S(2)}) collective-permute-start(bf16[2,1,10,3,1536]{4,3,2,1,0:T(4,128)(2,1)S(1)} %get-tuple-element.130), channel_id=1, source_target_pairs={{1,0},{2,1},{3,2},{4,3},{5,4},{6,5},{7,6},{9,8},{10,9},{11,10},{12... | collective-permute-start | bytes 552968 | tf_op jit(solution)/shard_map/ppermute | solution.py:17
Sparse Core Ops, SparseCore 0:
  49.9 67.5 all-gather.2
where the time goes:
time: 316 us; the launch traced here: 313 us
  local copies, waits for them, and re-layouts  129 us (41%)
  other arithmetic  78.6 us (25%)
  blocking collectives  34.5 us (11%)
  loops' own time  28.2 us (9%)
  between operations  13.6 us (4%)
  starting transfers between devices  13.1 us (4%)
  waiting for transfers between devices  11.5 us (4%)
  matrix products  4.55 us (1%)
    convert_element_type x49, local copies, waits for them, and re-layouts, value_step(): window.astype(jnp.float32)  62.9 us
    another operation x49, local copies, waits for them, and re-layouts  42.4 us
    all_gather x1, blocking collectives, shards(): tall_weight = lax.all_gather(out_weight, 'col', axis=0, tiled=True)  34.5 us
    add x7, other arithmetic, value_step(): return (summed + row_total, None)  33.4 us
    dot_general x7, other arithmetic, score_step(): jnp.einsum('ibshd,ibshd->ibsh', query_heads, window, preferred_element_ty...  19.2 us
    another operation x1, loops' own time, shards(): lax.scan(score_step, jnp.zeros((), jnp.float32), row_steps)  14.3 us
    another operation x1, loops' own time, shards(): lax.scan(value_step, initial_sum, (row_steps, attention_grid))  13.9 us
    convert_element_type x7, other arithmetic, value_step(): window.astype(jnp.float32)  10.4 us
  transfers between devices with their start and end apart: 5, of which 2 were waited for; matrix products, arithmetic and copies ran while one was open for 66% of the time, Pallas kernels for 0%

commit v1 on v0

v1 whole, which is shorter than its diff:
```python
import jax
import jax.numpy as jnp
import numpy as np
from jax import lax
from jax.experimental import pallas as pl
from jax.experimental.pallas import tpu as pltpu
from jax.sharding import Mesh, PartitionSpec as P

VM = pl.BlockSpec(memory_space=pltpu.VMEM)
SM = pl.BlockSpec(memory_space=pltpu.SMEM)
BF = jnp.bfloat16
F32 = jnp.float32
NT = (((1,), (1,)), ((), ()))


def col_pick():
    pick = np.zeros((64, 160), np.float32)
    for side, first in ((0, 0), (1, 13)):
        for r in range(10):
            for j in range(3):
                x = first + j
                if r < 3:
                    source = 64 + r * 16 + x
                elif r < 7:
                    source = (r - 3) * 16 + x
                else:
                    source = 112 + (r - 7) * 16 + x
                pick[side * 32 + r * 3 + j, source] = 1.0
    return pick


def pack_kernel(pick_ref, k_ref, v_ref, top_ref, bot_ref, left_ref, right_ref):
    pick = pick_ref[...]
    for n, own in ((0, k_ref), (1, v_ref)):
        tokens = jnp.concatenate(
            [own[...], top_ref[n * 48 : n * 48 + 48, :], bot_ref[n * 48 : n * 48 + 48, :]], 0
        )
        got = jnp.dot(pick, tokens, preferred_element_type=F32).astype(BF)
        left_ref[n * 32 : n * 32 + 32, :] = got[:32]
        right_ref[n * 32 : n * 32 + 32, :] = got[32:]


def attention_kernel(
    place_ref, q_ref, k_ref, v_ref, top_ref, bot_ref, left_ref, right_ref, bias_ref, o_ref
):
    heads = bias_ref.shape[0]
    shape = (64, 256)
    i = lax.broadcasted_iota(jnp.int32, shape, 0)
    j = lax.broadcasted_iota(jnp.int32, shape, 1)
    y, x = i >> 4, i & 15
    side = j & 31
    side_row = ((side * 171) >> 9) - 3
    side_col = side - (side_row + 3) * 3
    ky = jnp.where(
        j < 64,
        j >> 4,
        jnp.where(j < 112, (j >> 4) - 7, jnp.where(j < 160, (j >> 4) - 3, side_row)),
    )
    kx = jnp.where(j < 160, j & 15, jnp.where(j < 192, side_col - 3, side_col + 16))
    dy, dx = ky - y + 3, kx - x + 3
    gy, gx = ky + place_ref[0], kx + place_ref[1]
    inside = (dy >= 0) & (dy < 7) & (dx >= 0) & (dx < 7)
    inside = inside & (gy >= 0) & (gy < place_ref[2]) & (gx >= 0) & (gx < place_ref[3])
    inside = inside & ((j < 160) | (side < 30)) & (j < 224)
    code = jnp.where(inside, dy * 7 + dx, 127)
    code_low, code_high = code[:, :128], code[:, 128:]
    low = lax.broadcasted_iota(jnp.int32, (64, 128), 1) < 64
    zeros = jnp.zeros((32, 128), BF)
    none = jnp.zeros((64, 128), BF)

    for pair in range(heads // 2):
        c = slice(pair * 128, pair * 128 + 128)
        q = q_ref[:, c]
        q2 = jnp.concatenate([jnp.where(low, q, none), jnp.where(low, none, q)], 0)
        keys = jnp.concatenate(
            [k_ref[:, c], top_ref[:48, c], bot_ref[:48, c], left_ref[:32, c], right_ref[:32, c], zeros], 0
        )
        vals = jnp.concatenate(
            [v_ref[:, c], top_ref[48:, c], bot_ref[48:, c], left_ref[32:, c], right_ref[32:, c], zeros], 0
        )
        s = lax.dot_general(q2, keys, NT, preferred_element_type=F32)
        bias = []
        for h in (2 * pair, 2 * pair + 1):
            row = jnp.broadcast_to(bias_ref[h : h + 1, :], (64, 128))
            bias.append(
                jnp.concatenate(
                    [
                        jnp.take_along_axis(row, code_low, axis=1, mode="promise_in_bounds"),
                        jnp.take_along_axis(row, code_high, axis=1, mode="promise_in_bounds"),
                    ],
                    1,
                )
            )
        s = s * 0.125 + jnp.concatenate(bias, 0)
        e = jnp.exp(s - jnp.max(s, 1, keepdims=True))
        p = (e * (1.0 / jnp.sum(e, 1, keepdims=True))).astype(BF)
        o = jnp.dot(p, vals, preferred_element_type=F32)
        o_ref[:, c] = jnp.where(low, o[:64], o[64:]).astype(BF)


def project_kernel(core_ref, mine_ref, other_ref, w_ref, keep_ref, send_ref):
    mixed = jnp.concatenate([mine_ref[...], other_ref[...]], 0)
    total = None
    for xh in range(2):
        for y in range(4):
            block = xh * 4 + y
            feats = mixed[:, block * 192 : block * 192 + 192]
            parts = []
            for z in range(8):
                for xl in range(2):
                    w = w_ref[xh, xl, y, z]
                    tail = w[48:]
                    tail = jnp.concatenate([tail[:, :64], tail[:, 64:]], 0)
                    parts.append(jnp.concatenate([w[:48], tail], 1))
            wt = jnp.concatenate(parts, 0)
            term = lax.dot_general(feats, wt, NT, preferred_element_type=F32)
            total = term if total is None else total + term
    out = total.astype(BF)
    keep_ref[...] = out[:64]
    send_ref[...] = out[64:]


def assemble_kernel(core_ref, mine_ref, other_ref, o_ref):
    first = core_ref[0] == 0
    mine, other = mine_ref[...].astype(F32), other_ref[...].astype(F32)
    a = jnp.where(first, mine, other)
    b = jnp.where(first, other, mine)
    pieces = []
    for n in range(16):
        pieces += [a[:, n * 48 : n * 48 + 48], b[:, n * 48 : n * 48 + 48]]
    o_ref[...] = jnp.concatenate(pieces, 1).astype(BF)


def call(kernel, outs, n_in, smem=(), limit=48):
    return pl.pallas_call(
        kernel,
        out_shape=outs,
        in_specs=[SM if k in smem else VM for k in range(n_in)],
        out_specs=VM if isinstance(outs, jax.ShapeDtypeStruct) else tuple(VM for _ in outs),
        compiler_params=pltpu.CompilerParams(vmem_limit_bytes=limit * 1024 * 1024),
    )


def shards(queries, key_tokens, values, position_bias, out_weight):
    width = queries.shape[3]
    rows, cols = ("z", "xl", "core"), ("xh", "y")
    nr, nc = lax.axis_size(rows), lax.axis_size(cols)
    r, c = lax.axis_index(rows), lax.axis_index(cols)
    core = lax.axis_index("core")

    wt = out_weight.T
    packed = jnp.concatenate([wt[:, :128], jnp.concatenate([wt[:24, 128:], wt[24:, 128:]], 1)], 0)
    along_z = lax.all_to_all(jnp.broadcast_to(packed[None], (8, 72, 128)), "z", 0, 0, tiled=True)
    plane = lax.all_to_all(
        jnp.broadcast_to(along_z[None], (16, 8, 72, 128)), ("xh", "xl", "y"), 0, 0, tiled=True
    )
    weights = plane.reshape(2, 2, 4, 8, 72, 128)

    down = [(n, n + 1) for n in range(nr - 1)]
    up = [(n + 1, n) for n in range(nr - 1)]
    right = [(n, n + 1) for n in range(nc - 1)]
    left = [(n + 1, n) for n in range(nc - 1)]
    k, v, q = (a.reshape(64, width) for a in (key_tokens, values, queries))
    top = lax.ppermute(jnp.concatenate([k[16:], v[16:]], 0), rows, down)
    bot = lax.ppermute(jnp.concatenate([k[:48], v[:48]], 0), rows, up)
    side = jax.ShapeDtypeStruct((64, width), BF)
    to_left, to_right = call(pack_kernel, (side, side), 5)(jnp.asarray(col_pick(), BF), k, v, top, bot)
    from_left = lax.ppermute(to_right, cols, right)
    from_right = lax.ppermute(to_left, cols, left)

    place = jnp.stack([r * 4, c * 16, nr * 4, nc * 16]).astype(jnp.int32)
    bias = jnp.pad(position_bias, ((0, 0), (0, 128 - 49)), constant_values=-jnp.inf)
    mixed = call(attention_kernel, side, 9, smem=(0,))(
        place, q, k, v, top, bot, from_left, from_right, bias
    )
    swap = [(0, 1), (1, 0)]
    other = lax.ppermute(mixed, "core", swap)
    half = jax.ShapeDtypeStruct((64, width // 2), BF)
    core_id = core.astype(jnp.int32).reshape(1)
    keep, send = call(project_kernel, (half, half), 4, smem=(0,))(core_id, mixed, other, weights)
    got = lax.ppermute(send, "core", swap)
    out = call(assemble_kernel, side, 3, smem=(0,))(core_id, keep, got)
    return out.reshape(queries.shape)


def solution(mesh):
    fine = Mesh(mesh.devices.reshape(8, 2, 2, 2, 4), ("z", "xl", "core", "xh", "y"))
    rows, cols = ("z", "xl", "core"), ("xh", "y")
    tokens = P(None, rows, cols, None)
    return jax.shard_map(
        shards,
        mesh=fine,
        in_specs=(tokens, tokens, tokens, P(), P(cols, rows)),
        out_specs=tokens,
        check_vma=False,
    )
```

time: 316 us -> 89.9 us (0.28)
  the two profiles are of different devices: /device:TPU:248 before, /device:TPU:57 now
where the time goes in v1:
time: 89.9 us; the launch traced here: 89.5 us
  waiting for transfers between devices  39 us (43%)
  starting transfers between devices  20.7 us (23%)
  blocking collectives  14.9 us (17%)
  Pallas kernels  8.55 us (10%)
  local copies, waits for them, and re-layouts  5.92 us (7%)
    ppermute x1, waiting for transfers between devices, shards(): top = lax.ppermute(jnp.concatenate([k[16:], v[16:]], 0), rows, down)  25 us
    all_to_all x1, blocking collectives, shards(): lax.all_to_all(jnp.broadcast_to(packed[None], (8, 72, 128)), 'z', 0, 0, t...  14.9 us
    ppermute x1, waiting for transfers between devices, shards(): from_right = lax.ppermute(to_left, cols, left)  6.76 us
    all_to_all x1, starting transfers between devices, shards(): lax.all_to_all(jnp.broadcast_to(along_z[None], (16, 8, 72, 128)), ('xh',...  6.74 us
    ppermute x1, starting transfers between devices, shards(): top = lax.ppermute(jnp.concatenate([k[16:], v[16:]], 0), rows, down)  5.6 us
    pallas_call x1, Pallas kernels, shards(): call(attention_kernel, side, 9, smem=(0,))  5.4 us
    ppermute x1, starting transfers between devices, shards(): from_left = lax.ppermute(to_right, cols, right)  4.18 us
    ppermute x1, waiting for transfers between devices, shards(): bot = lax.ppermute(jnp.concatenate([k[:48], v[:48]], 0), rows, up)  3.8 us
  transfers between devices with their start and end apart: 7, of which 6 were waited for; matrix products, arithmetic and copies ran while one was open for 0% of the time, Pallas kernels for 7%

profile of v1, /device:TPU:57, one launch (start us, length us, event | category | flops | bytes accessed | tf_op | source)
XLA Modules:
  0.0 89.5 jit_solution(17576305180323810633)
XLA Ops:
  0.0 0.7 slice.44
  0.7 0.7 fusion.2
  1.4 0.1 maximum_maximum_fusion
  1.5 14.9 %all_to_all.10 = bf16[8,72,128]{2,1,0:T(8,128)(2,1)S(1)} all-to-all(bf16[8,72,128]{2,1,0:T(8,128)(2,1)S(1)} %broadcast_in_dim.4), channel_id=1, replica_groups=mesh['z'=8,'xl'=2,'core'=2,'xh'=2,'y'=4] {'z'}, dimensions={0} | all-to-all | bytes 294912 | tf_op jit(solution)/shard_map/all_to_all | solution.py:153
  16.5 1.9 %broadcast_in_dim.5 = bf16[16,8,72,128]{3,2,1,0:T(8,128)(2,1)} broadcast(bf16[8,72,128]{2,1,0:T(8,128)(2,1)S(1)} %all_to_all.10), dimensions={1,2,3} | broadcast | bytes 2506752 | tf_op jit(solution)/shard_map/broadcast_in_dim | solution.py:155
  18.3 0.0 copy-start
  18.3 0.0 copy-start.1
  18.3 6.7 %all-to-all-start.1 = ((bf16[16,8,72,128]{3,2,1,0:T(8,128)(2,1)}), bf16[16,8,72,128]{3,2,1,0:T(8,128)(2,1)S(1)}, u32[]{:S(2)}, u32[]{:S(2)}) async-start(bf16[16,8,72,128]{3,2,1,0:T(8,128)(2,1)} %broadcast_in_dim.5), calls=%async_computation.1 | async-start | bytes 4718592 | tf_op jit(solution)/shard_map/all_to_all | solution.py:154
  25.1 0.0 copy-done
  25.1 0.0 copy-start.5
  25.1 0.0 copy-start.6
  25.1 0.0 copy-done.1
  25.2 5.6 %collective-permute-start = (bf16[96,1536]{1,0:T(8,128)(2,1)S(1)}, bf16[96,1536]{1,0:T(8,128)(2,1)S(1)}, u32[]{:S(2)}, u32[]{:S(2)}) collective-permute-start(bf16[96,1536]{1,0:T(8,128)(2,1)S(1)} %pad_maximum_fusion), channel_id=1, source_target_pairs={{0,8},{8,16},{16,24},{24,32},{32,40},{40,48},{48,56},{56,64},{64,7... | collective-permute-start | bytes 884744 | tf_op jit(solution)/shard_map/ppermute | solution.py:164
  30.9 1.9 %collective-permute-start.1 = (bf16[96,1536]{1,0:T(8,128)(2,1)S(1)}, bf16[96,1536]{1,0:T(8,128)(2,1)S(1)}, u32[]{:S(2)}, u32[]{:S(2)}) collective-permute-start(bf16[96,1536]{1,0:T(8,128)(2,1)S(1)} %pad_maximum_fusion.1), channel_id=1, source_target_pairs={{8,0},{16,8},{24,16},{32,24},{40,32},{48,40},{56,48},{64,56},{72,6... | collective-permute-start | bytes 884744 | tf_op jit(solution)/shard_map/ppermute | solution.py:165
  32.8 25.0 %collective-permute-done.top_ref = bf16[96,1536]{1,0:T(8,128)(2,1)S(1)} collective-permute-done((bf16[96,1536]{1,0:T(8,128)(2,1)S(1)}, bf16[96,1536]{1,0:T(8,128)(2,1)S(1)}, u32[]{:S(2)}, u32[]{:S(2)}) %collective-permute-start) | collective-permute-done | bytes 294944 | tf_op jit(solution)/shard_map/ppermute | solution.py:164
  57.8 3.8 %collective-permute-done.1.bot_ref = bf16[96,1536]{1,0:T(8,128)(2,1)S(1)} collective-permute-done((bf16[96,1536]{1,0:T(8,128)(2,1)S(1)}, bf16[96,1536]{1,0:T(8,128)(2,1)S(1)}, u32[]{:S(2)}, u32[]{:S(2)}) %collective-permute-start.1) | collective-permute-done | bytes 294944 | tf_op jit(solution)/shard_map/ppermute | solution.py:165
  61.6 0.0 copy-done.5
  61.6 1.0 %shard_map.64 = (bf16[64,1536]{1,0:T(8,128)(2,1)}, bf16[64,1536]{1,0:T(8,128)(2,1)}) custom-call(bf16[64,160]{1,0:T(8,128)(2,1)S(1)} %copy-done.5, bf16[64,1536]{1,0:T(8,128)(2,1)S(1)} %bitcast.14, bf16[64,1536]{1,0:T(8,128)(2,1)S(1)} %bitcast.16, bf16[96,1536]{1,0:T(8,128)(2,1)S(1)} %collective-permute-done.top_ref, ...), custom_call_target="tpu_custom_call" | custom-call | tf_op jit(solution)/shard_map/pallas_call | solution.py:167
  62.6 4.2 %collective-permute-start.2 = (bf16[64,1536]{1,0:T(8,128)(2,1)}, bf16[64,1536]{1,0:T(8,128)(2,1)S(1)}, u32[]{:S(2)}, u32[]{:S(2)}) collective-permute-start(bf16[64,1536]{1,0:T(8,128)(2,1)} %get-tuple-element.9), channel_id=1, source_target_pairs={{0,1},{1,2},{2,3},{3,4},{4,5},{5,6},{6,7},{8,9},{9,10},{10,11},{11... | collective-permute-start | bytes 589832 | tf_op jit(solution)/shard_map/ppermute | solution.py:168
  66.8 1.9 %collective-permute-start.3 = (bf16[64,1536]{1,0:T(8,128)(2,1)}, bf16[64,1536]{1,0:T(8,128)(2,1)}, u32[]{:S(2)}, u32[]{:S(2)}) collective-permute-start(bf16[64,1536]{1,0:T(8,128)(2,1)} %get-tuple-element.10), channel_id=1, source_target_pairs={{1,0},{2,1},{3,2},{4,3},{5,4},{6,5},{7,6},{9,8},{10,9},{11,10},{12... | collective-permute-start | bytes 589832 | tf_op jit(solution)/shard_map/ppermute | solution.py:169
  68.7 0.0 copy-done.6
  68.8 0.1 pad_add_fusion.place_ref
  68.8 0.9 collective-permute-done.2.left_ref
  69.7 0.0 copy-start.3
  69.7 0.7 copy-done.3
  70.4 6.8 %collective-permute-done.3.right_ref = bf16[64,1536]{1,0:T(8,128)(2,1)} collective-permute-done((bf16[64,1536]{1,0:T(8,128)(2,1)}, bf16[64,1536]{1,0:T(8,128)(2,1)}, u32[]{:S(2)}, u32[]{:S(2)}) %collective-permute-start.3) | collective-permute-done | bytes 196640 | tf_op jit(solution)/shard_map/ppermute | solution.py:169
  77.1 0.0 copy-start.2
  77.1 0.9 %copy-done.2 = bf16[1,4,16,1536]{3,2,1,0:T(8,128)(2,1)S(1)} copy-done((bf16[1,4,16,1536]{3,2,1,0:T(8,128)(2,1)S(1)}, bf16[1,4,16,1536]{3,2,1,0:T(8,128)(2,1)}, u32[]{:S(2)}) %copy-start.2) | copy-done | bytes 196632
  78.1 0.0 copy-start.4
  78.1 0.9 %copy-done.4 = bf16[64,1536]{1,0:T(8,128)(2,1)S(1)} copy-done((bf16[64,1536]{1,0:T(8,128)(2,1)S(1)}, bf16[64,1536]{1,0:T(8,128)(2,1)}, u32[]{:S(2)}) %copy-start.4) | copy-done | bytes 196632
  79.0 5.4 %shard_map.65.mine_ref = bf16[64,1536]{1,0:T(8,128)(2,1)S(1)} custom-call(s32[4]{0:T(128)S(1)} %pad_add_fusion.place_ref, bf16[64,1536]{1,0:T(8,128)(2,1)S(1)} %bitcast.18, bf16[64,1536]{1,0:T(8,128)(2,1)S(1)} %bitcast.15, bf16[64,1536]{1,0:T(8,128)(2,1)S(1)} %bitcast.17, bf16[96,1536]{1,0:T(8,128)(2,1)S(1)} %collective-permute-done.top_ref, ...), custom_call_target="tpu_custom_call" | custom-call | tf_op jit(solution)/shard_map/pallas_call | solution.py:173
  84.4 0.1 collective-permute-start.4
  84.5 1.4 %collective-permute-done.4.other_ref = bf16[64,1536]{1,0:T(8,128)(2,1)S(1)} collective-permute-done((bf16[64,1536]{1,0:T(8,128)(2,1)S(1)}, bf16[64,1536]{1,0:T(8,128)(2,1)S(1)}, u32[]{:S(2)}, u32[]{:S(2)}) %collective-permute-start.4) | collective-permute-done | bytes 196640 | tf_op jit(solution)/shard_map/ppermute | solution.py:177
  85.9 0.0 all-to-all-done.1
  85.9 1.2 %shard_map.66 = (bf16[64,768]{1,0:T(8,128)(2,1)S(1)}, bf16[64,768]{1,0:T(8,128)(2,1)S(1)}) custom-call(s32[1]{0:T(128)} %bitcast.core_ref, bf16[64,1536]{1,0:T(8,128)(2,1)S(1)} %shard_map.65.mine_ref, bf16[64,1536]{1,0:T(8,128)(2,1)S(1)} %collective-permute-done.4.other_ref, bf16[2,2,4,8,72,128]{5,4,3,2,1,0:T(8,128)(2,1)S(1)} %bitcast.13), custom_call_target="tpu_custom_call" | custom-call | tf_op jit(solution)/shard_map/pallas_call | solution.py:180
  87.2 0.2 collective-permute-start.5
  87.4 1.2 %collective-permute-done.5.other_ref = bf16[64,768]{1,0:T(8,128)(2,1)S(1)} collective-permute-done((bf16[64,768]{1,0:T(8,128)(2,1)S(1)}, bf16[64,768]{1,0:T(8,128)(2,1)S(1)}, u32[]{:S(2)}, u32[]{:S(2)}) %collective-permute-start.5) | collective-permute-done | bytes 98336 | tf_op jit(solution)/shard_map/ppermute | solution.py:181
  88.6 0.9 %shard_map.67 = bf16[64,1536]{1,0:T(8,128)(2,1)} custom-call(s32[1]{0:T(128)} %bitcast.core_ref, bf16[64,768]{1,0:T(8,128)(2,1)S(1)} %get-tuple-element.11.mine_ref, bf16[64,768]{1,0:T(8,128)(2,1)S(1)} %collective-permute-done.5.other_ref), custom_call_target="tpu_custom_call" | custom-call | tf_op jit(solution)/shard_map/pallas_call | solution.py:182
  (7 shorter events, 0.1 us)
Async XLA Ops:
  18.3 6.7 %copy-start = (bf16[1,4,16,1536]{3,2,1,0:T(8,128)(2,1)S(1)}, bf16[1,4,16,1536]{3,2,1,0:T(8,128)(2,1)}, u32[]{:S(2)}) copy-start(bf16[1,4,16,1536]{3,2,1,0:T(8,128)(2,1)} %param.7) | copy-start | bytes 589828
  18.3 6.8 %copy-start.1 = (bf16[1,4,16,1536]{3,2,1,0:T(8,128)(2,1)S(1)}, bf16[1,4,16,1536]{3,2,1,0:T(8,128)(2,1)}, u32[]{:S(2)}) copy-start(bf16[1,4,16,1536]{3,2,1,0:T(8,128)(2,1)} %param.8) | copy-start | bytes 589828
  18.3 67.6 %all-to-all-start.1 = ((bf16[16,8,72,128]{3,2,1,0:T(8,128)(2,1)}), bf16[16,8,72,128]{3,2,1,0:T(8,128)(2,1)S(1)}, u32[]{:S(2)}, u32[]{:S(2)}) async-start(bf16[16,8,72,128]{3,2,1,0:T(8,128)(2,1)} %broadcast_in_dim.5), calls=%async_computation.1 | async-start | bytes 4718592 | tf_op jit(solution)/shard_map/all_to_all | solution.py:154
  25.1 36.5 %copy-start.5 = (bf16[64,160]{1,0:T(8,128)(2,1)S(1)}, bf16[64,160]{1,0:T(8,128)(2,1)}, u32[]{:S(2)}) copy-start(bf16[64,160]{1,0:T(8,128)(2,1)} %constant.33.clone.pick_ref) | copy-start | bytes 61444
  25.1 43.6 %copy-start.6 = (f32[24,49]{1,0:T(8,128)S(1)}, f32[24,49]{1,0:T(8,128)}, u32[]{:S(2)}) copy-start(f32[24,49]{1,0:T(8,128)} %param.9) | copy-start | bytes 14116
  25.2 32.6 %collective-permute-start = (bf16[96,1536]{1,0:T(8,128)(2,1)S(1)}, bf16[96,1536]{1,0:T(8,128)(2,1)S(1)}, u32[]{:S(2)}, u32[]{:S(2)}) collective-permute-start(bf16[96,1536]{1,0:T(8,128)(2,1)S(1)} %pad_maximum_fusion), channel_id=1, source_target_pairs={{0,8},{8,16},{16,24},{24,32},{32,40},{40,48},{48,56},{56,64},{64,7... | collective-permute-start | bytes 884744 | tf_op jit(solution)/shard_map/ppermute | solution.py:164
  30.9 30.7 %collective-permute-start.1 = (bf16[96,1536]{1,0:T(8,128)(2,1)S(1)}, bf16[96,1536]{1,0:T(8,128)(2,1)S(1)}, u32[]{:S(2)}, u32[]{:S(2)}) collective-permute-start(bf16[96,1536]{1,0:T(8,128)(2,1)S(1)} %pad_maximum_fusion.1), channel_id=1, source_target_pairs={{8,0},{16,8},{24,16},{32,24},{40,32},{48,40},{56,48},{64,56},{72,6... | collective-permute-start | bytes 884744 | tf_op jit(solution)/shard_map/ppermute | solution.py:165
  62.6 7.1 %collective-permute-start.2 = (bf16[64,1536]{1,0:T(8,128)(2,1)}, bf16[64,1536]{1,0:T(8,128)(2,1)S(1)}, u32[]{:S(2)}, u32[]{:S(2)}) collective-permute-start(bf16[64,1536]{1,0:T(8,128)(2,1)} %get-tuple-element.9), channel_id=1, source_target_pairs={{0,1},{1,2},{2,3},{3,4},{4,5},{5,6},{6,7},{8,9},{9,10},{10,11},{11... | collective-permute-start | bytes 589832 | tf_op jit(solution)/shard_map/ppermute | solution.py:168
  66.8 10.3 %collective-permute-start.3 = (bf16[64,1536]{1,0:T(8,128)(2,1)}, bf16[64,1536]{1,0:T(8,128)(2,1)}, u32[]{:S(2)}, u32[]{:S(2)}) collective-permute-start(bf16[64,1536]{1,0:T(8,128)(2,1)} %get-tuple-element.10), channel_id=1, source_target_pairs={{1,0},{2,1},{3,2},{4,3},{5,4},{6,5},{7,6},{9,8},{10,9},{11,10},{12... | collective-permute-start | bytes 589832 | tf_op jit(solution)/shard_map/ppermute | solution.py:169
  69.7 0.7 copy-start.3
  77.1 0.9 %copy-start.2 = (bf16[1,4,16,1536]{3,2,1,0:T(8,128)(2,1)S(1)}, bf16[1,4,16,1536]{3,2,1,0:T(8,128)(2,1)}, u32[]{:S(2)}) copy-start(bf16[1,4,16,1536]{3,2,1,0:T(8,128)(2,1)} %param.6) | copy-start | bytes 589828
  78.1 0.9 %copy-start.4 = (bf16[64,1536]{1,0:T(8,128)(2,1)S(1)}, bf16[64,1536]{1,0:T(8,128)(2,1)}, u32[]{:S(2)}) copy-start(bf16[64,1536]{1,0:T(8,128)(2,1)} %copy-done.3) | copy-start | bytes 589828
  84.4 1.5 %collective-permute-start.4 = (bf16[64,1536]{1,0:T(8,128)(2,1)S(1)}, bf16[64,1536]{1,0:T(8,128)(2,1)S(1)}, u32[]{:S(2)}, u32[]{:S(2)}) collective-permute-start(bf16[64,1536]{1,0:T(8,128)(2,1)S(1)} %shard_map.65.mine_ref), channel_id=1, source_target_pairs={{0,8},{8,0},{1,9},{9,1},{2,10},{10,2},{3,11},{11,3},{4,12},{12,4},... | collective-permute-start | bytes 589832 | tf_op jit(solution)/shard_map/ppermute | solution.py:177
  87.2 1.4 %collective-permute-start.5 = (bf16[64,768]{1,0:T(8,128)(2,1)S(1)}, bf16[64,768]{1,0:T(8,128)(2,1)S(1)}, u32[]{:S(2)}, u32[]{:S(2)}) collective-permute-start(bf16[64,768]{1,0:T(8,128)(2,1)S(1)} %get-tuple-element.12), channel_id=1, source_target_pairs={{0,8},{8,0},{1,9},{9,1},{2,10},{10,2},{3,11},{11,3},{4,12},{12,4},... | collective-permute-start | bytes 294920 | tf_op jit(solution)/shard_map/ppermute | solution.py:181

commit v2 on v1

--- a/solution.py
+++ b/solution.py
@@ -98,8 +98,8 @@
         o_ref[:, c] = jnp.where(low, o[:64], o[64:]).astype(BF)
 
 
-def project_kernel(core_ref, mine_ref, other_ref, w_ref, keep_ref, send_ref):
-    mixed = jnp.concatenate([mine_ref[...], other_ref[...]], 0)
+def project_kernel(a_ref, b_ref, c_ref, d_ref, w_ref, keep_ref, send_ref):
+    mixed = jnp.concatenate([a_ref[...], b_ref[...], c_ref[...], d_ref[...]], 0)
     total = None
     for xh in range(2):
         for y in range(4):
@@ -107,27 +107,30 @@
             feats = mixed[:, block * 192 : block * 192 + 192]
             parts = []
             for z in range(8):
-                for xl in range(2):
-                    w = w_ref[xh, xl, y, z]
-                    tail = w[48:]
-                    tail = jnp.concatenate([tail[:, :64], tail[:, 64:]], 0)
-                    parts.append(jnp.concatenate([w[:48], tail], 1))
+                w = w_ref[xh, y, z]
+                tail = w[48:]
+                tail = jnp.concatenate([tail[:, :64], tail[:, 64:]], 0)
+                parts.append(jnp.concatenate([w[:48], tail], 1))
             wt = jnp.concatenate(parts, 0)
             term = lax.dot_general(feats, wt, NT, preferred_element_type=F32)
             total = term if total is None else total + term
     out = total.astype(BF)
-    keep_ref[...] = out[:64]
-    send_ref[...] = out[64:]
-
-
-def assemble_kernel(core_ref, mine_ref, other_ref, o_ref):
-    first = core_ref[0] == 0
-    mine, other = mine_ref[...].astype(F32), other_ref[...].astype(F32)
-    a = jnp.where(first, mine, other)
-    b = jnp.where(first, other, mine)
+    keep_ref[...] = out[:128]
+    send_ref[...] = out[128:]
+
+
+def assemble_kernel(at_ref, keep_ref, core_ref, chip_ref, o_ref):
+    xl, core = at_ref[0], at_ref[1]
+    mine, other = keep_ref[:64, :].astype(F32), core_ref[:64, :].astype(F32)
+    far_mine, far_other = chip_ref[:64, :].astype(F32), chip_ref[64:, :].astype(F32)
+    here0, here1 = jnp.where(core == 0, mine, other), jnp.where(core == 0, other, mine)
+    far0, far1 = jnp.where(core == 0, far_mine, far_other), jnp.where(core == 0, far_other, far_mine)
+    a0, a1 = jnp.where(xl == 0, here0, far0), jnp.where(xl == 0, here1, far1)
+    b0, b1 = jnp.where(xl == 0, far0, here0), jnp.where(xl == 0, far1, here1)
     pieces = []
-    for n in range(16):
-        pieces += [a[:, n * 48 : n * 48 + 48], b[:, n * 48 : n * 48 + 48]]
+    for n in range(8):
+        c = slice(n * 48, n * 48 + 48)
+        pieces += [a0[:, c], a1[:, c], b0[:, c], b1[:, c]]
     o_ref[...] = jnp.concatenate(pieces, 1).astype(BF)
 
 
@@ -146,21 +149,16 @@
     rows, cols = ("z", "xl", "core"), ("xh", "y")
     nr, nc = lax.axis_size(rows), lax.axis_size(cols)
     r, c = lax.axis_index(rows), lax.axis_index(cols)
-    core = lax.axis_index("core")
-
-    wt = out_weight.T
-    packed = jnp.concatenate([wt[:, :128], jnp.concatenate([wt[:24, 128:], wt[24:, 128:]], 1)], 0)
-    along_z = lax.all_to_all(jnp.broadcast_to(packed[None], (8, 72, 128)), "z", 0, 0, tiled=True)
-    plane = lax.all_to_all(
-        jnp.broadcast_to(along_z[None], (16, 8, 72, 128)), ("xh", "xl", "y"), 0, 0, tiled=True
-    )
-    weights = plane.reshape(2, 2, 4, 8, 72, 128)
 
     down = [(n, n + 1) for n in range(nr - 1)]
     up = [(n + 1, n) for n in range(nr - 1)]
     right = [(n, n + 1) for n in range(nc - 1)]
     left = [(n + 1, n) for n in range(nc - 1)]
     k, v, q = (a.reshape(64, width) for a in (key_tokens, values, queries))
+    wt = out_weight.T
+    packed = jnp.concatenate([wt[:, :128], jnp.concatenate([wt[:24, 128:], wt[24:, 128:]], 1)], 0)
+    along_z = lax.all_to_all(jnp.broadcast_to(packed[None], (8, 72, 128)), "z", 0, 0, tiled=True)
+
     top = lax.ppermute(jnp.concatenate([k[16:], v[16:]], 0), rows, down)
     bot = lax.ppermute(jnp.concatenate([k[:48], v[:48]], 0), rows, up)
     side = jax.ShapeDtypeStruct((64, width), BF)
@@ -168,18 +166,27 @@
     from_left = lax.ppermute(to_right, cols, right)
     from_right = lax.ppermute(to_left, cols, left)
 
+    from_left, from_right, along_z = lax.optimization_barrier((from_left, from_right, along_z))
+    plane = lax.all_to_all(
+        jnp.broadcast_to(along_z[None], (8, 8, 72, 128)), ("xh", "y"), 0, 0, tiled=True
+    )
+    weights = plane.reshape(2, 4, 8, 72, 128)
+
     place = jnp.stack([r * 4, c * 16, nr * 4, nc * 16]).astype(jnp.int32)
     bias = jnp.pad(position_bias, ((0, 0), (0, 128 - 49)), constant_values=-jnp.inf)
     mixed = call(attention_kernel, side, 9, smem=(0,))(
         place, q, k, v, top, bot, from_left, from_right, bias
     )
     swap = [(0, 1), (1, 0)]
-    other = lax.ppermute(mixed, "core", swap)
-    half = jax.ShapeDtypeStruct((64, width // 2), BF)
-    core_id = core.astype(jnp.int32).reshape(1)
-    keep, send = call(project_kernel, (half, half), 4, smem=(0,))(core_id, mixed, other, weights)
-    got = lax.ppermute(send, "core", swap)
-    out = call(assemble_kernel, side, 3, smem=(0,))(core_id, keep, got)
+    next_mixed = lax.ppermute(mixed, "xl", swap)
+    core_mixed = lax.ppermute(mixed, "core", swap)
+    both_mixed = lax.ppermute(next_mixed, "core", swap)
+    part = jax.ShapeDtypeStruct((128, width // 4), BF)
+    keep, send = call(project_kernel, (part, part), 5)(mixed, next_mixed, core_mixed, both_mixed, weights)
+    by_core = lax.ppermute(send, "core", swap)
+    by_chip = lax.ppermute(jnp.concatenate([keep[64:], by_core[64:]], 0), "xl", swap)
+    at = jnp.stack([lax.axis_index("xl"), lax.axis_index("core")]).astype(jnp.int32)
+    out = call(assemble_kernel, side, 4, smem=(0,))(at, keep, by_core, by_chip)
     return out.reshape(queries.shape)
 
 

time: 89.9 us -> 69.6 us (0.77)
  the two profiles are of different devices: /device:TPU:57 before, /device:TPU:100 now
where the time goes in v2:
time: 69.6 us; the launch traced here: 69.2 us
  starting transfers between devices  34.2 us (49%)
  waiting for transfers between devices  23 us (33%)
  Pallas kernels  7.54 us (11%)
  local copies, waits for them, and re-layouts  3.99 us (6%)
    ppermute x1, waiting for transfers between devices, shards(): next_mixed = lax.ppermute(mixed, 'xl', swap)  12.5 us
    all_to_all x1, starting transfers between devices, shards(): lax.all_to_all(jnp.broadcast_to(packed[None], (8, 72, 128)), 'z', 0, 0, t...  8.87 us
    all_to_all x1, starting transfers between devices, shards(): lax.all_to_all(jnp.broadcast_to(along_z[None], (8, 8, 72, 128)), ('xh', '...  8.06 us
    ppermute x1, starting transfers between devices, shards(): from_right = lax.ppermute(to_left, cols, left)  5.97 us
    pallas_call x1, Pallas kernels, shards(): call(attention_kernel, side, 9, smem=(0,))  5.02 us
    ppermute x1, waiting for transfers between devices, shards(): lax.ppermute(jnp.concatenate([keep[64:], by_core[64:]], 0), 'xl', swap)  4.76 us
    ppermute x1, starting transfers between devices, shards(): bot = lax.ppermute(jnp.concatenate([k[:48], v[:48]], 0), rows, up)  4.54 us
    ppermute x1, starting transfers between devices, shards(): from_left = lax.ppermute(to_right, cols, right)  3.49 us
  transfers between devices with their start and end apart: 11, of which 6 were waited for; matrix products, arithmetic and copies ran while one was open for 1% of the time, Pallas kernels for 8%

profile of v2, /device:TPU:100, one launch (start us, length us, event | category | flops | bytes accessed | tf_op | source)
XLA Modules:
  0.0 69.2 jit_solution(5027599918692846310)
XLA Ops:
  0.0 0.0 copy-start.4
  0.0 1.0 %fusion = (bf16[1,3,16,1536]{3,2,1,0:T(8,128)(2,1)S(1)}, bf16[1,3,16,1536]{3,2,1,0:T(8,128)(2,1)S(1)}) fusion(bf16[1,4,16,1536]{3,2,1,0:T(8,128)(2,1)} %param.7), kind=kLoop, calls=%fused_computation.6 | loop fusion | bytes 589824 | tf_op jit(solution)/shard_map/slice | solution.py:163
  1.0 0.0 copy-start
  1.0 0.0 copy-start.1
  1.0 0.0 copy-start.3
  1.1 1.1 %fusion.1 = (bf16[1,3,16,1536]{3,2,1,0:T(8,128)(2,1)S(1)}, bf16[1,3,16,1536]{3,2,1,0:T(8,128)(2,1)S(1)}) fusion(bf16[1,4,16,1536]{3,2,1,0:T(8,128)(2,1)} %param.8), kind=kLoop, calls=%fused_computation.7 | loop fusion | bytes 589824 | tf_op jit(solution)/shard_map/slice | solution.py:163
  2.1 1.9 %collective-permute-start = (bf16[96,1536]{1,0:T(8,128)(2,1)S(1)}, bf16[96,1536]{1,0:T(8,128)(2,1)S(1)}, u32[]{:S(2)}, u32[]{:S(2)}) collective-permute-start(bf16[96,1536]{1,0:T(8,128)(2,1)S(1)} %pad_maximum_fusion), channel_id=1, source_target_pairs={{0,8},{8,16},{16,24},{24,32},{32,40},{40,48},{48,56},{56,64},{64,7... | collective-permute-start | bytes 884744 | tf_op jit(solution)/shard_map/ppermute | solution.py:162
  4.1 4.5 %collective-permute-start.1 = (bf16[96,1536]{1,0:T(8,128)(2,1)S(1)}, bf16[96,1536]{1,0:T(8,128)(2,1)S(1)}, u32[]{:S(2)}, u32[]{:S(2)}) collective-permute-start(bf16[96,1536]{1,0:T(8,128)(2,1)S(1)} %pad_maximum_fusion.1), channel_id=1, source_target_pairs={{8,0},{16,8},{24,16},{32,24},{40,32},{48,40},{56,48},{64,56},{72,6... | collective-permute-start | bytes 884744 | tf_op jit(solution)/shard_map/ppermute | solution.py:163
  8.6 0.0 copy-done.4
  8.7 0.1 maximum_maximum_fusion
  8.8 0.7 broadcast_in_dim.4
  9.4 8.9 %all-to-all-start = ((bf16[8,72,128]{2,1,0:T(8,128)(2,1)}), bf16[8,72,128]{2,1,0:T(8,128)(2,1)S(1)}, u32[]{:S(2)}, u32[]{:S(2)}) async-start(bf16[8,72,128]{2,1,0:T(8,128)(2,1)} %broadcast_in_dim.4), calls=%async_computation | async-start | bytes 294912 | tf_op jit(solution)/shard_map/all_to_all | solution.py:160
  18.3 0.0 collective-permute-done.top_ref
  18.3 0.0 collective-permute-done.1.bot_ref
  18.3 0.0 copy-done
  18.3 0.0 copy-done.1
  18.3 0.0 copy-done.3
  18.4 0.3 shard_map.64
  18.6 3.5 %collective-permute-start.2 = (bf16[64,1536]{1,0:T(8,128)(2,1)S(1)}, bf16[64,1536]{1,0:T(8,128)(2,1)S(1)}, u32[]{:S(2)}, u32[]{:S(2)}) collective-permute-start(bf16[64,1536]{1,0:T(8,128)(2,1)S(1)} %get-tuple-element.12), channel_id=1, source_target_pairs={{0,1},{1,2},{2,3},{3,4},{4,5},{5,6},{6,7},{8,9},{9,10},{10,11},{11... | collective-permute-start | bytes 589832 | tf_op jit(solution)/shard_map/ppermute | solution.py:166
  22.1 6.0 %collective-permute-start.3 = (bf16[64,1536]{1,0:T(8,128)(2,1)S(1)}, bf16[64,1536]{1,0:T(8,128)(2,1)S(1)}, u32[]{:S(2)}, u32[]{:S(2)}) collective-permute-start(bf16[64,1536]{1,0:T(8,128)(2,1)S(1)} %get-tuple-element.13), channel_id=1, source_target_pairs={{1,0},{2,1},{3,2},{4,3},{5,4},{6,5},{7,6},{9,8},{10,9},{11,10},{12... | collective-permute-start | bytes 589832 | tf_op jit(solution)/shard_map/ppermute | solution.py:167
  28.1 0.0 all-to-all-done
  28.1 1.7 %collective-permute-done.2.left_ref = bf16[64,1536]{1,0:T(8,128)(2,1)S(1)} collective-permute-done((bf16[64,1536]{1,0:T(8,128)(2,1)S(1)}, bf16[64,1536]{1,0:T(8,128)(2,1)S(1)}, u32[]{:S(2)}, u32[]{:S(2)}) %collective-permute-start.2) | collective-permute-done | bytes 196640 | tf_op jit(solution)/shard_map/ppermute | solution.py:166
  29.8 1.5 %collective-permute-done.3.right_ref = bf16[64,1536]{1,0:T(8,128)(2,1)S(1)} collective-permute-done((bf16[64,1536]{1,0:T(8,128)(2,1)S(1)}, bf16[64,1536]{1,0:T(8,128)(2,1)S(1)}, u32[]{:S(2)}, u32[]{:S(2)}) %collective-permute-start.3) | collective-permute-done | bytes 196640 | tf_op jit(solution)/shard_map/ppermute | solution.py:167
  31.3 1.2 %broadcast_in_dim.5 = bf16[8,8,72,128]{3,2,1,0:T(8,128)(2,1)} broadcast(bf16[8,72,128]{2,1,0:T(8,128)(2,1)S(1)} %all-to-all-done), dimensions={1,2,3} | broadcast | bytes 1327104 | tf_op jit(solution)/shard_map/broadcast_in_dim | solution.py:171
  32.5 0.0 copy-start.5
  32.5 0.0 copy-start.2
  32.5 8.1 %all-to-all-start.1 = ((bf16[8,8,72,128]{3,2,1,0:T(8,128)(2,1)}), bf16[8,8,72,128]{3,2,1,0:T(8,128)(2,1)S(1)}, u32[]{:S(2)}, u32[]{:S(2)}) async-start(bf16[8,8,72,128]{3,2,1,0:T(8,128)(2,1)} %broadcast_in_dim.5), calls=%async_computation.1 | async-start | bytes 2359296 | tf_op jit(solution)/shard_map/all_to_all | solution.py:170
  40.5 0.0 copy-done.5
  40.5 0.1 pad_add_fusion.1.place_ref
  40.6 0.0 copy-done.2
  40.6 5.0 %shard_map.65.a_ref = bf16[64,1536]{1,0:T(8,128)(2,1)S(1)} custom-call(s32[4]{0:T(128)S(1)} %pad_add_fusion.1.place_ref, bf16[64,1536]{1,0:T(8,128)(2,1)S(1)} %bitcast.19, bf16[64,1536]{1,0:T(8,128)(2,1)S(1)} %bitcast.16, bf16[64,1536]{1,0:T(8,128)(2,1)S(1)} %bitcast.18, bf16[96,1536]{1,0:T(8,128)(2,1)S(1)} %collective-permute-done.top_ref, ...), custom_call_target="tpu_custom_call" | custom-call | tf_op jit(solution)/shard_map/pallas_call | solution.py:177
  45.7 1.0 %collective-permute-start.4 = (bf16[64,1536]{1,0:T(8,128)(2,1)S(1)}, bf16[64,1536]{1,0:T(8,128)(2,1)S(1)}, u32[]{:S(2)}, u32[]{:S(2)}) collective-permute-start(bf16[64,1536]{1,0:T(8,128)(2,1)S(1)} %shard_map.65.a_ref), channel_id=1, source_target_pairs={{0,16},{16,0},{1,17},{17,1},{2,18},{18,2},{3,19},{19,3},{4,20},{20... | collective-permute-start | bytes 589832 | tf_op jit(solution)/shard_map/ppermute | solution.py:181
  46.7 0.0 collective-permute-start.5
  46.7 12.5 %collective-permute-done.4.b_ref = bf16[64,1536]{1,0:T(8,128)(2,1)S(1)} collective-permute-done((bf16[64,1536]{1,0:T(8,128)(2,1)S(1)}, bf16[64,1536]{1,0:T(8,128)(2,1)S(1)}, u32[]{:S(2)}, u32[]{:S(2)}) %collective-permute-start.4) | collective-permute-done | bytes 196640 | tf_op jit(solution)/shard_map/ppermute | solution.py:181
  59.2 0.0 collective-permute-start.6
  59.2 0.0 collective-permute-done.5.c_ref
  59.2 1.4 %collective-permute-done.6.d_ref = bf16[64,1536]{1,0:T(8,128)(2,1)S(1)} collective-permute-done((bf16[64,1536]{1,0:T(8,128)(2,1)S(1)}, bf16[64,1536]{1,0:T(8,128)(2,1)S(1)}, u32[]{:S(2)}, u32[]{:S(2)}) %collective-permute-start.6) | collective-permute-done | bytes 196640 | tf_op jit(solution)/shard_map/ppermute | solution.py:183
  60.6 0.0 all-to-all-done.1
  60.6 0.8 %shard_map.66 = (bf16[128,384]{1,0:T(8,128)(2,1)S(1)}, bf16[128,384]{1,0:T(8,128)(2,1)S(1)}) custom-call(bf16[64,1536]{1,0:T(8,128)(2,1)S(1)} %shard_map.65.a_ref, bf16[64,1536]{1,0:T(8,128)(2,1)S(1)} %collective-permute-done.4.b_ref, bf16[64,1536]{1,0:T(8,128)(2,1)S(1)} %collective-permute-done.5.c_ref, bf16[64,1536]{1,0:T(8,128)(2,1)S(1)} %collective-permute-done.6.d_ref, ...), custom_call_target="tpu_custom_call" | custom-call | tf_op jit(solution)/shard_map/pallas_call | solution.py:185
  61.4 0.2 collective-permute-start.7
  61.7 1.2 %collective-permute-done.7.core_ref = bf16[128,384]{1,0:T(8,128)(2,1)S(1)} collective-permute-done((bf16[128,384]{1,0:T(8,128)(2,1)S(1)}, bf16[128,384]{1,0:T(8,128)(2,1)S(1)}, u32[]{:S(2)}, u32[]{:S(2)}) %collective-permute-start.7) | collective-permute-done | bytes 98336 | tf_op jit(solution)/shard_map/ppermute | solution.py:186
  62.9 0.1 collective-permute-start.8
  63.0 0.1 pad_add_fusion.at_ref
  63.0 4.8 %collective-permute-done.8.chip_ref = bf16[128,384]{1,0:T(8,128)(2,1)S(1)} collective-permute-done((bf16[128,384]{1,0:T(8,128)(2,1)S(1)}, bf16[128,384]{1,0:T(8,128)(2,1)S(1)}, u32[]{:S(2)}, u32[]{:S(2)}) %collective-permute-start.8) | collective-permute-done | bytes 98336 | tf_op jit(solution)/shard_map/ppermute | solution.py:187
  67.8 1.4 %shard_map.67 = bf16[64,1536]{1,0:T(8,128)(2,1)} custom-call(s32[2]{0:T(128)S(1)} %pad_add_fusion.at_ref, bf16[128,384]{1,0:T(8,128)(2,1)S(1)} %get-tuple-element.17.keep_ref, bf16[128,384]{1,0:T(8,128)(2,1)S(1)} %collective-permute-done.7.core_ref, bf16[128,384]{1,0:T(8,128)(2,1)S(1)} %collective-permute-done.8.chip_ref), custom_call_target="tpu_custom_call" | custom-call | tf_op jit(solution)/shard_map/pallas_call | solution.py:189
  (9 shorter events, 0.1 us)
Async XLA Ops:
  0.0 8.6 %copy-start.4 = (bf16[192,48]{0,1:T(8,128)(2,1)S(1)}, bf16[192,48]{0,1:T(8,128)(2,1)}, u32[]{:S(2)}) copy-start(bf16[192,48]{0,1:T(8,128)(2,1)} %param.10) | copy-start | bytes 55300
  1.0 17.3 %copy-start = (bf16[1,4,16,1536]{3,2,1,0:T(8,128)(2,1)S(1)}, bf16[1,4,16,1536]{3,2,1,0:T(8,128)(2,1)}, u32[]{:S(2)}) copy-start(bf16[1,4,16,1536]{3,2,1,0:T(8,128)(2,1)} %param.7) | copy-start | bytes 589828
  1.0 17.3 %copy-start.1 = (bf16[1,4,16,1536]{3,2,1,0:T(8,128)(2,1)S(1)}, bf16[1,4,16,1536]{3,2,1,0:T(8,128)(2,1)}, u32[]{:S(2)}) copy-start(bf16[1,4,16,1536]{3,2,1,0:T(8,128)(2,1)} %param.8) | copy-start | bytes 589828
  1.0 17.3 %copy-start.3 = (bf16[64,160]{1,0:T(8,128)(2,1)S(1)}, bf16[64,160]{1,0:T(8,128)(2,1)}, u32[]{:S(2)}) copy-start(bf16[64,160]{1,0:T(8,128)(2,1)} %constant.33.clone.pick_ref) | copy-start | bytes 61444
  2.1 16.2 %collective-permute-start = (bf16[96,1536]{1,0:T(8,128)(2,1)S(1)}, bf16[96,1536]{1,0:T(8,128)(2,1)S(1)}, u32[]{:S(2)}, u32[]{:S(2)}) collective-permute-start(bf16[96,1536]{1,0:T(8,128)(2,1)S(1)} %pad_maximum_fusion), channel_id=1, source_target_pairs={{0,8},{8,16},{16,24},{24,32},{32,40},{40,48},{48,56},{56,64},{64,7... | collective-permute-start | bytes 884744 | tf_op jit(solution)/shard_map/ppermute | solution.py:162
  4.1 14.2 %collective-permute-start.1 = (bf16[96,1536]{1,0:T(8,128)(2,1)S(1)}, bf16[96,1536]{1,0:T(8,128)(2,1)S(1)}, u32[]{:S(2)}, u32[]{:S(2)}) collective-permute-start(bf16[96,1536]{1,0:T(8,128)(2,1)S(1)} %pad_maximum_fusion.1), channel_id=1, source_target_pairs={{8,0},{16,8},{24,16},{32,24},{40,32},{48,40},{56,48},{64,56},{72,6... | collective-permute-start | bytes 884744 | tf_op jit(solution)/shard_map/ppermute | solution.py:163
  9.4 18.7 %all-to-all-start = ((bf16[8,72,128]{2,1,0:T(8,128)(2,1)}), bf16[8,72,128]{2,1,0:T(8,128)(2,1)S(1)}, u32[]{:S(2)}, u32[]{:S(2)}) async-start(bf16[8,72,128]{2,1,0:T(8,128)(2,1)} %broadcast_in_dim.4), calls=%async_computation | async-start | bytes 294912 | tf_op jit(solution)/shard_map/all_to_all | solution.py:160
  18.6 11.2 %collective-permute-start.2 = (bf16[64,1536]{1,0:T(8,128)(2,1)S(1)}, bf16[64,1536]{1,0:T(8,128)(2,1)S(1)}, u32[]{:S(2)}, u32[]{:S(2)}) collective-permute-start(bf16[64,1536]{1,0:T(8,128)(2,1)S(1)} %get-tuple-element.12), channel_id=1, source_target_pairs={{0,1},{1,2},{2,3},{3,4},{4,5},{5,6},{6,7},{8,9},{9,10},{10,11},{11... | collective-permute-start | bytes 589832 | tf_op jit(solution)/shard_map/ppermute | solution.py:166
  22.1 9.1 %collective-permute-start.3 = (bf16[64,1536]{1,0:T(8,128)(2,1)S(1)}, bf16[64,1536]{1,0:T(8,128)(2,1)S(1)}, u32[]{:S(2)}, u32[]{:S(2)}) collective-permute-start(bf16[64,1536]{1,0:T(8,128)(2,1)S(1)} %get-tuple-element.13), channel_id=1, source_target_pairs={{1,0},{2,1},{3,2},{4,3},{5,4},{6,5},{7,6},{9,8},{10,9},{11,10},{12... | collective-permute-start | bytes 589832 | tf_op jit(solution)/shard_map/ppermute | solution.py:167
  32.5 8.1 %copy-start.5 = (f32[24,49]{1,0:T(8,128)S(1)}, f32[24,49]{1,0:T(8,128)}, u32[]{:S(2)}) copy-start(f32[24,49]{1,0:T(8,128)} %param.9) | copy-start | bytes 14116
  32.5 8.2 %copy-start.2 = (bf16[1,4,16,1536]{3,2,1,0:T(8,128)(2,1)S(1)}, bf16[1,4,16,1536]{3,2,1,0:T(8,128)(2,1)}, u32[]{:S(2)}) copy-start(bf16[1,4,16,1536]{3,2,1,0:T(8,128)(2,1)} %param.6) | copy-start | bytes 589828
  32.5 28.2 %all-to-all-start.1 = ((bf16[8,8,72,128]{3,2,1,0:T(8,128)(2,1)}), bf16[8,8,72,128]{3,2,1,0:T(8,128)(2,1)S(1)}, u32[]{:S(2)}, u32[]{:S(2)}) async-start(bf16[8,8,72,128]{3,2,1,0:T(8,128)(2,1)} %broadcast_in_dim.5), calls=%async_computation.1 | async-start | bytes 2359296 | tf_op jit(solution)/shard_map/all_to_all | solution.py:170
  45.7 13.5 %collective-permute-start.4 = (bf16[64,1536]{1,0:T(8,128)(2,1)S(1)}, bf16[64,1536]{1,0:T(8,128)(2,1)S(1)}, u32[]{:S(2)}, u32[]{:S(2)}) collective-permute-start(bf16[64,1536]{1,0:T(8,128)(2,1)S(1)} %shard_map.65.a_ref), channel_id=1, source_target_pairs={{0,16},{16,0},{1,17},{17,1},{2,18},{18,2},{3,19},{19,3},{4,20},{20... | collective-permute-start | bytes 589832 | tf_op jit(solution)/shard_map/ppermute | solution.py:181
  46.7 12.5 %collective-permute-start.5 = (bf16[64,1536]{1,0:T(8,128)(2,1)S(1)}, bf16[64,1536]{1,0:T(8,128)(2,1)S(1)}, u32[]{:S(2)}, u32[]{:S(2)}) collective-permute-start(bf16[64,1536]{1,0:T(8,128)(2,1)S(1)} %shard_map.65.a_ref), channel_id=1, source_target_pairs={{0,8},{8,0},{1,9},{9,1},{2,10},{10,2},{3,11},{11,3},{4,12},{12,4},... | collective-permute-start | bytes 589832 | tf_op jit(solution)/shard_map/ppermute | solution.py:182
  59.2 1.4 %collective-permute-start.6 = (bf16[64,1536]{1,0:T(8,128)(2,1)S(1)}, bf16[64,1536]{1,0:T(8,128)(2,1)S(1)}, u32[]{:S(2)}, u32[]{:S(2)}) collective-permute-start(bf16[64,1536]{1,0:T(8,128)(2,1)S(1)} %collective-permute-done.4.b_ref), channel_id=1, source_target_pairs={{0,8},{8,0},{1,9},{9,1},{2,10},{10,2},{3,11},{11,3},{4,12},{12,4},... | collective-permute-start | bytes 589832 | tf_op jit(solution)/shard_map/ppermute | solution.py:183
  61.4 1.4 %collective-permute-start.7 = (bf16[128,384]{1,0:T(8,128)(2,1)S(1)}, bf16[128,384]{1,0:T(8,128)(2,1)S(1)}, u32[]{:S(2)}, u32[]{:S(2)}) collective-permute-start(bf16[128,384]{1,0:T(8,128)(2,1)S(1)} %get-tuple-element.18), channel_id=1, source_target_pairs={{0,8},{8,0},{1,9},{9,1},{2,10},{10,2},{3,11},{11,3},{4,12},{12,4},... | collective-permute-start | bytes 294920 | tf_op jit(solution)/shard_map/ppermute | solution.py:186
  62.9 4.9 %collective-permute-start.8 = (bf16[128,384]{1,0:T(8,128)(2,1)S(1)}, bf16[128,384]{1,0:T(8,128)(2,1)S(1)}, u32[]{:S(2)}, u32[]{:S(2)}) collective-permute-start(bf16[128,384]{1,0:T(8,128)(2,1)S(1)} %pad_maximum_fusion.2), channel_id=1, source_target_pairs={{0,16},{16,0},{1,17},{17,1},{2,18},{18,2},{3,19},{19,3},{4,20},{20... | collective-permute-start | bytes 294920 | tf_op jit(solution)/shard_map/ppermute | solution.py:187

commit v3 on v2

--- a/solution.py
+++ b/solution.py
@@ -98,7 +98,7 @@
         o_ref[:, c] = jnp.where(low, o[:64], o[64:]).astype(BF)
 
 
-def project_kernel(a_ref, b_ref, c_ref, d_ref, w_ref, keep_ref, send_ref):
+def project_kernel(a_ref, b_ref, c_ref, d_ref, w_ref, keep_ref, chip_ref, core_ref, both_ref):
     mixed = jnp.concatenate([a_ref[...], b_ref[...], c_ref[...], d_ref[...]], 0)
     total = None
     for xh in range(2):
@@ -115,22 +115,22 @@
             term = lax.dot_general(feats, wt, NT, preferred_element_type=F32)
             total = term if total is None else total + term
     out = total.astype(BF)
-    keep_ref[...] = out[:128]
-    send_ref[...] = out[128:]
-
-
-def assemble_kernel(at_ref, keep_ref, core_ref, chip_ref, o_ref):
-    xl, core = at_ref[0], at_ref[1]
-    mine, other = keep_ref[:64, :].astype(F32), core_ref[:64, :].astype(F32)
-    far_mine, far_other = chip_ref[:64, :].astype(F32), chip_ref[64:, :].astype(F32)
-    here0, here1 = jnp.where(core == 0, mine, other), jnp.where(core == 0, other, mine)
-    far0, far1 = jnp.where(core == 0, far_mine, far_other), jnp.where(core == 0, far_other, far_mine)
-    a0, a1 = jnp.where(xl == 0, here0, far0), jnp.where(xl == 0, here1, far1)
-    b0, b1 = jnp.where(xl == 0, far0, here0), jnp.where(xl == 0, far1, here1)
-    pieces = []
-    for n in range(8):
-        c = slice(n * 48, n * 48 + 48)
-        pieces += [a0[:, c], a1[:, c], b0[:, c], b1[:, c]]
+    for n, ref in enumerate((keep_ref, chip_ref, core_ref, both_ref)):
+        ref[...] = out[n * 64 : n * 64 + 64]
+
+
+def assemble_kernel(at_ref, keep_ref, core_ref, chip_ref, both_ref, o_ref):
+    xl, core = at_ref[0] == 0, at_ref[1] == 0
+    mine, other, far, far_other = (ref[...].astype(F32) for ref in (keep_ref, core_ref, chip_ref, both_ref))
+    here0, here1 = jnp.where(core, mine, other), jnp.where(core, other, mine)
+    far0, far1 = jnp.where(core, far, far_other), jnp.where(core, far_other, far)
+    quarters = (
+        jnp.where(xl, here0, far0),
+        jnp.where(xl, here1, far1),
+        jnp.where(xl, far0, here0),
+        jnp.where(xl, far1, here1),
+    )
+    pieces = [part[:, n * 48 : n * 48 + 48] for n in range(8) for part in quarters]
     o_ref[...] = jnp.concatenate(pieces, 1).astype(BF)
 
 
@@ -150,17 +150,18 @@
     nr, nc = lax.axis_size(rows), lax.axis_size(cols)
     r, c = lax.axis_index(rows), lax.axis_index(cols)
 
-    down = [(n, n + 1) for n in range(nr - 1)]
-    up = [(n + 1, n) for n in range(nr - 1)]
-    right = [(n, n + 1) for n in range(nc - 1)]
-    left = [(n + 1, n) for n in range(nc - 1)]
+    down = [(n, (n + 1) % nr) for n in range(nr)]
+    up = [(n, (n - 1) % nr) for n in range(nr)]
+    right = [(n, (n + 1) % nc) for n in range(nc)]
+    left = [(n, (n - 1) % nc) for n in range(nc)]
     k, v, q = (a.reshape(64, width) for a in (key_tokens, values, queries))
     wt = out_weight.T
     packed = jnp.concatenate([wt[:, :128], jnp.concatenate([wt[:24, 128:], wt[24:, 128:]], 1)], 0)
     along_z = lax.all_to_all(jnp.broadcast_to(packed[None], (8, 72, 128)), "z", 0, 0, tiled=True)
 
-    top = lax.ppermute(jnp.concatenate([k[16:], v[16:]], 0), rows, down)
-    bot = lax.ppermute(jnp.concatenate([k[:48], v[:48]], 0), rows, up)
+    both = jnp.stack([k, v], 0)
+    top = lax.ppermute(both[:, 16:], rows, down).reshape(96, width)
+    bot = lax.ppermute(both[:, :48], rows, up).reshape(96, width)
     side = jax.ShapeDtypeStruct((64, width), BF)
     to_left, to_right = call(pack_kernel, (side, side), 5)(jnp.asarray(col_pick(), BF), k, v, top, bot)
     from_left = lax.ppermute(to_right, cols, right)
@@ -181,12 +182,15 @@
     next_mixed = lax.ppermute(mixed, "xl", swap)
     core_mixed = lax.ppermute(mixed, "core", swap)
     both_mixed = lax.ppermute(next_mixed, "core", swap)
-    part = jax.ShapeDtypeStruct((128, width // 4), BF)
-    keep, send = call(project_kernel, (part, part), 5)(mixed, next_mixed, core_mixed, both_mixed, weights)
-    by_core = lax.ppermute(send, "core", swap)
-    by_chip = lax.ppermute(jnp.concatenate([keep[64:], by_core[64:]], 0), "xl", swap)
+    part = jax.ShapeDtypeStruct((64, width // 4), BF)
+    keep, to_chip, to_core, to_both = call(project_kernel, (part,) * 4, 5)(
+        mixed, next_mixed, core_mixed, both_mixed, weights
+    )
+    by_both = lax.ppermute(to_both, ("xl", "core"), [(n, 3 - n) for n in range(4)])
+    by_chip = lax.ppermute(to_chip, "xl", swap)
+    by_core = lax.ppermute(to_core, "core", swap)
     at = jnp.stack([lax.axis_index("xl"), lax.axis_index("core")]).astype(jnp.int32)
-    out = call(assemble_kernel, side, 4, smem=(0,))(at, keep, by_core, by_chip)
+    out = call(assemble_kernel, side, 5, smem=(0,))(at, keep, by_core, by_chip, by_both)
     return out.reshape(queries.shape)
 
 

time: 69.6 us -> 62.1 us (0.89)
  the two profiles are of different devices: /device:TPU:100 before, /device:TPU:1 now
where the time goes in v3:
time: 62.1 us; the launch traced here: 61.3 us
  starting transfers between devices  30.2 us (49%)
  waiting for transfers between devices  18.6 us (30%)
  Pallas kernels  7.54 us (12%)
  local copies, waits for them, and re-layouts  3.32 us (5%)
  other arithmetic  1.45 us (2%)
    ppermute x1, waiting for transfers between devices, shards(): next_mixed = lax.ppermute(mixed, 'xl', swap)  11.3 us
    all_to_all x1, starting transfers between devices, shards(): lax.all_to_all(jnp.broadcast_to(packed[None], (8, 72, 128)), 'z', 0, 0, t...  7.64 us
    all_to_all x1, starting transfers between devices, shards(): lax.all_to_all(jnp.broadcast_to(along_z[None], (8, 8, 72, 128)), ('xh', '...  7.35 us
    pallas_call x1, Pallas kernels, shards(): call(attention_kernel, side, 9, smem=(0,))  5.02 us
    ppermute x1, starting transfers between devices, shards(): from_right = lax.ppermute(to_left, cols, left)  3.87 us
    all_to_all x1, waiting for transfers between devices, shards(): lax.all_to_all(jnp.broadcast_to(packed[None], (8, 72, 128)), 'z', 0, 0, t...  3.62 us
    ppermute x1, starting transfers between devices, shards(): bot = lax.ppermute(both[:, :48], rows, up).reshape(96, width)  3.31 us
    ppermute x1, starting transfers between devices, shards(): next_mixed = lax.ppermute(mixed, 'xl', swap)  2.21 us
  transfers between devices with their start and end apart: 12, of which 5 were waited for; matrix products, arithmetic and copies ran while one was open for 4% of the time, Pallas kernels for 9%

profile of v3, /device:TPU:1, one launch (start us, length us, event | category | flops | bytes accessed | tf_op | source)
XLA Modules:
  0.0 61.3 jit_solution(4965233410510291659)
XLA Ops:
  0.0 0.0 copy-start.3
  0.0 0.0 copy-start
  0.0 0.0 copy-start.1
  0.0 1.2 %pad_maximum_fusion = (bf16[2,48,1536]{2,1,0:T(8,128)(2,1)S(1)}, bf16[2,48,1536]{2,1,0:T(8,128)(2,1)S(1)}) fusion(bf16[1,64,1536]{2,1,0:T(8,128)(2,1)} %bitcast.18, bf16[1,64,1536]{2,1,0:T(8,128)(2,1)} %bitcast.15), kind=kLoop, calls=%fused_computation.3 | loop fusion | flops 1179648 | bytes 983040 | tf_op jit(solution)/shard_map/stack | solution.py:162
  1.2 3.3 %collective-permute-start.1 = (bf16[2,48,1536]{2,1,0:T(8,128)(2,1)S(1)}, bf16[2,48,1536]{2,1,0:T(8,128)(2,1)S(1)}, u32[]{:S(2)}, u32[]{:S(2)}) collective-permute-start(bf16[2,48,1536]{2,1,0:T(8,128)(2,1)S(1)} %get-tuple-element.23), channel_id=1, source_target_pairs={{0,248},{8,0},{16,8},{24,16},{32,24},{40,32},{48,40},{56,48},{64,5... | collective-permute-start | bytes 884744 | tf_op jit(solution)/shard_map/ppermute | solution.py:164
  4.5 0.0 collective-permute-start
  4.5 0.7 %slice.22 = bf16[48,128]{1,0:T(8,128)(2,1)S(1)} slice(bf16[48,192]{1,0:T(8,128)(2,1)} %bitcast.26), slice={[0:48], [0:128]} | slice | bytes 24576 | tf_op jit(solution)/shard_map/slice | solution.py:159
  5.3 0.7 %fusion.1 = (bf16[24,64]{1,0:T(8,128)(2,1)S(1)}, bf16[24,64]{1,0:T(8,128)(2,1)S(1)}) fusion(bf16[48,192]{1,0:T(8,128)(2,1)} %bitcast.27), kind=kLoop, calls=%fused_computation.7 | loop fusion | bytes 12288 | tf_op jit(solution)/shard_map/slice | solution.py:159
  6.0 0.1 maximum_maximum_fusion
  6.0 0.7 %broadcast_in_dim.4 = bf16[8,72,128]{2,1,0:T(8,128)(2,1)} broadcast(bf16[72,128]{1,0:T(8,128)(2,1)S(1)} %maximum_maximum_fusion), dimensions={1,2} | broadcast | bytes 165888 | tf_op jit(solution)/shard_map/broadcast_in_dim | solution.py:160
  6.7 7.6 %all-to-all-start = ((bf16[8,72,128]{2,1,0:T(8,128)(2,1)}), bf16[8,72,128]{2,1,0:T(8,128)(2,1)S(1)}, u32[]{:S(2)}, u32[]{:S(2)}) async-start(bf16[8,72,128]{2,1,0:T(8,128)(2,1)} %broadcast_in_dim.4), calls=%async_computation | async-start | bytes 294912 | tf_op jit(solution)/shard_map/all_to_all | solution.py:160
  14.4 0.0 collective-permute-done.1
  14.4 0.0 collective-permute-done
  14.4 0.0 copy-done.3
  14.4 0.0 copy-done
  14.4 0.0 copy-done.1
  14.4 0.3 shard_map.64
  14.7 1.4 %collective-permute-start.2 = (bf16[64,1536]{1,0:T(8,128)(2,1)S(1)}, bf16[64,1536]{1,0:T(8,128)(2,1)S(1)}, u32[]{:S(2)}, u32[]{:S(2)}) collective-permute-start(bf16[64,1536]{1,0:T(8,128)(2,1)S(1)} %get-tuple-element.14), channel_id=1, source_target_pairs={{0,1},{1,2},{2,3},{3,4},{4,5},{5,6},{6,7},{7,0},{8,9},{9,10},{10,1... | collective-permute-start | bytes 589832 | tf_op jit(solution)/shard_map/ppermute | solution.py:167
  16.1 3.9 %collective-permute-start.3 = (bf16[64,1536]{1,0:T(8,128)(2,1)S(1)}, bf16[64,1536]{1,0:T(8,128)(2,1)S(1)}, u32[]{:S(2)}, u32[]{:S(2)}) collective-permute-start(bf16[64,1536]{1,0:T(8,128)(2,1)S(1)} %get-tuple-element.15), channel_id=1, source_target_pairs={{0,7},{1,0},{2,1},{3,2},{4,3},{5,4},{6,5},{7,6},{8,15},{9,8},{10,9... | collective-permute-start | bytes 589832 | tf_op jit(solution)/shard_map/ppermute | solution.py:168
  19.9 3.6 %all-to-all-done = bf16[8,72,128]{2,1,0:T(8,128)(2,1)S(1)} async-done(((bf16[8,72,128]{2,1,0:T(8,128)(2,1)}), bf16[8,72,128]{2,1,0:T(8,128)(2,1)S(1)}, u32[]{:S(2)}, u32[]{:S(2)}) %all-to-all-start) | async-done | bytes 147488 | tf_op jit(solution)/shard_map/all_to_all | solution.py:160
  23.6 0.0 collective-permute-done.2.left_ref
  23.6 0.0 collective-permute-done.3.right_ref
  23.6 1.2 %broadcast_in_dim.5 = bf16[8,8,72,128]{3,2,1,0:T(8,128)(2,1)} broadcast(bf16[8,72,128]{2,1,0:T(8,128)(2,1)S(1)} %all-to-all-done), dimensions={1,2,3} | broadcast | bytes 1327104 | tf_op jit(solution)/shard_map/broadcast_in_dim | solution.py:172
  24.8 0.0 copy-start.4
  24.8 0.0 copy-start.2
  24.8 7.4 %all-to-all-start.1 = ((bf16[8,8,72,128]{3,2,1,0:T(8,128)(2,1)}), bf16[8,8,72,128]{3,2,1,0:T(8,128)(2,1)S(1)}, u32[]{:S(2)}, u32[]{:S(2)}) async-start(bf16[8,8,72,128]{3,2,1,0:T(8,128)(2,1)} %broadcast_in_dim.5), calls=%async_computation.1 | async-start | bytes 2359296 | tf_op jit(solution)/shard_map/all_to_all | solution.py:171
  32.1 0.0 copy-done.4
  32.2 0.1 pad_add_fusion.1.place_ref
  32.2 0.0 copy-done.2
  32.2 5.0 %shard_map.65.a_ref = bf16[64,1536]{1,0:T(8,128)(2,1)S(1)} custom-call(s32[4]{0:T(128)S(1)} %pad_add_fusion.1.place_ref, bf16[64,1536]{1,0:T(8,128)(2,1)S(1)} %bitcast.25, bf16[64,1536]{1,0:T(8,128)(2,1)S(1)} %bitcast.17, bf16[64,1536]{1,0:T(8,128)(2,1)S(1)} %bitcast.20, bf16[96,1536]{1,0:T(8,128)(2,1)S(1)} %bitcast.24, bf16[96,1536]{1,0:T(8,128)(2,1)S(1)} %bitcast.22, ...), custom_call_target="tpu_custom_call" | custom-call | tf_op jit(solution)/shard_map/pallas_call | solution.py:178
  37.3 2.2 %collective-permute-start.4 = (bf16[64,1536]{1,0:T(8,128)(2,1)S(1)}, bf16[64,1536]{1,0:T(8,128)(2,1)S(1)}, u32[]{:S(2)}, u32[]{:S(2)}) collective-permute-start(bf16[64,1536]{1,0:T(8,128)(2,1)S(1)} %shard_map.65.a_ref), channel_id=1, source_target_pairs={{0,16},{16,0},{1,17},{17,1},{2,18},{18,2},{3,19},{19,3},{4,20},{20... | collective-permute-start | bytes 589832 | tf_op jit(solution)/shard_map/ppermute | solution.py:182
  39.5 1.0 %collective-permute-start.5 = (bf16[64,1536]{1,0:T(8,128)(2,1)S(1)}, bf16[64,1536]{1,0:T(8,128)(2,1)S(1)}, u32[]{:S(2)}, u32[]{:S(2)}) collective-permute-start(bf16[64,1536]{1,0:T(8,128)(2,1)S(1)} %shard_map.65.a_ref), channel_id=1, source_target_pairs={{0,8},{8,0},{1,9},{9,1},{2,10},{10,2},{3,11},{11,3},{4,12},{12,4},... | collective-permute-start | bytes 589832 | tf_op jit(solution)/shard_map/ppermute | solution.py:183
  40.5 11.3 %collective-permute-done.4.b_ref = bf16[64,1536]{1,0:T(8,128)(2,1)S(1)} collective-permute-done((bf16[64,1536]{1,0:T(8,128)(2,1)S(1)}, bf16[64,1536]{1,0:T(8,128)(2,1)S(1)}, u32[]{:S(2)}, u32[]{:S(2)}) %collective-permute-start.4) | collective-permute-done | bytes 196640 | tf_op jit(solution)/shard_map/ppermute | solution.py:182
  51.8 1.1 %collective-permute-start.6 = (bf16[64,1536]{1,0:T(8,128)(2,1)S(1)}, bf16[64,1536]{1,0:T(8,128)(2,1)S(1)}, u32[]{:S(2)}, u32[]{:S(2)}) collective-permute-start(bf16[64,1536]{1,0:T(8,128)(2,1)S(1)} %collective-permute-done.4.b_ref), channel_id=1, source_target_pairs={{0,8},{8,0},{1,9},{9,1},{2,10},{10,2},{3,11},{11,3},{4,12},{12,4},... | collective-permute-start | bytes 589832 | tf_op jit(solution)/shard_map/ppermute | solution.py:184
  52.9 0.0 collective-permute-done.5.c_ref
  53.0 1.1 %collective-permute-done.6.d_ref = bf16[64,1536]{1,0:T(8,128)(2,1)S(1)} collective-permute-done((bf16[64,1536]{1,0:T(8,128)(2,1)S(1)}, bf16[64,1536]{1,0:T(8,128)(2,1)S(1)}, u32[]{:S(2)}, u32[]{:S(2)}) %collective-permute-start.6) | collective-permute-done | bytes 196640 | tf_op jit(solution)/shard_map/ppermute | solution.py:184
  54.0 0.0 all-to-all-done.1
  54.0 0.8 %shard_map.66 = (bf16[64,384]{1,0:T(8,128)(2,1)S(1)}, bf16[64,384]{1,0:T(8,128)(2,1)S(1)}, bf16[64,384]{1,0:T(8,128)(2,1)S(1)}, bf16[64,384]{1,0:T(8,128)(2,1)S(1)}) custom-call(bf16[64,1536]{1,0:T(8,128)(2,1)S(1)} %shard_map.65.a_ref, bf16[64,1536]{1,0:T(8,128)(2,1)S(1)} %collective-permute-done.4.b_ref, bf16[64,1536]{1,0:T(8,128)(2,1)S(1)} %collective-permute-done.5.c_ref, ...), custom_call_target="tpu_custom_call" | custom-call | tf_op jit(solution)/shard_map/pallas_call | solution.py:186
  54.8 0.5 collective-permute-start.7
  55.3 0.0 collective-permute-start.8
  55.3 1.8 %collective-permute-start.9 = (bf16[64,384]{1,0:T(8,128)(2,1)S(1)}, bf16[64,384]{1,0:T(8,128)(2,1)S(1)}, u32[]{:S(2)}, u32[]{:S(2)}) collective-permute-start(bf16[64,384]{1,0:T(8,128)(2,1)S(1)} %get-tuple-element.22), channel_id=1, source_target_pairs={{0,24},{8,16},{16,8},{24,0},{1,25},{9,17},{17,9},{25,1},{2,26},{10... | collective-permute-start | bytes 147464 | tf_op jit(solution)/shard_map/ppermute | solution.py:189
  57.1 0.1 pad_add_fusion.at_ref
  57.2 0.0 collective-permute-done.7.core_ref
  57.2 1.1 %collective-permute-done.8.chip_ref = bf16[64,384]{1,0:T(8,128)(2,1)S(1)} collective-permute-done((bf16[64,384]{1,0:T(8,128)(2,1)S(1)}, bf16[64,384]{1,0:T(8,128)(2,1)S(1)}, u32[]{:S(2)}, u32[]{:S(2)}) %collective-permute-start.8) | collective-permute-done | bytes 49184 | tf_op jit(solution)/shard_map/ppermute | solution.py:190
  58.2 1.6 %collective-permute-done.9.both_ref = bf16[64,384]{1,0:T(8,128)(2,1)S(1)} collective-permute-done((bf16[64,384]{1,0:T(8,128)(2,1)S(1)}, bf16[64,384]{1,0:T(8,128)(2,1)S(1)}, u32[]{:S(2)}, u32[]{:S(2)}) %collective-permute-start.9) | collective-permute-done | bytes 49184 | tf_op jit(solution)/shard_map/ppermute | solution.py:189
  59.8 1.4 %shard_map.67 = bf16[64,1536]{1,0:T(8,128)(2,1)} custom-call(s32[2]{0:T(128)S(1)} %pad_add_fusion.at_ref, bf16[64,384]{1,0:T(8,128)(2,1)S(1)} %get-tuple-element.19.keep_ref, bf16[64,384]{1,0:T(8,128)(2,1)S(1)} %collective-permute-done.7.core_ref, bf16[64,384]{1,0:T(8,128)(2,1)S(1)} %collective-permute-done.8.chip_ref, ...), custom_call_target="tpu_custom_call" | custom-call | tf_op jit(solution)/shard_map/pallas_call | solution.py:193
  (2 shorter events, 0.0 us)
Async XLA Ops:
  0.0 14.4 %copy-start.3 = (bf16[64,160]{1,0:T(8,128)(2,1)S(1)}, bf16[64,160]{1,0:T(8,128)(2,1)}, u32[]{:S(2)}) copy-start(bf16[64,160]{1,0:T(8,128)(2,1)} %constant.33.clone.pick_ref) | copy-start | bytes 61444
  0.0 14.4 %copy-start = (bf16[1,4,16,1536]{3,2,1,0:T(8,128)(2,1)S(1)}, bf16[1,4,16,1536]{3,2,1,0:T(8,128)(2,1)}, u32[]{:S(2)}) copy-start(bf16[1,4,16,1536]{3,2,1,0:T(8,128)(2,1)} %param.7) | copy-start | bytes 589828
  0.0 14.4 %copy-start.1 = (bf16[1,4,16,1536]{3,2,1,0:T(8,128)(2,1)S(1)}, bf16[1,4,16,1536]{3,2,1,0:T(8,128)(2,1)}, u32[]{:S(2)}) copy-start(bf16[1,4,16,1536]{3,2,1,0:T(8,128)(2,1)} %param.8) | copy-start | bytes 589828
  1.2 13.1 %collective-permute-start.1 = (bf16[2,48,1536]{2,1,0:T(8,128)(2,1)S(1)}, bf16[2,48,1536]{2,1,0:T(8,128)(2,1)S(1)}, u32[]{:S(2)}, u32[]{:S(2)}) collective-permute-start(bf16[2,48,1536]{2,1,0:T(8,128)(2,1)S(1)} %get-tuple-element.23), channel_id=1, source_target_pairs={{0,248},{8,0},{16,8},{24,16},{32,24},{40,32},{48,40},{56,48},{64,5... | collective-permute-start | bytes 884744 | tf_op jit(solution)/shard_map/ppermute | solution.py:164
  4.5 9.8 %collective-permute-start = (bf16[2,48,1536]{2,1,0:T(8,128)(2,1)S(1)}, bf16[2,48,1536]{2,1,0:T(8,128)(2,1)S(1)}, u32[]{:S(2)}, u32[]{:S(2)}) collective-permute-start(bf16[2,48,1536]{2,1,0:T(8,128)(2,1)S(1)} %get-tuple-element.24), channel_id=1, source_target_pairs={{0,8},{8,16},{16,24},{24,32},{32,40},{40,48},{48,56},{56,64},{64,7... | collective-permute-start | bytes 884744 | tf_op jit(solution)/shard_map/ppermute | solution.py:163
  6.7 16.8 %all-to-all-start = ((bf16[8,72,128]{2,1,0:T(8,128)(2,1)}), bf16[8,72,128]{2,1,0:T(8,128)(2,1)S(1)}, u32[]{:S(2)}, u32[]{:S(2)}) async-start(bf16[8,72,128]{2,1,0:T(8,128)(2,1)} %broadcast_in_dim.4), calls=%async_computation | async-start | bytes 294912 | tf_op jit(solution)/shard_map/all_to_all | solution.py:160
  14.7 8.9 %collective-permute-start.2 = (bf16[64,1536]{1,0:T(8,128)(2,1)S(1)}, bf16[64,1536]{1,0:T(8,128)(2,1)S(1)}, u32[]{:S(2)}, u32[]{:S(2)}) collective-permute-start(bf16[64,1536]{1,0:T(8,128)(2,1)S(1)} %get-tuple-element.14), channel_id=1, source_target_pairs={{0,1},{1,2},{2,3},{3,4},{4,5},{5,6},{6,7},{7,0},{8,9},{9,10},{10,1... | collective-permute-start | bytes 589832 | tf_op jit(solution)/shard_map/ppermute | solution.py:167
  16.1 7.5 %collective-permute-start.3 = (bf16[64,1536]{1,0:T(8,128)(2,1)S(1)}, bf16[64,1536]{1,0:T(8,128)(2,1)S(1)}, u32[]{:S(2)}, u32[]{:S(2)}) collective-permute-start(bf16[64,1536]{1,0:T(8,128)(2,1)S(1)} %get-tuple-element.15), channel_id=1, source_target_pairs={{0,7},{1,0},{2,1},{3,2},{4,3},{5,4},{6,5},{7,6},{8,15},{9,8},{10,9... | collective-permute-start | bytes 589832 | tf_op jit(solution)/shard_map/ppermute | solution.py:168
  24.8 7.4 %copy-start.4 = (f32[24,49]{1,0:T(8,128)S(1)}, f32[24,49]{1,0:T(8,128)}, u32[]{:S(2)}) copy-start(f32[24,49]{1,0:T(8,128)} %param.9) | copy-start | bytes 14116
  24.8 7.5 %copy-start.2 = (bf16[1,4,16,1536]{3,2,1,0:T(8,128)(2,1)S(1)}, bf16[1,4,16,1536]{3,2,1,0:T(8,128)(2,1)}, u32[]{:S(2)}) copy-start(bf16[1,4,16,1536]{3,2,1,0:T(8,128)(2,1)} %param.6) | copy-start | bytes 589828
  24.8 29.2 %all-to-all-start.1 = ((bf16[8,8,72,128]{3,2,1,0:T(8,128)(2,1)}), bf16[8,8,72,128]{3,2,1,0:T(8,128)(2,1)S(1)}, u32[]{:S(2)}, u32[]{:S(2)}) async-start(bf16[8,8,72,128]{3,2,1,0:T(8,128)(2,1)} %broadcast_in_dim.5), calls=%async_computation.1 | async-start | bytes 2359296 | tf_op jit(solution)/shard_map/all_to_all | solution.py:171
  37.3 14.5 %collective-permute-start.4 = (bf16[64,1536]{1,0:T(8,128)(2,1)S(1)}, bf16[64,1536]{1,0:T(8,128)(2,1)S(1)}, u32[]{:S(2)}, u32[]{:S(2)}) collective-permute-start(bf16[64,1536]{1,0:T(8,128)(2,1)S(1)} %shard_map.65.a_ref), channel_id=1, source_target_pairs={{0,16},{16,0},{1,17},{17,1},{2,18},{18,2},{3,19},{19,3},{4,20},{20... | collective-permute-start | bytes 589832 | tf_op jit(solution)/shard_map/ppermute | solution.py:182
  39.5 13.5 %collective-permute-start.5 = (bf16[64,1536]{1,0:T(8,128)(2,1)S(1)}, bf16[64,1536]{1,0:T(8,128)(2,1)S(1)}, u32[]{:S(2)}, u32[]{:S(2)}) collective-permute-start(bf16[64,1536]{1,0:T(8,128)(2,1)S(1)} %shard_map.65.a_ref), channel_id=1, source_target_pairs={{0,8},{8,0},{1,9},{9,1},{2,10},{10,2},{3,11},{11,3},{4,12},{12,4},... | collective-permute-start | bytes 589832 | tf_op jit(solution)/shard_map/ppermute | solution.py:183
  51.8 2.2 %collective-permute-start.6 = (bf16[64,1536]{1,0:T(8,128)(2,1)S(1)}, bf16[64,1536]{1,0:T(8,128)(2,1)S(1)}, u32[]{:S(2)}, u32[]{:S(2)}) collective-permute-start(bf16[64,1536]{1,0:T(8,128)(2,1)S(1)} %collective-permute-done.4.b_ref), channel_id=1, source_target_pairs={{0,8},{8,0},{1,9},{9,1},{2,10},{10,2},{3,11},{11,3},{4,12},{12,4},... | collective-permute-start | bytes 589832 | tf_op jit(solution)/shard_map/ppermute | solution.py:184
  54.8 2.3 %collective-permute-start.7 = (bf16[64,384]{1,0:T(8,128)(2,1)S(1)}, bf16[64,384]{1,0:T(8,128)(2,1)S(1)}, u32[]{:S(2)}, u32[]{:S(2)}) collective-permute-start(bf16[64,384]{1,0:T(8,128)(2,1)S(1)} %get-tuple-element.20), channel_id=1, source_target_pairs={{0,8},{8,0},{1,9},{9,1},{2,10},{10,2},{3,11},{11,3},{4,12},{12,4},... | collective-permute-start | bytes 147464 | tf_op jit(solution)/shard_map/ppermute | solution.py:191
  55.3 2.9 %collective-permute-start.8 = (bf16[64,384]{1,0:T(8,128)(2,1)S(1)}, bf16[64,384]{1,0:T(8,128)(2,1)S(1)}, u32[]{:S(2)}, u32[]{:S(2)}) collective-permute-start(bf16[64,384]{1,0:T(8,128)(2,1)S(1)} %get-tuple-element.21), channel_id=1, source_target_pairs={{0,16},{16,0},{1,17},{17,1},{2,18},{18,2},{3,19},{19,3},{4,20},{20... | collective-permute-start | bytes 147464 | tf_op jit(solution)/shard_map/ppermute | solution.py:190
  55.3 4.5 %collective-permute-start.9 = (bf16[64,384]{1,0:T(8,128)(2,1)S(1)}, bf16[64,384]{1,0:T(8,128)(2,1)S(1)}, u32[]{:S(2)}, u32[]{:S(2)}) collective-permute-start(bf16[64,384]{1,0:T(8,128)(2,1)S(1)} %get-tuple-element.22), channel_id=1, source_target_pairs={{0,24},{8,16},{16,8},{24,0},{1,25},{9,17},{17,9},{25,1},{2,26},{10... | collective-permute-start | bytes 147464 | tf_op jit(solution)/shard_map/ppermute | solution.py:189

commit v4 on v3

--- a/solution.py
+++ b/solution.py
@@ -27,6 +27,13 @@
                     source = 112 + (r - 7) * 16 + x
                 pick[side * 32 + r * 3 + j, source] = 1.0
     return pick
+
+
+def weight_kernel(wt_ref, out_ref):
+    w = wt_ref[...]
+    packed = jnp.concatenate([w[:, :128], jnp.concatenate([w[:24, 128:], w[24:, 128:]], 1)], 0)
+    for n in range(out_ref.shape[0]):
+        out_ref[n] = packed
 
 
 def pack_kernel(pick_ref, k_ref, v_ref, top_ref, bot_ref, left_ref, right_ref):
@@ -98,21 +105,26 @@
         o_ref[:, c] = jnp.where(low, o[:64], o[64:]).astype(BF)
 
 
-def project_kernel(a_ref, b_ref, c_ref, d_ref, w_ref, keep_ref, chip_ref, core_ref, both_ref):
+def unpack_kernel(w0_ref, w1_ref, w3_ref, w2_ref, out_ref):
+    for xh in range(2):
+        for k, w_ref in enumerate((w0_ref, w1_ref, w2_ref, w3_ref)):
+            for z in range(8):
+                w = w_ref[xh, z]
+                tail = w[48:]
+                tail = jnp.concatenate([tail[:, :64], tail[:, 64:]], 0)
+                out_ref[xh * 4 + k, z * 48 : z * 48 + 48, :] = jnp.concatenate([w[:48], tail], 1)
+
+
+def project_kernel(y_ref, a_ref, b_ref, c_ref, d_ref, w_ref, keep_ref, chip_ref, core_ref, both_ref):
     mixed = jnp.concatenate([a_ref[...], b_ref[...], c_ref[...], d_ref[...]], 0)
+    odd, upper = (y_ref[0] & 1) == 1, y_ref[0] >= 2
     total = None
     for xh in range(2):
-        for y in range(4):
-            block = xh * 4 + y
-            feats = mixed[:, block * 192 : block * 192 + 192]
-            parts = []
-            for z in range(8):
-                w = w_ref[xh, y, z]
-                tail = w[48:]
-                tail = jnp.concatenate([tail[:, :64], tail[:, 64:]], 0)
-                parts.append(jnp.concatenate([w[:48], tail], 1))
-            wt = jnp.concatenate(parts, 0)
-            term = lax.dot_general(feats, wt, NT, preferred_element_type=F32)
+        f = [mixed[:, xh * 768 + n * 192 : xh * 768 + n * 192 + 192] for n in range(4)]
+        f = [jnp.where(odd, f[n ^ 1], f[n]) for n in range(4)]
+        f = [jnp.where(upper, f[n ^ 2], f[n]) for n in range(4)]
+        for k in range(4):
+            term = lax.dot_general(f[k], w_ref[xh * 4 + k], NT, preferred_element_type=F32)
             total = term if total is None else total + term
     out = total.astype(BF)
     for n, ref in enumerate((keep_ref, chip_ref, core_ref, both_ref)):
@@ -120,26 +132,24 @@
 
 
 def assemble_kernel(at_ref, keep_ref, core_ref, chip_ref, both_ref, o_ref):
-    xl, core = at_ref[0] == 0, at_ref[1] == 0
-    mine, other, far, far_other = (ref[...].astype(F32) for ref in (keep_ref, core_ref, chip_ref, both_ref))
-    here0, here1 = jnp.where(core, mine, other), jnp.where(core, other, mine)
-    far0, far1 = jnp.where(core, far, far_other), jnp.where(core, far_other, far)
-    quarters = (
-        jnp.where(xl, here0, far0),
-        jnp.where(xl, here1, far1),
-        jnp.where(xl, far0, here0),
-        jnp.where(xl, far1, here1),
-    )
-    pieces = [part[:, n * 48 : n * 48 + 48] for n in range(8) for part in quarters]
-    o_ref[...] = jnp.concatenate(pieces, 1).astype(BF)
-
-
-def call(kernel, outs, n_in, smem=(), limit=48):
+    parts = (keep_ref, core_ref, chip_ref, both_ref)
+    for me in range(4):
+
+        @pl.when(at_ref[0] * 2 + at_ref[1] == me)
+        def _():
+            quarters = [parts[me ^ q][...] for q in range(4)]
+            pieces = [part[:, n * 48 : n * 48 + 48] for n in range(8) for part in quarters]
+            o_ref[...] = jnp.concatenate(pieces, 1)
+
+
+def call(kernel, outs, n_in, smem=(), limit=48, flops=0):
+    cost = pl.CostEstimate(flops=flops, bytes_accessed=4 * 1024 * 1024, transcendentals=0) if flops else None
     return pl.pallas_call(
         kernel,
         out_shape=outs,
         in_specs=[SM if k in smem else VM for k in range(n_in)],
         out_specs=VM if isinstance(outs, jax.ShapeDtypeStruct) else tuple(VM for _ in outs),
+        cost_estimate=cost,
         compiler_params=pltpu.CompilerParams(vmem_limit_bytes=limit * 1024 * 1024),
     )
 
@@ -155,36 +165,34 @@
     right = [(n, (n + 1) % nc) for n in range(nc)]
     left = [(n, (n - 1) % nc) for n in range(nc)]
     k, v, q = (a.reshape(64, width) for a in (key_tokens, values, queries))
-    wt = out_weight.T
-    packed = jnp.concatenate([wt[:, :128], jnp.concatenate([wt[:24, 128:], wt[24:, 128:]], 1)], 0)
-    along_z = lax.all_to_all(jnp.broadcast_to(packed[None], (8, 72, 128)), "z", 0, 0, tiled=True)
+    packed = call(weight_kernel, jax.ShapeDtypeStruct((16, 72, 128), BF), 1)(out_weight.T)
+    along_zx = lax.all_to_all(packed, ("xh", "z"), 0, 0, tiled=True)
 
     both = jnp.stack([k, v], 0)
     top = lax.ppermute(both[:, 16:], rows, down).reshape(96, width)
     bot = lax.ppermute(both[:, :48], rows, up).reshape(96, width)
     side = jax.ShapeDtypeStruct((64, width), BF)
-    to_left, to_right = call(pack_kernel, (side, side), 5)(jnp.asarray(col_pick(), BF), k, v, top, bot)
+    to_left, to_right = call(pack_kernel, (side, side), 5, flops=50000000000)(jnp.asarray(col_pick(), BF), k, v, top, bot)
     from_left = lax.ppermute(to_right, cols, right)
     from_right = lax.ppermute(to_left, cols, left)
 
-    from_left, from_right, along_z = lax.optimization_barrier((from_left, from_right, along_z))
-    plane = lax.all_to_all(
-        jnp.broadcast_to(along_z[None], (8, 8, 72, 128)), ("xh", "y"), 0, 0, tiled=True
-    )
-    weights = plane.reshape(2, 4, 8, 72, 128)
+    near = along_zx.reshape(2, 8, 72, 128)
+    stages = [near] + [lax.ppermute(near, "y", [(n, n ^ k) for n in range(4)]) for k in (1, 3, 2)]
 
     place = jnp.stack([r * 4, c * 16, nr * 4, nc * 16]).astype(jnp.int32)
     bias = jnp.pad(position_bias, ((0, 0), (0, 128 - 49)), constant_values=-jnp.inf)
-    mixed = call(attention_kernel, side, 9, smem=(0,))(
+    mixed = call(attention_kernel, side, 9, smem=(0,), flops=50000000000)(
         place, q, k, v, top, bot, from_left, from_right, bias
     )
     swap = [(0, 1), (1, 0)]
     next_mixed = lax.ppermute(mixed, "xl", swap)
     core_mixed = lax.ppermute(mixed, "core", swap)
     both_mixed = lax.ppermute(next_mixed, "core", swap)
+    weights = call(unpack_kernel, jax.ShapeDtypeStruct((8, 384, 192), BF), 4, flops=100000000000)(*stages)
     part = jax.ShapeDtypeStruct((64, width // 4), BF)
-    keep, to_chip, to_core, to_both = call(project_kernel, (part,) * 4, 5)(
-        mixed, next_mixed, core_mixed, both_mixed, weights
+    y = lax.axis_index("y").astype(jnp.int32).reshape(1)
+    keep, to_chip, to_core, to_both = call(project_kernel, (part,) * 4, 6, smem=(0,))(
+        y, mixed, next_mixed, core_mixed, both_mixed, weights
     )
     by_both = lax.ppermute(to_both, ("xl", "core"), [(n, 3 - n) for n in range(4)])
     by_chip = lax.ppermute(to_chip, "xl", swap)

time: 62.1 us -> 53.3 us (0.86); the launches traced: 61.3 us -> 53.1 us
  waiting for transfers between devices: 18.6 us -> 12.8 us
  local copies, waits for them, and re-layouts: 3.32 us -> 0.77 us
  Pallas kernels: 7.54 us -> 8.63 us
  starting transfers between devices: 30.2 us -> 29.4 us
    ppermute x1, waiting for transfers between devices: 11.3 us -> 3.1 us  [shards(): next_mixed = lax.ppermute(mixed, 'xl', swap)]
    all_to_all x2 -> x1, starting transfers between devices: 15 us -> 10.1 us  [shards(): along_zx = lax.all_to_all(packed, ('xh', 'z'), 0, 0, tiled=True)]
    ppermute x0 -> x3, starting transfers between devices: none -> 3.69 us  [shards(): lax.ppermute(near, 'y', [(n, n ^ k) for n in range(4)])]
    all_to_all x2 -> x1, waiting for transfers between devices: 3.63 us -> 6.01 us  [shards(): along_zx = lax.all_to_all(packed, ('xh', 'z'), 0, 0, tiled=True)]
    broadcast_in_dim x2 -> x0, local copies, waits for them, and re-layouts: 1.87 us -> none  [the longest x1 1.19 us: shards(): jnp.broadcast_to(along_z[None], (8, 8, 72, 128))]
    slice x2 -> x0, local copies, waits for them, and re-layouts: 1.42 us -> none  [the longest x1 0.71 us: shards(): wt[:24, 128:]]
    ppermute x1, starting transfers between devices: 1.15 us -> 2.5 us  [shards(): both_mixed = lax.ppermute(next_mixed, 'core', swap)]
    ppermute x1, starting transfers between devices: 2.21 us -> 1.01 us  [shards(): next_mixed = lax.ppermute(mixed, 'xl', swap)]
  transfers between devices with their start and end apart: 12 -> 14, of which waited for: 5 -> 6; matrix products, arithmetic and copies ran while one was open for 4% -> 0% of each run, Pallas kernels for 9% -> 12%
where the time goes in v4:
time: 53.3 us; the launch traced here: 53.1 us
  starting transfers between devices  29.4 us (55%)
  waiting for transfers between devices  12.8 us (24%)
  Pallas kernels  8.63 us (16%)
  other arithmetic  1.37 us (3%)
  local copies, waits for them, and re-layouts  0.77 us (1%)
    all_to_all x1, starting transfers between devices, shards(): along_zx = lax.all_to_all(packed, ('xh', 'z'), 0, 0, tiled=True)  10.1 us
    all_to_all x1, waiting for transfers between devices, shards(): along_zx = lax.all_to_all(packed, ('xh', 'z'), 0, 0, tiled=True)  6.01 us
    pallas_call x1, Pallas kernels, shards(): call(attention_kernel, side, 9, smem=(0,), flops=50000000000)  5.02 us
    ppermute x1, starting transfers between devices, shards(): from_right = lax.ppermute(to_left, cols, left)  4.11 us
    ppermute x3, starting transfers between devices, shards(): lax.ppermute(near, 'y', [(n, n ^ k) for n in range(4)])  3.69 us
    ppermute x1, starting transfers between devices, shards(): bot = lax.ppermute(both[:, :48], rows, up).reshape(96, width)  3.31 us
    ppermute x1, waiting for transfers between devices, shards(): next_mixed = lax.ppermute(mixed, 'xl', swap)  3.1 us
    ppermute x1, starting transfers between devices, shards(): both_mixed = lax.ppermute(next_mixed, 'core', swap)  2.5 us
  transfers between devices with their start and end apart: 14, of which 6 were waited for; matrix products, arithmetic and copies ran while one was open for 0% of the time, Pallas kernels for 12%

profile of v4, /device:TPU:1, one launch (start us, length us, event | category | flops | bytes accessed | tf_op | source)
XLA Modules:
  0.0 53.1 jit_solution(6872781415584082244)
XLA Ops:
  0.0 0.0 copy-start.4
  0.0 0.0 copy-start
  0.0 0.0 copy-start.1
  0.0 1.2 %pad_maximum_fusion = (bf16[2,48,1536]{2,1,0:T(8,128)(2,1)S(1)}, bf16[2,48,1536]{2,1,0:T(8,128)(2,1)S(1)}) fusion(bf16[1,64,1536]{2,1,0:T(8,128)(2,1)} %bitcast.22, bf16[1,64,1536]{2,1,0:T(8,128)(2,1)} %bitcast.19), kind=kLoop, calls=%fused_computation.3 | loop fusion | flops 1179648 | bytes 983040 | tf_op jit(solution)/shard_map/stack | solution.py:171
  1.2 3.3 %collective-permute-start.1 = (bf16[2,48,1536]{2,1,0:T(8,128)(2,1)S(1)}, bf16[2,48,1536]{2,1,0:T(8,128)(2,1)S(1)}, u32[]{:S(2)}, u32[]{:S(2)}) collective-permute-start(bf16[2,48,1536]{2,1,0:T(8,128)(2,1)S(1)} %get-tuple-element.17), channel_id=1, source_target_pairs={{0,248},{8,0},{16,8},{24,16},{32,24},{40,32},{48,40},{56,48},{64,5... | collective-permute-start | bytes 884744 | tf_op jit(solution)/shard_map/ppermute | solution.py:173
  4.5 0.0 collective-permute-start
  4.5 0.7 %copy-done.2 = bf16[192,48]{0,1:T(8,128)(2,1)S(1)} copy-done((bf16[192,48]{0,1:T(8,128)(2,1)S(1)}, bf16[192,48]{0,1:T(8,128)(2,1)}, u32[]{:S(2)}) %copy-start.2) | copy-done | bytes 18456
  5.3 0.8 %shard_map.66 = bf16[16,72,128]{2,1,0:T(8,128)(2,1)} custom-call(bf16[48,192]{1,0:T(8,128)(2,1)S(1)} %bitcast.25), custom_call_target="tpu_custom_call" | custom-call | tf_op jit(solution)/shard_map/pallas_call | solution.py:168
  6.1 10.1 %all-to-all-start = ((bf16[16,72,128]{2,1,0:T(8,128)(2,1)}), bf16[16,72,128]{2,1,0:T(8,128)(2,1)S(1)}, u32[]{:S(2)}, u32[]{:S(2)}) async-start(bf16[16,72,128]{2,1,0:T(8,128)(2,1)} %shard_map.66), calls=%async_computation | async-start | bytes 589824 | tf_op jit(solution)/shard_map/all_to_all | solution.py:169
  16.2 0.0 collective-permute-done.1
  16.2 0.0 collective-permute-done
  16.2 0.0 copy-done.4
  16.2 0.0 copy-done
  16.2 0.0 copy-done.1
  16.2 0.0 copy-start.5
  16.2 0.0 copy-start.3
  16.3 0.3 shard_map.64
  16.5 1.4 %collective-permute-start.2 = (bf16[64,1536]{1,0:T(8,128)(2,1)S(1)}, bf16[64,1536]{1,0:T(8,128)(2,1)S(1)}, u32[]{:S(2)}, u32[]{:S(2)}) collective-permute-start(bf16[64,1536]{1,0:T(8,128)(2,1)S(1)} %get-tuple-element.11), channel_id=1, source_target_pairs={{0,1},{1,2},{2,3},{3,4},{4,5},{5,6},{6,7},{7,0},{8,9},{9,10},{10,1... | collective-permute-start | bytes 589832 | tf_op jit(solution)/shard_map/ppermute | solution.py:176
  17.9 4.1 %collective-permute-start.3 = (bf16[64,1536]{1,0:T(8,128)(2,1)S(1)}, bf16[64,1536]{1,0:T(8,128)(2,1)S(1)}, u32[]{:S(2)}, u32[]{:S(2)}) collective-permute-start(bf16[64,1536]{1,0:T(8,128)(2,1)S(1)} %get-tuple-element.12), channel_id=1, source_target_pairs={{0,7},{1,0},{2,1},{3,2},{4,3},{5,4},{6,5},{7,6},{8,15},{9,8},{10,9... | collective-permute-start | bytes 589832 | tf_op jit(solution)/shard_map/ppermute | solution.py:177
  22.0 0.0 copy-done.5
  22.0 0.1 pad_add_fusion.1.place_ref
  22.1 6.0 %all-to-all-done = bf16[16,72,128]{2,1,0:T(8,128)(2,1)S(1)} async-done(((bf16[16,72,128]{2,1,0:T(8,128)(2,1)}), bf16[16,72,128]{2,1,0:T(8,128)(2,1)S(1)}, u32[]{:S(2)}, u32[]{:S(2)}) %all-to-all-start) | async-done | bytes 294944 | tf_op jit(solution)/shard_map/all_to_all | solution.py:169
  28.1 2.9 %collective-permute-start.9 = (bf16[2,8,72,128]{3,2,1,0:T(8,128)(2,1)S(1)}, bf16[2,8,72,128]{3,2,1,0:T(8,128)(2,1)S(1)}, u32[]{:S(2)}, u32[]{:S(2)}) collective-permute-start(bf16[2,8,72,128]{3,2,1,0:T(8,128)(2,1)S(1)} %bitcast.15), channel_id=1, source_target_pairs={{0,2},{1,3},{2,0},{3,1},{4,6},{5,7},{6,4},{7,5},{8,10},{9,11},{10,... | collective-permute-start | bytes 884744 | tf_op jit(solution)/shard_map/ppermute | solution.py:180
  31.0 0.8 %collective-permute-start.8 = (bf16[2,8,72,128]{3,2,1,0:T(8,128)(2,1)S(1)}, bf16[2,8,72,128]{3,2,1,0:T(8,128)(2,1)S(1)}, u32[]{:S(2)}, u32[]{:S(2)}) collective-permute-start(bf16[2,8,72,128]{3,2,1,0:T(8,128)(2,1)S(1)} %bitcast.16), channel_id=1, source_target_pairs={{0,3},{1,2},{2,1},{3,0},{4,7},{5,6},{6,5},{7,4},{8,11},{9,10},{10,... | collective-permute-start | bytes 884744 | tf_op jit(solution)/shard_map/ppermute | solution.py:180
  31.8 0.0 collective-permute-start.7
  31.8 0.0 collective-permute-done.2.left_ref
  31.8 0.0 collective-permute-done.3.right_ref
  31.8 0.0 copy-done.3
  31.8 5.0 %shard_map.65.a_ref = bf16[64,1536]{1,0:T(8,128)(2,1)S(1)} custom-call(s32[4]{0:T(128)S(1)} %pad_add_fusion.1.place_ref, bf16[64,1536]{1,0:T(8,128)(2,1)S(1)} %bitcast.30, bf16[64,1536]{1,0:T(8,128)(2,1)S(1)} %bitcast.21, bf16[64,1536]{1,0:T(8,128)(2,1)S(1)} %bitcast.24, bf16[96,1536]{1,0:T(8,128)(2,1)S(1)} %bitcast.29, bf16[96,1536]{1,0:T(8,128)(2,1)S(1)} %bitcast.27, ...), custom_call_target="tpu_custom_call" | custom-call | flops 49999998976 | bytes 4194304 | tf_op jit(solution)/shard_map/pallas_call | solution.py:184
  36.9 1.0 %collective-permute-start.4 = (bf16[64,1536]{1,0:T(8,128)(2,1)S(1)}, bf16[64,1536]{1,0:T(8,128)(2,1)S(1)}, u32[]{:S(2)}, u32[]{:S(2)}) collective-permute-start(bf16[64,1536]{1,0:T(8,128)(2,1)S(1)} %shard_map.65.a_ref), channel_id=1, source_target_pairs={{0,16},{16,0},{1,17},{17,1},{2,18},{18,2},{3,19},{19,3},{4,20},{20... | collective-permute-start | bytes 589832 | tf_op jit(solution)/shard_map/ppermute | solution.py:188
  37.9 0.8 %collective-permute-start.5 = (bf16[64,1536]{1,0:T(8,128)(2,1)S(1)}, bf16[64,1536]{1,0:T(8,128)(2,1)S(1)}, u32[]{:S(2)}, u32[]{:S(2)}) collective-permute-start(bf16[64,1536]{1,0:T(8,128)(2,1)S(1)} %shard_map.65.a_ref), channel_id=1, source_target_pairs={{0,8},{8,0},{1,9},{9,1},{2,10},{10,2},{3,11},{11,3},{4,12},{12,4},... | collective-permute-start | bytes 589832 | tf_op jit(solution)/shard_map/ppermute | solution.py:189
  38.7 3.1 %collective-permute-done.4.b_ref = bf16[64,1536]{1,0:T(8,128)(2,1)S(1)} collective-permute-done((bf16[64,1536]{1,0:T(8,128)(2,1)S(1)}, bf16[64,1536]{1,0:T(8,128)(2,1)S(1)}, u32[]{:S(2)}, u32[]{:S(2)}) %collective-permute-start.4) | collective-permute-done | bytes 196640 | tf_op jit(solution)/shard_map/ppermute | solution.py:188
  41.8 2.5 %collective-permute-start.6 = (bf16[64,1536]{1,0:T(8,128)(2,1)S(1)}, bf16[64,1536]{1,0:T(8,128)(2,1)S(1)}, u32[]{:S(2)}, u32[]{:S(2)}) collective-permute-start(bf16[64,1536]{1,0:T(8,128)(2,1)S(1)} %collective-permute-done.4.b_ref), channel_id=1, source_target_pairs={{0,8},{8,0},{1,9},{9,1},{2,10},{10,2},{3,11},{11,3},{4,12},{12,4},... | collective-permute-start | bytes 589832 | tf_op jit(solution)/shard_map/ppermute | solution.py:190
  44.3 0.0 collective-permute-done.9.w2_ref
  44.3 0.6 %collective-permute-done.8.w3_ref = bf16[2,8,72,128]{3,2,1,0:T(8,128)(2,1)S(1)} collective-permute-done((bf16[2,8,72,128]{3,2,1,0:T(8,128)(2,1)S(1)}, bf16[2,8,72,128]{3,2,1,0:T(8,128)(2,1)S(1)}, u32[]{:S(2)}, u32[]{:S(2)}) %collective-permute-start.8) | collective-permute-done | bytes 294944 | tf_op jit(solution)/shard_map/ppermute | solution.py:180
  44.9 0.0 collective-permute-done.7.w1_ref
  44.9 0.2 shard_map.67.w_ref
  45.1 0.0 collective-permute-done.5.c_ref
  45.1 0.2 collective-permute-done.6.d_ref
  45.3 0.9 %shard_map.68 = (bf16[64,384]{1,0:T(8,128)(2,1)S(1)}, bf16[64,384]{1,0:T(8,128)(2,1)S(1)}, bf16[64,384]{1,0:T(8,128)(2,1)S(1)}, bf16[64,384]{1,0:T(8,128)(2,1)S(1)}) custom-call(s32[1]{0:T(128)} %bitcast.2.y_ref, bf16[64,1536]{1,0:T(8,128)(2,1)S(1)} %shard_map.65.a_ref, bf16[64,1536]{1,0:T(8,128)(2,1)S(1)} %collective-permute-done.4.b_ref, ...), custom_call_target="tpu_custom_call" | custom-call | tf_op jit(solution)/shard_map/pallas_call | solution.py:194
  46.2 0.7 %collective-permute-start.10 = (bf16[64,384]{1,0:T(8,128)(2,1)S(1)}, bf16[64,384]{1,0:T(8,128)(2,1)S(1)}, u32[]{:S(2)}, u32[]{:S(2)}) collective-permute-start(bf16[64,384]{1,0:T(8,128)(2,1)S(1)} %get-tuple-element.14), channel_id=1, source_target_pairs={{0,8},{8,0},{1,9},{9,1},{2,10},{10,2},{3,11},{11,3},{4,12},{12,4},... | collective-permute-start | bytes 147464 | tf_op jit(solution)/shard_map/ppermute | solution.py:199
  47.0 0.9 %collective-permute-start.11 = (bf16[64,384]{1,0:T(8,128)(2,1)S(1)}, bf16[64,384]{1,0:T(8,128)(2,1)S(1)}, u32[]{:S(2)}, u32[]{:S(2)}) collective-permute-start(bf16[64,384]{1,0:T(8,128)(2,1)S(1)} %get-tuple-element.15), channel_id=1, source_target_pairs={{0,16},{16,0},{1,17},{17,1},{2,18},{18,2},{3,19},{19,3},{4,20},{20... | collective-permute-start | bytes 147464 | tf_op jit(solution)/shard_map/ppermute | solution.py:198
  47.9 0.8 %collective-permute-start.12 = (bf16[64,384]{1,0:T(8,128)(2,1)S(1)}, bf16[64,384]{1,0:T(8,128)(2,1)S(1)}, u32[]{:S(2)}, u32[]{:S(2)}) collective-permute-start(bf16[64,384]{1,0:T(8,128)(2,1)S(1)} %get-tuple-element.16), channel_id=1, source_target_pairs={{0,24},{8,16},{16,8},{24,0},{1,25},{9,17},{17,9},{25,1},{2,26},{10... | collective-permute-start | bytes 147464 | tf_op jit(solution)/shard_map/ppermute | solution.py:197
  48.7 0.1 pad_add_fusion.at_ref
  48.8 0.0 collective-permute-done.10.core_ref
  48.8 1.1 %collective-permute-done.11.chip_ref = bf16[64,384]{1,0:T(8,128)(2,1)S(1)} collective-permute-done((bf16[64,384]{1,0:T(8,128)(2,1)S(1)}, bf16[64,384]{1,0:T(8,128)(2,1)S(1)}, u32[]{:S(2)}, u32[]{:S(2)}) %collective-permute-start.11) | collective-permute-done | bytes 49184 | tf_op jit(solution)/shard_map/ppermute | solution.py:198
  49.9 1.7 %collective-permute-done.12.both_ref = bf16[64,384]{1,0:T(8,128)(2,1)S(1)} collective-permute-done((bf16[64,384]{1,0:T(8,128)(2,1)S(1)}, bf16[64,384]{1,0:T(8,128)(2,1)S(1)}, u32[]{:S(2)}, u32[]{:S(2)}) %collective-permute-start.12) | collective-permute-done | bytes 49184 | tf_op jit(solution)/shard_map/ppermute | solution.py:197
  51.6 1.5 %shard_map.69 = bf16[64,1536]{1,0:T(8,128)(2,1)} custom-call(s32[2]{0:T(128)S(1)} %pad_add_fusion.at_ref, bf16[64,384]{1,0:T(8,128)(2,1)S(1)} %get-tuple-element.13.keep_ref, bf16[64,384]{1,0:T(8,128)(2,1)S(1)} %collective-permute-done.10.core_ref, bf16[64,384]{1,0:T(8,128)(2,1)S(1)} %collective-permute-done.11.chip_ref, ...), custom_call_target="tpu_custom_call" | custom-call | tf_op jit(solution)/shard_map/pallas_call | solution.py:201
  (3 shorter events, 0.0 us)
Async XLA Ops:
  0.0 16.2 %copy-start.4 = (bf16[64,160]{1,0:T(8,128)(2,1)S(1)}, bf16[64,160]{1,0:T(8,128)(2,1)}, u32[]{:S(2)}) copy-start(bf16[64,160]{1,0:T(8,128)(2,1)} %constant.33.clone.pick_ref) | copy-start | bytes 61444
  0.0 16.2 %copy-start = (bf16[1,4,16,1536]{3,2,1,0:T(8,128)(2,1)S(1)}, bf16[1,4,16,1536]{3,2,1,0:T(8,128)(2,1)}, u32[]{:S(2)}) copy-start(bf16[1,4,16,1536]{3,2,1,0:T(8,128)(2,1)} %param.7) | copy-start | bytes 589828
  0.0 16.2 %copy-start.1 = (bf16[1,4,16,1536]{3,2,1,0:T(8,128)(2,1)S(1)}, bf16[1,4,16,1536]{3,2,1,0:T(8,128)(2,1)}, u32[]{:S(2)}) copy-start(bf16[1,4,16,1536]{3,2,1,0:T(8,128)(2,1)} %param.8) | copy-start | bytes 589828
  1.2 15.0 %collective-permute-start.1 = (bf16[2,48,1536]{2,1,0:T(8,128)(2,1)S(1)}, bf16[2,48,1536]{2,1,0:T(8,128)(2,1)S(1)}, u32[]{:S(2)}, u32[]{:S(2)}) collective-permute-start(bf16[2,48,1536]{2,1,0:T(8,128)(2,1)S(1)} %get-tuple-element.17), channel_id=1, source_target_pairs={{0,248},{8,0},{16,8},{24,16},{32,24},{40,32},{48,40},{56,48},{64,5... | collective-permute-start | bytes 884744 | tf_op jit(solution)/shard_map/ppermute | solution.py:173
  4.5 11.6 %collective-permute-start = (bf16[2,48,1536]{2,1,0:T(8,128)(2,1)S(1)}, bf16[2,48,1536]{2,1,0:T(8,128)(2,1)S(1)}, u32[]{:S(2)}, u32[]{:S(2)}) collective-permute-start(bf16[2,48,1536]{2,1,0:T(8,128)(2,1)S(1)} %get-tuple-element.18), channel_id=1, source_target_pairs={{0,8},{8,16},{16,24},{24,32},{32,40},{40,48},{48,56},{56,64},{64,7... | collective-permute-start | bytes 884744 | tf_op jit(solution)/shard_map/ppermute | solution.py:172
  4.5 0.7 %copy-start.2 = (bf16[192,48]{0,1:T(8,128)(2,1)S(1)}, bf16[192,48]{0,1:T(8,128)(2,1)}, u32[]{:S(2)}) copy-start(bf16[192,48]{0,1:T(8,128)(2,1)} %param.10) | copy-start | bytes 55300
  6.1 22.0 %all-to-all-start = ((bf16[16,72,128]{2,1,0:T(8,128)(2,1)}), bf16[16,72,128]{2,1,0:T(8,128)(2,1)S(1)}, u32[]{:S(2)}, u32[]{:S(2)}) async-start(bf16[16,72,128]{2,1,0:T(8,128)(2,1)} %shard_map.66), calls=%async_computation | async-start | bytes 589824 | tf_op jit(solution)/shard_map/all_to_all | solution.py:169
  16.2 5.8 %copy-start.5 = (f32[24,49]{1,0:T(8,128)S(1)}, f32[24,49]{1,0:T(8,128)}, u32[]{:S(2)}) copy-start(f32[24,49]{1,0:T(8,128)} %param.9) | copy-start | bytes 14116
  16.2 15.6 %copy-start.3 = (bf16[1,4,16,1536]{3,2,1,0:T(8,128)(2,1)S(1)}, bf16[1,4,16,1536]{3,2,1,0:T(8,128)(2,1)}, u32[]{:S(2)}) copy-start(bf16[1,4,16,1536]{3,2,1,0:T(8,128)(2,1)} %param.6) | copy-start | bytes 589828
  16.5 15.3 %collective-permute-start.2 = (bf16[64,1536]{1,0:T(8,128)(2,1)S(1)}, bf16[64,1536]{1,0:T(8,128)(2,1)S(1)}, u32[]{:S(2)}, u32[]{:S(2)}) collective-permute-start(bf16[64,1536]{1,0:T(8,128)(2,1)S(1)} %get-tuple-element.11), channel_id=1, source_target_pairs={{0,1},{1,2},{2,3},{3,4},{4,5},{5,6},{6,7},{7,0},{8,9},{9,10},{10,1... | collective-permute-start | bytes 589832 | tf_op jit(solution)/shard_map/ppermute | solution.py:176
  17.9 13.9 %collective-permute-start.3 = (bf16[64,1536]{1,0:T(8,128)(2,1)S(1)}, bf16[64,1536]{1,0:T(8,128)(2,1)S(1)}, u32[]{:S(2)}, u32[]{:S(2)}) collective-permute-start(bf16[64,1536]{1,0:T(8,128)(2,1)S(1)} %get-tuple-element.12), channel_id=1, source_target_pairs={{0,7},{1,0},{2,1},{3,2},{4,3},{5,4},{6,5},{7,6},{8,15},{9,8},{10,9... | collective-permute-start | bytes 589832 | tf_op jit(solution)/shard_map/ppermute | solution.py:177
  28.1 16.1 %collective-permute-start.9 = (bf16[2,8,72,128]{3,2,1,0:T(8,128)(2,1)S(1)}, bf16[2,8,72,128]{3,2,1,0:T(8,128)(2,1)S(1)}, u32[]{:S(2)}, u32[]{:S(2)}) collective-permute-start(bf16[2,8,72,128]{3,2,1,0:T(8,128)(2,1)S(1)} %bitcast.15), channel_id=1, source_target_pairs={{0,2},{1,3},{2,0},{3,1},{4,6},{5,7},{6,4},{7,5},{8,10},{9,11},{10,... | collective-permute-start | bytes 884744 | tf_op jit(solution)/shard_map/ppermute | solution.py:180
  31.0 13.8 %collective-permute-start.8 = (bf16[2,8,72,128]{3,2,1,0:T(8,128)(2,1)S(1)}, bf16[2,8,72,128]{3,2,1,0:T(8,128)(2,1)S(1)}, u32[]{:S(2)}, u32[]{:S(2)}) collective-permute-start(bf16[2,8,72,128]{3,2,1,0:T(8,128)(2,1)S(1)} %bitcast.16), channel_id=1, source_target_pairs={{0,3},{1,2},{2,1},{3,0},{4,7},{5,6},{6,5},{7,4},{8,11},{9,10},{10,... | collective-permute-start | bytes 884744 | tf_op jit(solution)/shard_map/ppermute | solution.py:180
  31.8 13.1 %collective-permute-start.7 = (bf16[2,8,72,128]{3,2,1,0:T(8,128)(2,1)S(1)}, bf16[2,8,72,128]{3,2,1,0:T(8,128)(2,1)S(1)}, u32[]{:S(2)}, u32[]{:S(2)}) collective-permute-start(bf16[2,8,72,128]{3,2,1,0:T(8,128)(2,1)S(1)} %bitcast.17), channel_id=1, source_target_pairs={{0,1},{1,0},{2,3},{3,2},{4,5},{5,4},{6,7},{7,6},{8,9},{9,8},{10,11... | collective-permute-start | bytes 884744 | tf_op jit(solution)/shard_map/ppermute | solution.py:180
  36.9 4.9 %collective-permute-start.4 = (bf16[64,1536]{1,0:T(8,128)(2,1)S(1)}, bf16[64,1536]{1,0:T(8,128)(2,1)S(1)}, u32[]{:S(2)}, u32[]{:S(2)}) collective-permute-start(bf16[64,1536]{1,0:T(8,128)(2,1)S(1)} %shard_map.65.a_ref), channel_id=1, source_target_pairs={{0,16},{16,0},{1,17},{17,1},{2,18},{18,2},{3,19},{19,3},{4,20},{20... | collective-permute-start | bytes 589832 | tf_op jit(solution)/shard_map/ppermute | solution.py:188
  37.9 7.2 %collective-permute-start.5 = (bf16[64,1536]{1,0:T(8,128)(2,1)S(1)}, bf16[64,1536]{1,0:T(8,128)(2,1)S(1)}, u32[]{:S(2)}, u32[]{:S(2)}) collective-permute-start(bf16[64,1536]{1,0:T(8,128)(2,1)S(1)} %shard_map.65.a_ref), channel_id=1, source_target_pairs={{0,8},{8,0},{1,9},{9,1},{2,10},{10,2},{3,11},{11,3},{4,12},{12,4},... | collective-permute-start | bytes 589832 | tf_op jit(solution)/shard_map/ppermute | solution.py:189
  41.8 3.6 %collective-permute-start.6 = (bf16[64,1536]{1,0:T(8,128)(2,1)S(1)}, bf16[64,1536]{1,0:T(8,128)(2,1)S(1)}, u32[]{:S(2)}, u32[]{:S(2)}) collective-permute-start(bf16[64,1536]{1,0:T(8,128)(2,1)S(1)} %collective-permute-done.4.b_ref), channel_id=1, source_target_pairs={{0,8},{8,0},{1,9},{9,1},{2,10},{10,2},{3,11},{11,3},{4,12},{12,4},... | collective-permute-start | bytes 589832 | tf_op jit(solution)/shard_map/ppermute | solution.py:190
  46.2 2.6 %collective-permute-start.10 = (bf16[64,384]{1,0:T(8,128)(2,1)S(1)}, bf16[64,384]{1,0:T(8,128)(2,1)S(1)}, u32[]{:S(2)}, u32[]{:S(2)}) collective-permute-start(bf16[64,384]{1,0:T(8,128)(2,1)S(1)} %get-tuple-element.14), channel_id=1, source_target_pairs={{0,8},{8,0},{1,9},{9,1},{2,10},{10,2},{3,11},{11,3},{4,12},{12,4},... | collective-permute-start | bytes 147464 | tf_op jit(solution)/shard_map/ppermute | solution.py:199
  47.0 3.0 %collective-permute-start.11 = (bf16[64,384]{1,0:T(8,128)(2,1)S(1)}, bf16[64,384]{1,0:T(8,128)(2,1)S(1)}, u32[]{:S(2)}, u32[]{:S(2)}) collective-permute-start(bf16[64,384]{1,0:T(8,128)(2,1)S(1)} %get-tuple-element.15), channel_id=1, source_target_pairs={{0,16},{16,0},{1,17},{17,1},{2,18},{18,2},{3,19},{19,3},{4,20},{20... | collective-permute-start | bytes 147464 | tf_op jit(solution)/shard_map/ppermute | solution.py:198
  47.9 3.7 %collective-permute-start.12 = (bf16[64,384]{1,0:T(8,128)(2,1)S(1)}, bf16[64,384]{1,0:T(8,128)(2,1)S(1)}, u32[]{:S(2)}, u32[]{:S(2)}) collective-permute-start(bf16[64,384]{1,0:T(8,128)(2,1)S(1)} %get-tuple-element.16), channel_id=1, source_target_pairs={{0,24},{8,16},{16,8},{24,0},{1,25},{9,17},{17,9},{25,1},{2,26},{10... | collective-permute-start | bytes 147464 | tf_op jit(solution)/shard_map/ppermute | solution.py:197

commit v5 on v4

--- a/solution.py
+++ b/solution.py
@@ -1,6 +1,5 @@
 import jax
 import jax.numpy as jnp
-import numpy as np
 from jax import lax
 from jax.experimental import pallas as pl
 from jax.experimental.pallas import tpu as pltpu
@@ -13,22 +12,6 @@
 NT = (((1,), (1,)), ((), ()))
 
 
-def col_pick():
-    pick = np.zeros((64, 160), np.float32)
-    for side, first in ((0, 0), (1, 13)):
-        for r in range(10):
-            for j in range(3):
-                x = first + j
-                if r < 3:
-                    source = 64 + r * 16 + x
-                elif r < 7:
-                    source = (r - 3) * 16 + x
-                else:
-                    source = 112 + (r - 7) * 16 + x
-                pick[side * 32 + r * 3 + j, source] = 1.0
-    return pick
-
-
 def weight_kernel(wt_ref, out_ref):
     w = wt_ref[...]
     packed = jnp.concatenate([w[:, :128], jnp.concatenate([w[:24, 128:], w[24:, 128:]], 1)], 0)
@@ -36,11 +19,17 @@
         out_ref[n] = packed
 
 
-def pack_kernel(pick_ref, k_ref, v_ref, top_ref, bot_ref, left_ref, right_ref):
-    pick = pick_ref[...]
-    for n, own in ((0, k_ref), (1, v_ref)):
+def pack_kernel(up_ref, down_ref, top_ref, bot_ref, left_ref, right_ref):
+    i = lax.broadcasted_iota(jnp.int32, (64, 160), 0)
+    source = lax.broadcasted_iota(jnp.int32, (64, 160), 1)
+    t = i & 31
+    r = (t * 171) >> 9
+    x = t - r * 3 + (i >> 5) * 13
+    start = jnp.where(r < 3, r * 16 + 64, jnp.where(r < 7, r * 16 - 48, r * 16))
+    pick = jnp.where((source == start + x) & (t < 30), 1.0, 0.0).astype(BF)
+    for n in range(2):
         tokens = jnp.concatenate(
-            [own[...], top_ref[n * 48 : n * 48 + 48, :], bot_ref[n * 48 : n * 48 + 48, :]], 0
+            [up_ref[n], down_ref[n, 32:, :], top_ref[n * 48 : n * 48 + 48, :], bot_ref[n * 48 : n * 48 + 48, :]], 0
         )
         got = jnp.dot(pick, tokens, preferred_element_type=F32).astype(BF)
         left_ref[n * 32 : n * 32 + 32, :] = got[:32]
@@ -169,10 +158,11 @@
     along_zx = lax.all_to_all(packed, ("xh", "z"), 0, 0, tiled=True)
 
     both = jnp.stack([k, v], 0)
-    top = lax.ppermute(both[:, 16:], rows, down).reshape(96, width)
-    bot = lax.ppermute(both[:, :48], rows, up).reshape(96, width)
+    to_down, to_up = both[:, 16:], both[:, :48]
+    top = lax.ppermute(to_down, rows, down).reshape(96, width)
+    bot = lax.ppermute(to_up, rows, up).reshape(96, width)
     side = jax.ShapeDtypeStruct((64, width), BF)
-    to_left, to_right = call(pack_kernel, (side, side), 5, flops=50000000000)(jnp.asarray(col_pick(), BF), k, v, top, bot)
+    to_left, to_right = call(pack_kernel, (side, side), 4, flops=50000000000)(to_up, to_down, top, bot)
     from_left = lax.ppermute(to_right, cols, right)
     from_right = lax.ppermute(to_left, cols, left)
 

time: 53.3 us -> 53.3 us (level)
  no operation moved by 1% of the time
where the time goes in v5:
time: 53.3 us; the launch traced here: 53 us
  starting transfers between devices  29.3 us (55%)
  waiting for transfers between devices  12.8 us (24%)
  Pallas kernels  8.64 us (16%)
  other arithmetic  1.31 us (2%)
  local copies, waits for them, and re-layouts  0.77 us (1%)
    all_to_all x1, starting transfers between devices, shards(): along_zx = lax.all_to_all(packed, ('xh', 'z'), 0, 0, tiled=True)  10.1 us
    all_to_all x1, waiting for transfers between devices, shards(): along_zx = lax.all_to_all(packed, ('xh', 'z'), 0, 0, tiled=True)  6.01 us
    pallas_call x1, Pallas kernels, shards(): call(attention_kernel, side, 9, smem=(0,), flops=50000000000)  5.02 us
    ppermute x1, starting transfers between devices, shards(): from_right = lax.ppermute(to_left, cols, left)  4.11 us
    ppermute x3, starting transfers between devices, shards(): lax.ppermute(near, 'y', [(n, n ^ k) for n in range(4)])  3.69 us
    ppermute x1, starting transfers between devices, shards(): bot = lax.ppermute(to_up, rows, up).reshape(96, width)  3.32 us
    ppermute x1, waiting for transfers between devices, shards(): next_mixed = lax.ppermute(mixed, 'xl', swap)  3.1 us
    ppermute x1, starting transfers between devices, shards(): both_mixed = lax.ppermute(next_mixed, 'core', swap)  2.5 us
  transfers between devices with their start and end apart: 14, of which 6 were waited for; matrix products, arithmetic and copies ran while one was open for 0% of the time, Pallas kernels for 12%

profile of v5, /device:TPU:1, one launch (start us, length us, event | category | flops | bytes accessed | tf_op | source)
XLA Modules:
  0.0 53.0 jit_solution(2685274680925057242)
XLA Ops:
  0.0 1.2 %pad_maximum_fusion = (bf16[2,48,1536]{2,1,0:T(8,128)(2,1)S(1)}, bf16[2,48,1536]{2,1,0:T(8,128)(2,1)S(1)}) fusion(bf16[1,64,1536]{2,1,0:T(8,128)(2,1)} %bitcast.21, bf16[1,64,1536]{2,1,0:T(8,128)(2,1)} %bitcast.19), kind=kLoop, calls=%fused_computation.3 | loop fusion | flops 1179648 | bytes 983040 | tf_op jit(solution)/shard_map/stack | solution.py:160
  1.2 3.3 %collective-permute-start.1 = (bf16[2,48,1536]{2,1,0:T(8,128)(2,1)S(1)}, bf16[2,48,1536]{2,1,0:T(8,128)(2,1)S(1)}, u32[]{:S(2)}, u32[]{:S(2)}) collective-permute-start(bf16[2,48,1536]{2,1,0:T(8,128)(2,1)S(1)} %get-tuple-element.17.up_ref), channel_id=1, source_target_pairs={{0,248},{8,0},{16,8},{24,16},{32,24},{40,32},{48,40},{56,48},{64,5... | collective-permute-start | bytes 884744 | tf_op jit(solution)/shard_map/ppermute | solution.py:163
  4.5 0.0 collective-permute-start
  4.5 0.0 copy-start.2
  4.5 0.7 %copy-done.2 = bf16[192,48]{0,1:T(8,128)(2,1)S(1)} copy-done((bf16[192,48]{0,1:T(8,128)(2,1)S(1)}, bf16[192,48]{0,1:T(8,128)(2,1)}, u32[]{:S(2)}) %copy-start.2) | copy-done | bytes 18456
  5.2 0.8 %shard_map.57 = bf16[16,72,128]{2,1,0:T(8,128)(2,1)} custom-call(bf16[48,192]{1,0:T(8,128)(2,1)S(1)} %bitcast.23), custom_call_target="tpu_custom_call" | custom-call | tf_op jit(solution)/shard_map/pallas_call | solution.py:157
  6.0 10.1 %all-to-all-start = ((bf16[16,72,128]{2,1,0:T(8,128)(2,1)}), bf16[16,72,128]{2,1,0:T(8,128)(2,1)S(1)}, u32[]{:S(2)}, u32[]{:S(2)}) async-start(bf16[16,72,128]{2,1,0:T(8,128)(2,1)} %shard_map.57), calls=%async_computation | async-start | bytes 589824 | tf_op jit(solution)/shard_map/all_to_all | solution.py:158
  16.1 0.0 collective-permute-done.1
  16.1 0.0 collective-permute-done
  16.1 0.0 copy-start.4
  16.2 0.0 copy-start
  16.2 0.0 copy-start.1
  16.2 0.0 copy-start.3
  16.2 0.3 shard_map.55
  16.5 1.4 %collective-permute-start.2 = (bf16[64,1536]{1,0:T(8,128)(2,1)S(1)}, bf16[64,1536]{1,0:T(8,128)(2,1)S(1)}, u32[]{:S(2)}, u32[]{:S(2)}) collective-permute-start(bf16[64,1536]{1,0:T(8,128)(2,1)S(1)} %get-tuple-element.11), channel_id=1, source_target_pairs={{0,1},{1,2},{2,3},{3,4},{4,5},{5,6},{6,7},{7,0},{8,9},{9,10},{10,1... | collective-permute-start | bytes 589832 | tf_op jit(solution)/shard_map/ppermute | solution.py:166
  17.9 4.1 %collective-permute-start.3 = (bf16[64,1536]{1,0:T(8,128)(2,1)S(1)}, bf16[64,1536]{1,0:T(8,128)(2,1)S(1)}, u32[]{:S(2)}, u32[]{:S(2)}) collective-permute-start(bf16[64,1536]{1,0:T(8,128)(2,1)S(1)} %get-tuple-element.12), channel_id=1, source_target_pairs={{0,7},{1,0},{2,1},{3,2},{4,3},{5,4},{6,5},{7,6},{8,15},{9,8},{10,9... | collective-permute-start | bytes 589832 | tf_op jit(solution)/shard_map/ppermute | solution.py:167
  22.0 0.0 copy-done.4
  22.0 0.1 pad_add_fusion.1.place_ref
  22.1 6.0 %all-to-all-done = bf16[16,72,128]{2,1,0:T(8,128)(2,1)S(1)} async-done(((bf16[16,72,128]{2,1,0:T(8,128)(2,1)}), bf16[16,72,128]{2,1,0:T(8,128)(2,1)S(1)}, u32[]{:S(2)}, u32[]{:S(2)}) %all-to-all-start) | async-done | bytes 294944 | tf_op jit(solution)/shard_map/all_to_all | solution.py:158
  28.1 2.9 %collective-permute-start.9 = (bf16[2,8,72,128]{3,2,1,0:T(8,128)(2,1)S(1)}, bf16[2,8,72,128]{3,2,1,0:T(8,128)(2,1)S(1)}, u32[]{:S(2)}, u32[]{:S(2)}) collective-permute-start(bf16[2,8,72,128]{3,2,1,0:T(8,128)(2,1)S(1)} %bitcast.15), channel_id=1, source_target_pairs={{0,2},{1,3},{2,0},{3,1},{4,6},{5,7},{6,4},{7,5},{8,10},{9,11},{10,... | collective-permute-start | bytes 884744 | tf_op jit(solution)/shard_map/ppermute | solution.py:170
  31.0 0.8 %collective-permute-start.8 = (bf16[2,8,72,128]{3,2,1,0:T(8,128)(2,1)S(1)}, bf16[2,8,72,128]{3,2,1,0:T(8,128)(2,1)S(1)}, u32[]{:S(2)}, u32[]{:S(2)}) collective-permute-start(bf16[2,8,72,128]{3,2,1,0:T(8,128)(2,1)S(1)} %bitcast.16), channel_id=1, source_target_pairs={{0,3},{1,2},{2,1},{3,0},{4,7},{5,6},{6,5},{7,4},{8,11},{9,10},{10,... | collective-permute-start | bytes 884744 | tf_op jit(solution)/shard_map/ppermute | solution.py:170
  31.8 0.0 collective-permute-start.7
  31.8 0.0 collective-permute-done.2.left_ref
  31.8 0.0 collective-permute-done.3.right_ref
  31.8 0.0 copy-done
  31.8 0.0 copy-done.1
  31.8 0.0 copy-done.3
  31.8 5.0 %shard_map.56.a_ref = bf16[64,1536]{1,0:T(8,128)(2,1)S(1)} custom-call(s32[4]{0:T(128)S(1)} %pad_add_fusion.1.place_ref, bf16[64,1536]{1,0:T(8,128)(2,1)S(1)} %bitcast.28, bf16[64,1536]{1,0:T(8,128)(2,1)S(1)} %bitcast.20, bf16[64,1536]{1,0:T(8,128)(2,1)S(1)} %bitcast.22, bf16[96,1536]{1,0:T(8,128)(2,1)S(1)} %bitcast.27, bf16[96,1536]{1,0:T(8,128)(2,1)S(1)} %bitcast.25, ...), custom_call_target="tpu_custom_call" | custom-call | flops 49999998976 | bytes 4194304 | tf_op jit(solution)/shard_map/pallas_call | solution.py:174
  36.8 1.0 %collective-permute-start.4 = (bf16[64,1536]{1,0:T(8,128)(2,1)S(1)}, bf16[64,1536]{1,0:T(8,128)(2,1)S(1)}, u32[]{:S(2)}, u32[]{:S(2)}) collective-permute-start(bf16[64,1536]{1,0:T(8,128)(2,1)S(1)} %shard_map.56.a_ref), channel_id=1, source_target_pairs={{0,16},{16,0},{1,17},{17,1},{2,18},{18,2},{3,19},{19,3},{4,20},{20... | collective-permute-start | bytes 589832 | tf_op jit(solution)/shard_map/ppermute | solution.py:178
  37.8 0.8 %collective-permute-start.5 = (bf16[64,1536]{1,0:T(8,128)(2,1)S(1)}, bf16[64,1536]{1,0:T(8,128)(2,1)S(1)}, u32[]{:S(2)}, u32[]{:S(2)}) collective-permute-start(bf16[64,1536]{1,0:T(8,128)(2,1)S(1)} %shard_map.56.a_ref), channel_id=1, source_target_pairs={{0,8},{8,0},{1,9},{9,1},{2,10},{10,2},{3,11},{11,3},{4,12},{12,4},... | collective-permute-start | bytes 589832 | tf_op jit(solution)/shard_map/ppermute | solution.py:179
  38.6 3.1 %collective-permute-done.4.b_ref = bf16[64,1536]{1,0:T(8,128)(2,1)S(1)} collective-permute-done((bf16[64,1536]{1,0:T(8,128)(2,1)S(1)}, bf16[64,1536]{1,0:T(8,128)(2,1)S(1)}, u32[]{:S(2)}, u32[]{:S(2)}) %collective-permute-start.4) | collective-permute-done | bytes 196640 | tf_op jit(solution)/shard_map/ppermute | solution.py:178
  41.7 2.5 %collective-permute-start.6 = (bf16[64,1536]{1,0:T(8,128)(2,1)S(1)}, bf16[64,1536]{1,0:T(8,128)(2,1)S(1)}, u32[]{:S(2)}, u32[]{:S(2)}) collective-permute-start(bf16[64,1536]{1,0:T(8,128)(2,1)S(1)} %collective-permute-done.4.b_ref), channel_id=1, source_target_pairs={{0,8},{8,0},{1,9},{9,1},{2,10},{10,2},{3,11},{11,3},{4,12},{12,4},... | collective-permute-start | bytes 589832 | tf_op jit(solution)/shard_map/ppermute | solution.py:180
  44.2 0.0 collective-permute-done.9.w2_ref
  44.2 0.6 %collective-permute-done.8.w3_ref = bf16[2,8,72,128]{3,2,1,0:T(8,128)(2,1)S(1)} collective-permute-done((bf16[2,8,72,128]{3,2,1,0:T(8,128)(2,1)S(1)}, bf16[2,8,72,128]{3,2,1,0:T(8,128)(2,1)S(1)}, u32[]{:S(2)}, u32[]{:S(2)}) %collective-permute-start.8) | collective-permute-done | bytes 294944 | tf_op jit(solution)/shard_map/ppermute | solution.py:170
  44.8 0.0 collective-permute-done.7.w1_ref
  44.8 0.2 shard_map.58.w_ref
  45.0 0.0 collective-permute-done.5.c_ref
  45.1 0.2 collective-permute-done.6.d_ref
  45.3 0.9 %shard_map.59 = (bf16[64,384]{1,0:T(8,128)(2,1)S(1)}, bf16[64,384]{1,0:T(8,128)(2,1)S(1)}, bf16[64,384]{1,0:T(8,128)(2,1)S(1)}, bf16[64,384]{1,0:T(8,128)(2,1)S(1)}) custom-call(s32[1]{0:T(128)} %bitcast.2.y_ref, bf16[64,1536]{1,0:T(8,128)(2,1)S(1)} %shard_map.56.a_ref, bf16[64,1536]{1,0:T(8,128)(2,1)S(1)} %collective-permute-done.4.b_ref, ...), custom_call_target="tpu_custom_call" | custom-call | tf_op jit(solution)/shard_map/pallas_call | solution.py:184
  46.2 0.7 %collective-permute-start.10 = (bf16[64,384]{1,0:T(8,128)(2,1)S(1)}, bf16[64,384]{1,0:T(8,128)(2,1)S(1)}, u32[]{:S(2)}, u32[]{:S(2)}) collective-permute-start(bf16[64,384]{1,0:T(8,128)(2,1)S(1)} %get-tuple-element.14), channel_id=1, source_target_pairs={{0,8},{8,0},{1,9},{9,1},{2,10},{10,2},{3,11},{11,3},{4,12},{12,4},... | collective-permute-start | bytes 147464 | tf_op jit(solution)/shard_map/ppermute | solution.py:189
  46.9 0.9 %collective-permute-start.11 = (bf16[64,384]{1,0:T(8,128)(2,1)S(1)}, bf16[64,384]{1,0:T(8,128)(2,1)S(1)}, u32[]{:S(2)}, u32[]{:S(2)}) collective-permute-start(bf16[64,384]{1,0:T(8,128)(2,1)S(1)} %get-tuple-element.15), channel_id=1, source_target_pairs={{0,16},{16,0},{1,17},{17,1},{2,18},{18,2},{3,19},{19,3},{4,20},{20... | collective-permute-start | bytes 147464 | tf_op jit(solution)/shard_map/ppermute | solution.py:188
  47.8 0.8 %collective-permute-start.12 = (bf16[64,384]{1,0:T(8,128)(2,1)S(1)}, bf16[64,384]{1,0:T(8,128)(2,1)S(1)}, u32[]{:S(2)}, u32[]{:S(2)}) collective-permute-start(bf16[64,384]{1,0:T(8,128)(2,1)S(1)} %get-tuple-element.16), channel_id=1, source_target_pairs={{0,24},{8,16},{16,8},{24,0},{1,25},{9,17},{17,9},{25,1},{2,26},{10... | collective-permute-start | bytes 147464 | tf_op jit(solution)/shard_map/ppermute | solution.py:187
  48.6 0.1 pad_add_fusion.at_ref
  48.7 0.0 collective-permute-done.10.core_ref
  48.7 1.1 %collective-permute-done.11.chip_ref = bf16[64,384]{1,0:T(8,128)(2,1)S(1)} collective-permute-done((bf16[64,384]{1,0:T(8,128)(2,1)S(1)}, bf16[64,384]{1,0:T(8,128)(2,1)S(1)}, u32[]{:S(2)}, u32[]{:S(2)}) %collective-permute-start.11) | collective-permute-done | bytes 49184 | tf_op jit(solution)/shard_map/ppermute | solution.py:188
  49.9 1.7 %collective-permute-done.12.both_ref = bf16[64,384]{1,0:T(8,128)(2,1)S(1)} collective-permute-done((bf16[64,384]{1,0:T(8,128)(2,1)S(1)}, bf16[64,384]{1,0:T(8,128)(2,1)S(1)}, u32[]{:S(2)}, u32[]{:S(2)}) %collective-permute-start.12) | collective-permute-done | bytes 49184 | tf_op jit(solution)/shard_map/ppermute | solution.py:187
  51.6 1.5 %shard_map.60 = bf16[64,1536]{1,0:T(8,128)(2,1)} custom-call(s32[2]{0:T(128)S(1)} %pad_add_fusion.at_ref, bf16[64,384]{1,0:T(8,128)(2,1)S(1)} %get-tuple-element.13.keep_ref, bf16[64,384]{1,0:T(8,128)(2,1)S(1)} %collective-permute-done.10.core_ref, bf16[64,384]{1,0:T(8,128)(2,1)S(1)} %collective-permute-done.11.chip_ref, ...), custom_call_target="tpu_custom_call" | custom-call | tf_op jit(solution)/shard_map/pallas_call | solution.py:191
  (2 shorter events, 0.0 us)
Async XLA Ops:
  1.2 15.0 %collective-permute-start.1 = (bf16[2,48,1536]{2,1,0:T(8,128)(2,1)S(1)}, bf16[2,48,1536]{2,1,0:T(8,128)(2,1)S(1)}, u32[]{:S(2)}, u32[]{:S(2)}) collective-permute-start(bf16[2,48,1536]{2,1,0:T(8,128)(2,1)S(1)} %get-tuple-element.17.up_ref), channel_id=1, source_target_pairs={{0,248},{8,0},{16,8},{24,16},{32,24},{40,32},{48,40},{56,48},{64,5... | collective-permute-start | bytes 884744 | tf_op jit(solution)/shard_map/ppermute | solution.py:163
  4.5 11.6 %collective-permute-start = (bf16[2,48,1536]{2,1,0:T(8,128)(2,1)S(1)}, bf16[2,48,1536]{2,1,0:T(8,128)(2,1)S(1)}, u32[]{:S(2)}, u32[]{:S(2)}) collective-permute-start(bf16[2,48,1536]{2,1,0:T(8,128)(2,1)S(1)} %get-tuple-element.18.down_ref), channel_id=1, source_target_pairs={{0,8},{8,16},{16,24},{24,32},{32,40},{40,48},{48,56},{56,64},{64,7... | collective-permute-start | bytes 884744 | tf_op jit(solution)/shard_map/ppermute | solution.py:162
  4.5 0.7 %copy-start.2 = (bf16[192,48]{0,1:T(8,128)(2,1)S(1)}, bf16[192,48]{0,1:T(8,128)(2,1)}, u32[]{:S(2)}) copy-start(bf16[192,48]{0,1:T(8,128)(2,1)} %param.9) | copy-start | bytes 55300
  6.0 22.0 %all-to-all-start = ((bf16[16,72,128]{2,1,0:T(8,128)(2,1)}), bf16[16,72,128]{2,1,0:T(8,128)(2,1)S(1)}, u32[]{:S(2)}, u32[]{:S(2)}) async-start(bf16[16,72,128]{2,1,0:T(8,128)(2,1)} %shard_map.57), calls=%async_computation | async-start | bytes 589824 | tf_op jit(solution)/shard_map/all_to_all | solution.py:158
  16.1 5.8 %copy-start.4 = (f32[24,49]{1,0:T(8,128)S(1)}, f32[24,49]{1,0:T(8,128)}, u32[]{:S(2)}) copy-start(f32[24,49]{1,0:T(8,128)} %param.8) | copy-start | bytes 14116
  16.2 15.6 %copy-start = (bf16[1,4,16,1536]{3,2,1,0:T(8,128)(2,1)S(1)}, bf16[1,4,16,1536]{3,2,1,0:T(8,128)(2,1)}, u32[]{:S(2)}) copy-start(bf16[1,4,16,1536]{3,2,1,0:T(8,128)(2,1)} %param.6) | copy-start | bytes 589828
  16.2 15.6 %copy-start.1 = (bf16[1,4,16,1536]{3,2,1,0:T(8,128)(2,1)S(1)}, bf16[1,4,16,1536]{3,2,1,0:T(8,128)(2,1)}, u32[]{:S(2)}) copy-start(bf16[1,4,16,1536]{3,2,1,0:T(8,128)(2,1)} %param.7) | copy-start | bytes 589828
  16.2 15.6 %copy-start.3 = (bf16[1,4,16,1536]{3,2,1,0:T(8,128)(2,1)S(1)}, bf16[1,4,16,1536]{3,2,1,0:T(8,128)(2,1)}, u32[]{:S(2)}) copy-start(bf16[1,4,16,1536]{3,2,1,0:T(8,128)(2,1)} %param.5) | copy-start | bytes 589828
  16.5 15.3 %collective-permute-start.2 = (bf16[64,1536]{1,0:T(8,128)(2,1)S(1)}, bf16[64,1536]{1,0:T(8,128)(2,1)S(1)}, u32[]{:S(2)}, u32[]{:S(2)}) collective-permute-start(bf16[64,1536]{1,0:T(8,128)(2,1)S(1)} %get-tuple-element.11), channel_id=1, source_target_pairs={{0,1},{1,2},{2,3},{3,4},{4,5},{5,6},{6,7},{7,0},{8,9},{9,10},{10,1... | collective-permute-start | bytes 589832 | tf_op jit(solution)/shard_map/ppermute | solution.py:166
  17.9 13.9 %collective-permute-start.3 = (bf16[64,1536]{1,0:T(8,128)(2,1)S(1)}, bf16[64,1536]{1,0:T(8,128)(2,1)S(1)}, u32[]{:S(2)}, u32[]{:S(2)}) collective-permute-start(bf16[64,1536]{1,0:T(8,128)(2,1)S(1)} %get-tuple-element.12), channel_id=1, source_target_pairs={{0,7},{1,0},{2,1},{3,2},{4,3},{5,4},{6,5},{7,6},{8,15},{9,8},{10,9... | collective-permute-start | bytes 589832 | tf_op jit(solution)/shard_map/ppermute | solution.py:167
  28.1 16.2 %collective-permute-start.9 = (bf16[2,8,72,128]{3,2,1,0:T(8,128)(2,1)S(1)}, bf16[2,8,72,128]{3,2,1,0:T(8,128)(2,1)S(1)}, u32[]{:S(2)}, u32[]{:S(2)}) collective-permute-start(bf16[2,8,72,128]{3,2,1,0:T(8,128)(2,1)S(1)} %bitcast.15), channel_id=1, source_target_pairs={{0,2},{1,3},{2,0},{3,1},{4,6},{5,7},{6,4},{7,5},{8,10},{9,11},{10,... | collective-permute-start | bytes 884744 | tf_op jit(solution)/shard_map/ppermute | solution.py:170
  31.0 13.8 %collective-permute-start.8 = (bf16[2,8,72,128]{3,2,1,0:T(8,128)(2,1)S(1)}, bf16[2,8,72,128]{3,2,1,0:T(8,128)(2,1)S(1)}, u32[]{:S(2)}, u32[]{:S(2)}) collective-permute-start(bf16[2,8,72,128]{3,2,1,0:T(8,128)(2,1)S(1)} %bitcast.16), channel_id=1, source_target_pairs={{0,3},{1,2},{2,1},{3,0},{4,7},{5,6},{6,5},{7,4},{8,11},{9,10},{10,... | collective-permute-start | bytes 884744 | tf_op jit(solution)/shard_map/ppermute | solution.py:170
  31.8 13.1 %collective-permute-start.7 = (bf16[2,8,72,128]{3,2,1,0:T(8,128)(2,1)S(1)}, bf16[2,8,72,128]{3,2,1,0:T(8,128)(2,1)S(1)}, u32[]{:S(2)}, u32[]{:S(2)}) collective-permute-start(bf16[2,8,72,128]{3,2,1,0:T(8,128)(2,1)S(1)} %bitcast.17), channel_id=1, source_target_pairs={{0,1},{1,0},{2,3},{3,2},{4,5},{5,4},{6,7},{7,6},{8,9},{9,8},{10,11... | collective-permute-start | bytes 884744 | tf_op jit(solution)/shard_map/ppermute | solution.py:170
  36.8 4.9 %collective-permute-start.4 = (bf16[64,1536]{1,0:T(8,128)(2,1)S(1)}, bf16[64,1536]{1,0:T(8,128)(2,1)S(1)}, u32[]{:S(2)}, u32[]{:S(2)}) collective-permute-start(bf16[64,1536]{1,0:T(8,128)(2,1)S(1)} %shard_map.56.a_ref), channel_id=1, source_target_pairs={{0,16},{16,0},{1,17},{17,1},{2,18},{18,2},{3,19},{19,3},{4,20},{20... | collective-permute-start | bytes 589832 | tf_op jit(solution)/shard_map/ppermute | solution.py:178
  37.8 7.2 %collective-permute-start.5 = (bf16[64,1536]{1,0:T(8,128)(2,1)S(1)}, bf16[64,1536]{1,0:T(8,128)(2,1)S(1)}, u32[]{:S(2)}, u32[]{:S(2)}) collective-permute-start(bf16[64,1536]{1,0:T(8,128)(2,1)S(1)} %shard_map.56.a_ref), channel_id=1, source_target_pairs={{0,8},{8,0},{1,9},{9,1},{2,10},{10,2},{3,11},{11,3},{4,12},{12,4},... | collective-permute-start | bytes 589832 | tf_op jit(solution)/shard_map/ppermute | solution.py:179
  41.7 3.6 %collective-permute-start.6 = (bf16[64,1536]{1,0:T(8,128)(2,1)S(1)}, bf16[64,1536]{1,0:T(8,128)(2,1)S(1)}, u32[]{:S(2)}, u32[]{:S(2)}) collective-permute-start(bf16[64,1536]{1,0:T(8,128)(2,1)S(1)} %collective-permute-done.4.b_ref), channel_id=1, source_target_pairs={{0,8},{8,0},{1,9},{9,1},{2,10},{10,2},{3,11},{11,3},{4,12},{12,4},... | collective-permute-start | bytes 589832 | tf_op jit(solution)/shard_map/ppermute | solution.py:180
  46.2 2.5 %collective-permute-start.10 = (bf16[64,384]{1,0:T(8,128)(2,1)S(1)}, bf16[64,384]{1,0:T(8,128)(2,1)S(1)}, u32[]{:S(2)}, u32[]{:S(2)}) collective-permute-start(bf16[64,384]{1,0:T(8,128)(2,1)S(1)} %get-tuple-element.14), channel_id=1, source_target_pairs={{0,8},{8,0},{1,9},{9,1},{2,10},{10,2},{3,11},{11,3},{4,12},{12,4},... | collective-permute-start | bytes 147464 | tf_op jit(solution)/shard_map/ppermute | solution.py:189
  46.9 3.0 %collective-permute-start.11 = (bf16[64,384]{1,0:T(8,128)(2,1)S(1)}, bf16[64,384]{1,0:T(8,128)(2,1)S(1)}, u32[]{:S(2)}, u32[]{:S(2)}) collective-permute-start(bf16[64,384]{1,0:T(8,128)(2,1)S(1)} %get-tuple-element.15), channel_id=1, source_target_pairs={{0,16},{16,0},{1,17},{17,1},{2,18},{18,2},{3,19},{19,3},{4,20},{20... | collective-permute-start | bytes 147464 | tf_op jit(solution)/shard_map/ppermute | solution.py:188
  47.8 3.7 %collective-permute-start.12 = (bf16[64,384]{1,0:T(8,128)(2,1)S(1)}, bf16[64,384]{1,0:T(8,128)(2,1)S(1)}, u32[]{:S(2)}, u32[]{:S(2)}) collective-permute-start(bf16[64,384]{1,0:T(8,128)(2,1)S(1)} %get-tuple-element.16), channel_id=1, source_target_pairs={{0,24},{8,16},{16,8},{24,0},{1,25},{9,17},{17,9},{25,1},{2,26},{10... | collective-permute-start | bytes 147464 | tf_op jit(solution)/shard_map/ppermute | solution.py:187

commit v6 on v5

--- a/solution.py
+++ b/solution.py
@@ -154,7 +154,7 @@
     right = [(n, (n + 1) % nc) for n in range(nc)]
     left = [(n, (n - 1) % nc) for n in range(nc)]
     k, v, q = (a.reshape(64, width) for a in (key_tokens, values, queries))
-    packed = call(weight_kernel, jax.ShapeDtypeStruct((16, 72, 128), BF), 1)(out_weight.T)
+    packed = call(weight_kernel, jax.ShapeDtypeStruct((16, 72, 128), BF), 1, limit=4)(out_weight.T)
     along_zx = lax.all_to_all(packed, ("xh", "z"), 0, 0, tiled=True)
 
     both = jnp.stack([k, v], 0)
@@ -184,9 +184,9 @@
     keep, to_chip, to_core, to_both = call(project_kernel, (part,) * 4, 6, smem=(0,))(
         y, mixed, next_mixed, core_mixed, both_mixed, weights
     )
+    by_core = lax.ppermute(to_core, "core", swap)
+    by_chip = lax.ppermute(to_chip, "xl", swap)
     by_both = lax.ppermute(to_both, ("xl", "core"), [(n, 3 - n) for n in range(4)])
-    by_chip = lax.ppermute(to_chip, "xl", swap)
-    by_core = lax.ppermute(to_core, "core", swap)
     at = jnp.stack([lax.axis_index("xl"), lax.axis_index("core")]).astype(jnp.int32)
     out = call(assemble_kernel, side, 5, smem=(0,))(at, keep, by_core, by_chip, by_both)
     return out.reshape(queries.shape)

time: 53.3 us -> 53.3 us (level)
  no operation moved by 1% of the time
where the time goes in v6:
time: 53.3 us; the launch traced here: 53 us
  starting transfers between devices  29.3 us (55%)
  waiting for transfers between devices  12.8 us (24%)
  Pallas kernels  8.64 us (16%)
  other arithmetic  1.31 us (2%)
  local copies, waits for them, and re-layouts  0.77 us (1%)
    all_to_all x1, starting transfers between devices, shards(): along_zx = lax.all_to_all(packed, ('xh', 'z'), 0, 0, tiled=True)  10.1 us
    all_to_all x1, waiting for transfers between devices, shards(): along_zx = lax.all_to_all(packed, ('xh', 'z'), 0, 0, tiled=True)  6.01 us
    pallas_call x1, Pallas kernels, shards(): call(attention_kernel, side, 9, smem=(0,), flops=50000000000)  5.02 us
    ppermute x1, starting transfers between devices, shards(): from_right = lax.ppermute(to_left, cols, left)  4.11 us
    ppermute x3, starting transfers between devices, shards(): lax.ppermute(near, 'y', [(n, n ^ k) for n in range(4)])  3.69 us
    ppermute x1, starting transfers between devices, shards(): bot = lax.ppermute(to_up, rows, up).reshape(96, width)  3.32 us
    ppermute x1, waiting for transfers between devices, shards(): next_mixed = lax.ppermute(mixed, 'xl', swap)  3.1 us
    ppermute x1, starting transfers between devices, shards(): both_mixed = lax.ppermute(next_mixed, 'core', swap)  2.5 us
  transfers between devices with their start and end apart: 14, of which 6 were waited for; matrix products, arithmetic and copies ran while one was open for 0% of the time, Pallas kernels for 12%

profile of v6, /device:TPU:1, one launch (start us, length us, event | category | flops | bytes accessed | tf_op | source)
XLA Modules:
  0.0 53.0 jit_solution(843110807195404701)
XLA Ops:
  0.0 1.2 %pad_maximum_fusion = (bf16[2,48,1536]{2,1,0:T(8,128)(2,1)S(1)}, bf16[2,48,1536]{2,1,0:T(8,128)(2,1)S(1)}) fusion(bf16[1,64,1536]{2,1,0:T(8,128)(2,1)} %bitcast.21, bf16[1,64,1536]{2,1,0:T(8,128)(2,1)} %bitcast.19), kind=kLoop, calls=%fused_computation.3 | loop fusion | flops 1179648 | bytes 983040 | tf_op jit(solution)/shard_map/stack | solution.py:160
  1.2 3.3 %collective-permute-start.1 = (bf16[2,48,1536]{2,1,0:T(8,128)(2,1)S(1)}, bf16[2,48,1536]{2,1,0:T(8,128)(2,1)S(1)}, u32[]{:S(2)}, u32[]{:S(2)}) collective-permute-start(bf16[2,48,1536]{2,1,0:T(8,128)(2,1)S(1)} %get-tuple-element.17.up_ref), channel_id=1, source_target_pairs={{0,248},{8,0},{16,8},{24,16},{32,24},{40,32},{48,40},{56,48},{64,5... | collective-permute-start | bytes 884744 | tf_op jit(solution)/shard_map/ppermute | solution.py:163
  4.5 0.0 collective-permute-start
  4.5 0.0 copy-start.2
  4.5 0.7 %copy-done.2 = bf16[192,48]{0,1:T(8,128)(2,1)S(1)} copy-done((bf16[192,48]{0,1:T(8,128)(2,1)S(1)}, bf16[192,48]{0,1:T(8,128)(2,1)}, u32[]{:S(2)}) %copy-start.2) | copy-done | bytes 18456
  5.2 0.8 %shard_map.57 = bf16[16,72,128]{2,1,0:T(8,128)(2,1)} custom-call(bf16[48,192]{1,0:T(8,128)(2,1)S(1)} %bitcast.23), custom_call_target="tpu_custom_call" | custom-call | tf_op jit(solution)/shard_map/pallas_call | solution.py:157
  6.0 10.1 %all-to-all-start = ((bf16[16,72,128]{2,1,0:T(8,128)(2,1)}), bf16[16,72,128]{2,1,0:T(8,128)(2,1)S(1)}, u32[]{:S(2)}, u32[]{:S(2)}) async-start(bf16[16,72,128]{2,1,0:T(8,128)(2,1)} %shard_map.57), calls=%async_computation | async-start | bytes 589824 | tf_op jit(solution)/shard_map/all_to_all | solution.py:158
  16.1 0.0 collective-permute-done.1
  16.1 0.0 collective-permute-done
  16.1 0.0 copy-start.4
  16.2 0.0 copy-start
  16.2 0.0 copy-start.1
  16.2 0.0 copy-start.3
  16.2 0.3 shard_map.55
  16.5 1.4 %collective-permute-start.2 = (bf16[64,1536]{1,0:T(8,128)(2,1)S(1)}, bf16[64,1536]{1,0:T(8,128)(2,1)S(1)}, u32[]{:S(2)}, u32[]{:S(2)}) collective-permute-start(bf16[64,1536]{1,0:T(8,128)(2,1)S(1)} %get-tuple-element.11), channel_id=1, source_target_pairs={{0,1},{1,2},{2,3},{3,4},{4,5},{5,6},{6,7},{7,0},{8,9},{9,10},{10,1... | collective-permute-start | bytes 589832 | tf_op jit(solution)/shard_map/ppermute | solution.py:166
  17.9 4.1 %collective-permute-start.3 = (bf16[64,1536]{1,0:T(8,128)(2,1)S(1)}, bf16[64,1536]{1,0:T(8,128)(2,1)S(1)}, u32[]{:S(2)}, u32[]{:S(2)}) collective-permute-start(bf16[64,1536]{1,0:T(8,128)(2,1)S(1)} %get-tuple-element.12), channel_id=1, source_target_pairs={{0,7},{1,0},{2,1},{3,2},{4,3},{5,4},{6,5},{7,6},{8,15},{9,8},{10,9... | collective-permute-start | bytes 589832 | tf_op jit(solution)/shard_map/ppermute | solution.py:167
  22.0 0.0 copy-done.4
  22.0 0.1 pad_add_fusion.1.place_ref
  22.1 6.0 %all-to-all-done = bf16[16,72,128]{2,1,0:T(8,128)(2,1)S(1)} async-done(((bf16[16,72,128]{2,1,0:T(8,128)(2,1)}), bf16[16,72,128]{2,1,0:T(8,128)(2,1)S(1)}, u32[]{:S(2)}, u32[]{:S(2)}) %all-to-all-start) | async-done | bytes 294944 | tf_op jit(solution)/shard_map/all_to_all | solution.py:158
  28.1 2.9 %collective-permute-start.9 = (bf16[2,8,72,128]{3,2,1,0:T(8,128)(2,1)S(1)}, bf16[2,8,72,128]{3,2,1,0:T(8,128)(2,1)S(1)}, u32[]{:S(2)}, u32[]{:S(2)}) collective-permute-start(bf16[2,8,72,128]{3,2,1,0:T(8,128)(2,1)S(1)} %bitcast.15), channel_id=1, source_target_pairs={{0,2},{1,3},{2,0},{3,1},{4,6},{5,7},{6,4},{7,5},{8,10},{9,11},{10,... | collective-permute-start | bytes 884744 | tf_op jit(solution)/shard_map/ppermute | solution.py:170
  31.0 0.8 %collective-permute-start.8 = (bf16[2,8,72,128]{3,2,1,0:T(8,128)(2,1)S(1)}, bf16[2,8,72,128]{3,2,1,0:T(8,128)(2,1)S(1)}, u32[]{:S(2)}, u32[]{:S(2)}) collective-permute-start(bf16[2,8,72,128]{3,2,1,0:T(8,128)(2,1)S(1)} %bitcast.16), channel_id=1, source_target_pairs={{0,3},{1,2},{2,1},{3,0},{4,7},{5,6},{6,5},{7,4},{8,11},{9,10},{10,... | collective-permute-start | bytes 884744 | tf_op jit(solution)/shard_map/ppermute | solution.py:170
  31.8 0.0 collective-permute-start.7
  31.8 0.0 collective-permute-done.2.left_ref
  31.8 0.0 collective-permute-done.3.right_ref
  31.8 0.0 copy-done
  31.8 0.0 copy-done.1
  31.8 0.0 copy-done.3
  31.8 5.0 %shard_map.56.a_ref = bf16[64,1536]{1,0:T(8,128)(2,1)S(1)} custom-call(s32[4]{0:T(128)S(1)} %pad_add_fusion.1.place_ref, bf16[64,1536]{1,0:T(8,128)(2,1)S(1)} %bitcast.28, bf16[64,1536]{1,0:T(8,128)(2,1)S(1)} %bitcast.20, bf16[64,1536]{1,0:T(8,128)(2,1)S(1)} %bitcast.22, bf16[96,1536]{1,0:T(8,128)(2,1)S(1)} %bitcast.27, bf16[96,1536]{1,0:T(8,128)(2,1)S(1)} %bitcast.25, ...), custom_call_target="tpu_custom_call" | custom-call | flops 49999998976 | bytes 4194304 | tf_op jit(solution)/shard_map/pallas_call | solution.py:174
  36.8 1.0 %collective-permute-start.4 = (bf16[64,1536]{1,0:T(8,128)(2,1)S(1)}, bf16[64,1536]{1,0:T(8,128)(2,1)S(1)}, u32[]{:S(2)}, u32[]{:S(2)}) collective-permute-start(bf16[64,1536]{1,0:T(8,128)(2,1)S(1)} %shard_map.56.a_ref), channel_id=1, source_target_pairs={{0,16},{16,0},{1,17},{17,1},{2,18},{18,2},{3,19},{19,3},{4,20},{20... | collective-permute-start | bytes 589832 | tf_op jit(solution)/shard_map/ppermute | solution.py:178
  37.8 0.8 %collective-permute-start.5 = (bf16[64,1536]{1,0:T(8,128)(2,1)S(1)}, bf16[64,1536]{1,0:T(8,128)(2,1)S(1)}, u32[]{:S(2)}, u32[]{:S(2)}) collective-permute-start(bf16[64,1536]{1,0:T(8,128)(2,1)S(1)} %shard_map.56.a_ref), channel_id=1, source_target_pairs={{0,8},{8,0},{1,9},{9,1},{2,10},{10,2},{3,11},{11,3},{4,12},{12,4},... | collective-permute-start | bytes 589832 | tf_op jit(solution)/shard_map/ppermute | solution.py:179
  38.6 3.1 %collective-permute-done.4.b_ref = bf16[64,1536]{1,0:T(8,128)(2,1)S(1)} collective-permute-done((bf16[64,1536]{1,0:T(8,128)(2,1)S(1)}, bf16[64,1536]{1,0:T(8,128)(2,1)S(1)}, u32[]{:S(2)}, u32[]{:S(2)}) %collective-permute-start.4) | collective-permute-done | bytes 196640 | tf_op jit(solution)/shard_map/ppermute | solution.py:178
  41.7 2.5 %collective-permute-start.6 = (bf16[64,1536]{1,0:T(8,128)(2,1)S(1)}, bf16[64,1536]{1,0:T(8,128)(2,1)S(1)}, u32[]{:S(2)}, u32[]{:S(2)}) collective-permute-start(bf16[64,1536]{1,0:T(8,128)(2,1)S(1)} %collective-permute-done.4.b_ref), channel_id=1, source_target_pairs={{0,8},{8,0},{1,9},{9,1},{2,10},{10,2},{3,11},{11,3},{4,12},{12,4},... | collective-permute-start | bytes 589832 | tf_op jit(solution)/shard_map/ppermute | solution.py:180
  44.2 0.0 collective-permute-done.9.w2_ref
  44.2 0.6 %collective-permute-done.8.w3_ref = bf16[2,8,72,128]{3,2,1,0:T(8,128)(2,1)S(1)} collective-permute-done((bf16[2,8,72,128]{3,2,1,0:T(8,128)(2,1)S(1)}, bf16[2,8,72,128]{3,2,1,0:T(8,128)(2,1)S(1)}, u32[]{:S(2)}, u32[]{:S(2)}) %collective-permute-start.8) | collective-permute-done | bytes 294944 | tf_op jit(solution)/shard_map/ppermute | solution.py:170
  44.8 0.0 collective-permute-done.7.w1_ref
  44.8 0.2 shard_map.58.w_ref
  45.0 0.0 collective-permute-done.5.c_ref
  45.1 0.2 collective-permute-done.6.d_ref
  45.3 0.9 %shard_map.59 = (bf16[64,384]{1,0:T(8,128)(2,1)S(1)}, bf16[64,384]{1,0:T(8,128)(2,1)S(1)}, bf16[64,384]{1,0:T(8,128)(2,1)S(1)}, bf16[64,384]{1,0:T(8,128)(2,1)S(1)}) custom-call(s32[1]{0:T(128)} %bitcast.2.y_ref, bf16[64,1536]{1,0:T(8,128)(2,1)S(1)} %shard_map.56.a_ref, bf16[64,1536]{1,0:T(8,128)(2,1)S(1)} %collective-permute-done.4.b_ref, ...), custom_call_target="tpu_custom_call" | custom-call | tf_op jit(solution)/shard_map/pallas_call | solution.py:184
  46.2 0.7 %collective-permute-start.10 = (bf16[64,384]{1,0:T(8,128)(2,1)S(1)}, bf16[64,384]{1,0:T(8,128)(2,1)S(1)}, u32[]{:S(2)}, u32[]{:S(2)}) collective-permute-start(bf16[64,384]{1,0:T(8,128)(2,1)S(1)} %get-tuple-element.14), channel_id=1, source_target_pairs={{0,8},{8,0},{1,9},{9,1},{2,10},{10,2},{3,11},{11,3},{4,12},{12,4},... | collective-permute-start | bytes 147464 | tf_op jit(solution)/shard_map/ppermute | solution.py:187
  46.9 0.9 %collective-permute-start.11 = (bf16[64,384]{1,0:T(8,128)(2,1)S(1)}, bf16[64,384]{1,0:T(8,128)(2,1)S(1)}, u32[]{:S(2)}, u32[]{:S(2)}) collective-permute-start(bf16[64,384]{1,0:T(8,128)(2,1)S(1)} %get-tuple-element.15), channel_id=1, source_target_pairs={{0,16},{16,0},{1,17},{17,1},{2,18},{18,2},{3,19},{19,3},{4,20},{20... | collective-permute-start | bytes 147464 | tf_op jit(solution)/shard_map/ppermute | solution.py:188
  47.8 0.8 %collective-permute-start.12 = (bf16[64,384]{1,0:T(8,128)(2,1)S(1)}, bf16[64,384]{1,0:T(8,128)(2,1)S(1)}, u32[]{:S(2)}, u32[]{:S(2)}) collective-permute-start(bf16[64,384]{1,0:T(8,128)(2,1)S(1)} %get-tuple-element.16), channel_id=1, source_target_pairs={{0,24},{8,16},{16,8},{24,0},{1,25},{9,17},{17,9},{25,1},{2,26},{10... | collective-permute-start | bytes 147464 | tf_op jit(solution)/shard_map/ppermute | solution.py:189
  48.6 0.1 pad_add_fusion.at_ref
  48.7 0.0 collective-permute-done.10.core_ref
  48.7 1.1 %collective-permute-done.11.chip_ref = bf16[64,384]{1,0:T(8,128)(2,1)S(1)} collective-permute-done((bf16[64,384]{1,0:T(8,128)(2,1)S(1)}, bf16[64,384]{1,0:T(8,128)(2,1)S(1)}, u32[]{:S(2)}, u32[]{:S(2)}) %collective-permute-start.11) | collective-permute-done | bytes 49184 | tf_op jit(solution)/shard_map/ppermute | solution.py:188
  49.9 1.7 %collective-permute-done.12.both_ref = bf16[64,384]{1,0:T(8,128)(2,1)S(1)} collective-permute-done((bf16[64,384]{1,0:T(8,128)(2,1)S(1)}, bf16[64,384]{1,0:T(8,128)(2,1)S(1)}, u32[]{:S(2)}, u32[]{:S(2)}) %collective-permute-start.12) | collective-permute-done | bytes 49184 | tf_op jit(solution)/shard_map/ppermute | solution.py:189
  51.6 1.5 %shard_map.60 = bf16[64,1536]{1,0:T(8,128)(2,1)} custom-call(s32[2]{0:T(128)S(1)} %pad_add_fusion.at_ref, bf16[64,384]{1,0:T(8,128)(2,1)S(1)} %get-tuple-element.13.keep_ref, bf16[64,384]{1,0:T(8,128)(2,1)S(1)} %collective-permute-done.10.core_ref, bf16[64,384]{1,0:T(8,128)(2,1)S(1)} %collective-permute-done.11.chip_ref, ...), custom_call_target="tpu_custom_call" | custom-call | tf_op jit(solution)/shard_map/pallas_call | solution.py:191
  (2 shorter events, 0.0 us)
Async XLA Ops:
  1.2 15.0 %collective-permute-start.1 = (bf16[2,48,1536]{2,1,0:T(8,128)(2,1)S(1)}, bf16[2,48,1536]{2,1,0:T(8,128)(2,1)S(1)}, u32[]{:S(2)}, u32[]{:S(2)}) collective-permute-start(bf16[2,48,1536]{2,1,0:T(8,128)(2,1)S(1)} %get-tuple-element.17.up_ref), channel_id=1, source_target_pairs={{0,248},{8,0},{16,8},{24,16},{32,24},{40,32},{48,40},{56,48},{64,5... | collective-permute-start | bytes 884744 | tf_op jit(solution)/shard_map/ppermute | solution.py:163
  4.5 11.6 %collective-permute-start = (bf16[2,48,1536]{2,1,0:T(8,128)(2,1)S(1)}, bf16[2,48,1536]{2,1,0:T(8,128)(2,1)S(1)}, u32[]{:S(2)}, u32[]{:S(2)}) collective-permute-start(bf16[2,48,1536]{2,1,0:T(8,128)(2,1)S(1)} %get-tuple-element.18.down_ref), channel_id=1, source_target_pairs={{0,8},{8,16},{16,24},{24,32},{32,40},{40,48},{48,56},{56,64},{64,7... | collective-permute-start | bytes 884744 | tf_op jit(solution)/shard_map/ppermute | solution.py:162
  4.5 0.7 %copy-start.2 = (bf16[192,48]{0,1:T(8,128)(2,1)S(1)}, bf16[192,48]{0,1:T(8,128)(2,1)}, u32[]{:S(2)}) copy-start(bf16[192,48]{0,1:T(8,128)(2,1)} %param.9) | copy-start | bytes 55300
  6.0 22.0 %all-to-all-start = ((bf16[16,72,128]{2,1,0:T(8,128)(2,1)}), bf16[16,72,128]{2,1,0:T(8,128)(2,1)S(1)}, u32[]{:S(2)}, u32[]{:S(2)}) async-start(bf16[16,72,128]{2,1,0:T(8,128)(2,1)} %shard_map.57), calls=%async_computation | async-start | bytes 589824 | tf_op jit(solution)/shard_map/all_to_all | solution.py:158
  16.1 5.8 %copy-start.4 = (f32[24,49]{1,0:T(8,128)S(1)}, f32[24,49]{1,0:T(8,128)}, u32[]{:S(2)}) copy-start(f32[24,49]{1,0:T(8,128)} %param.8) | copy-start | bytes 14116
  16.2 15.6 %copy-start = (bf16[1,4,16,1536]{3,2,1,0:T(8,128)(2,1)S(1)}, bf16[1,4,16,1536]{3,2,1,0:T(8,128)(2,1)}, u32[]{:S(2)}) copy-start(bf16[1,4,16,1536]{3,2,1,0:T(8,128)(2,1)} %param.6) | copy-start | bytes 589828
  16.2 15.6 %copy-start.1 = (bf16[1,4,16,1536]{3,2,1,0:T(8,128)(2,1)S(1)}, bf16[1,4,16,1536]{3,2,1,0:T(8,128)(2,1)}, u32[]{:S(2)}) copy-start(bf16[1,4,16,1536]{3,2,1,0:T(8,128)(2,1)} %param.7) | copy-start | bytes 589828
  16.2 15.6 %copy-start.3 = (bf16[1,4,16,1536]{3,2,1,0:T(8,128)(2,1)S(1)}, bf16[1,4,16,1536]{3,2,1,0:T(8,128)(2,1)}, u32[]{:S(2)}) copy-start(bf16[1,4,16,1536]{3,2,1,0:T(8,128)(2,1)} %param.5) | copy-start | bytes 589828
  16.5 15.3 %collective-permute-start.2 = (bf16[64,1536]{1,0:T(8,128)(2,1)S(1)}, bf16[64,1536]{1,0:T(8,128)(2,1)S(1)}, u32[]{:S(2)}, u32[]{:S(2)}) collective-permute-start(bf16[64,1536]{1,0:T(8,128)(2,1)S(1)} %get-tuple-element.11), channel_id=1, source_target_pairs={{0,1},{1,2},{2,3},{3,4},{4,5},{5,6},{6,7},{7,0},{8,9},{9,10},{10,1... | collective-permute-start | bytes 589832 | tf_op jit(solution)/shard_map/ppermute | solution.py:166
  17.9 13.9 %collective-permute-start.3 = (bf16[64,1536]{1,0:T(8,128)(2,1)S(1)}, bf16[64,1536]{1,0:T(8,128)(2,1)S(1)}, u32[]{:S(2)}, u32[]{:S(2)}) collective-permute-start(bf16[64,1536]{1,0:T(8,128)(2,1)S(1)} %get-tuple-element.12), channel_id=1, source_target_pairs={{0,7},{1,0},{2,1},{3,2},{4,3},{5,4},{6,5},{7,6},{8,15},{9,8},{10,9... | collective-permute-start | bytes 589832 | tf_op jit(solution)/shard_map/ppermute | solution.py:167
  28.1 16.2 %collective-permute-start.9 = (bf16[2,8,72,128]{3,2,1,0:T(8,128)(2,1)S(1)}, bf16[2,8,72,128]{3,2,1,0:T(8,128)(2,1)S(1)}, u32[]{:S(2)}, u32[]{:S(2)}) collective-permute-start(bf16[2,8,72,128]{3,2,1,0:T(8,128)(2,1)S(1)} %bitcast.15), channel_id=1, source_target_pairs={{0,2},{1,3},{2,0},{3,1},{4,6},{5,7},{6,4},{7,5},{8,10},{9,11},{10,... | collective-permute-start | bytes 884744 | tf_op jit(solution)/shard_map/ppermute | solution.py:170
  31.0 13.8 %collective-permute-start.8 = (bf16[2,8,72,128]{3,2,1,0:T(8,128)(2,1)S(1)}, bf16[2,8,72,128]{3,2,1,0:T(8,128)(2,1)S(1)}, u32[]{:S(2)}, u32[]{:S(2)}) collective-permute-start(bf16[2,8,72,128]{3,2,1,0:T(8,128)(2,1)S(1)} %bitcast.16), channel_id=1, source_target_pairs={{0,3},{1,2},{2,1},{3,0},{4,7},{5,6},{6,5},{7,4},{8,11},{9,10},{10,... | collective-permute-start | bytes 884744 | tf_op jit(solution)/shard_map/ppermute | solution.py:170
  31.8 13.1 %collective-permute-start.7 = (bf16[2,8,72,128]{3,2,1,0:T(8,128)(2,1)S(1)}, bf16[2,8,72,128]{3,2,1,0:T(8,128)(2,1)S(1)}, u32[]{:S(2)}, u32[]{:S(2)}) collective-permute-start(bf16[2,8,72,128]{3,2,1,0:T(8,128)(2,1)S(1)} %bitcast.17), channel_id=1, source_target_pairs={{0,1},{1,0},{2,3},{3,2},{4,5},{5,4},{6,7},{7,6},{8,9},{9,8},{10,11... | collective-permute-start | bytes 884744 | tf_op jit(solution)/shard_map/ppermute | solution.py:170
  36.8 4.9 %collective-permute-start.4 = (bf16[64,1536]{1,0:T(8,128)(2,1)S(1)}, bf16[64,1536]{1,0:T(8,128)(2,1)S(1)}, u32[]{:S(2)}, u32[]{:S(2)}) collective-permute-start(bf16[64,1536]{1,0:T(8,128)(2,1)S(1)} %shard_map.56.a_ref), channel_id=1, source_target_pairs={{0,16},{16,0},{1,17},{17,1},{2,18},{18,2},{3,19},{19,3},{4,20},{20... | collective-permute-start | bytes 589832 | tf_op jit(solution)/shard_map/ppermute | solution.py:178
  37.8 7.2 %collective-permute-start.5 = (bf16[64,1536]{1,0:T(8,128)(2,1)S(1)}, bf16[64,1536]{1,0:T(8,128)(2,1)S(1)}, u32[]{:S(2)}, u32[]{:S(2)}) collective-permute-start(bf16[64,1536]{1,0:T(8,128)(2,1)S(1)} %shard_map.56.a_ref), channel_id=1, source_target_pairs={{0,8},{8,0},{1,9},{9,1},{2,10},{10,2},{3,11},{11,3},{4,12},{12,4},... | collective-permute-start | bytes 589832 | tf_op jit(solution)/shard_map/ppermute | solution.py:179
  41.7 3.6 %collective-permute-start.6 = (bf16[64,1536]{1,0:T(8,128)(2,1)S(1)}, bf16[64,1536]{1,0:T(8,128)(2,1)S(1)}, u32[]{:S(2)}, u32[]{:S(2)}) collective-permute-start(bf16[64,1536]{1,0:T(8,128)(2,1)S(1)} %collective-permute-done.4.b_ref), channel_id=1, source_target_pairs={{0,8},{8,0},{1,9},{9,1},{2,10},{10,2},{3,11},{11,3},{4,12},{12,4},... | collective-permute-start | bytes 589832 | tf_op jit(solution)/shard_map/ppermute | solution.py:180
  46.2 2.5 %collective-permute-start.10 = (bf16[64,384]{1,0:T(8,128)(2,1)S(1)}, bf16[64,384]{1,0:T(8,128)(2,1)S(1)}, u32[]{:S(2)}, u32[]{:S(2)}) collective-permute-start(bf16[64,384]{1,0:T(8,128)(2,1)S(1)} %get-tuple-element.14), channel_id=1, source_target_pairs={{0,8},{8,0},{1,9},{9,1},{2,10},{10,2},{3,11},{11,3},{4,12},{12,4},... | collective-permute-start | bytes 147464 | tf_op jit(solution)/shard_map/ppermute | solution.py:187
  46.9 3.0 %collective-permute-start.11 = (bf16[64,384]{1,0:T(8,128)(2,1)S(1)}, bf16[64,384]{1,0:T(8,128)(2,1)S(1)}, u32[]{:S(2)}, u32[]{:S(2)}) collective-permute-start(bf16[64,384]{1,0:T(8,128)(2,1)S(1)} %get-tuple-element.15), channel_id=1, source_target_pairs={{0,16},{16,0},{1,17},{17,1},{2,18},{18,2},{3,19},{19,3},{4,20},{20... | collective-permute-start | bytes 147464 | tf_op jit(solution)/shard_map/ppermute | solution.py:188
  47.8 3.7 %collective-permute-start.12 = (bf16[64,384]{1,0:T(8,128)(2,1)S(1)}, bf16[64,384]{1,0:T(8,128)(2,1)S(1)}, u32[]{:S(2)}, u32[]{:S(2)}) collective-permute-start(bf16[64,384]{1,0:T(8,128)(2,1)S(1)} %get-tuple-element.16), channel_id=1, source_target_pairs={{0,24},{8,16},{16,8},{24,0},{1,25},{9,17},{17,9},{25,1},{2,26},{10... | collective-permute-start | bytes 147464 | tf_op jit(solution)/shard_map/ppermute | solution.py:189

commit v7 on v6

--- a/solution.py
+++ b/solution.py
@@ -94,7 +94,7 @@
         o_ref[:, c] = jnp.where(low, o[:64], o[64:]).astype(BF)
 
 
-def unpack_kernel(w0_ref, w1_ref, w3_ref, w2_ref, out_ref):
+def unpack_kernel(w0_ref, w3_ref, w1_ref, w2_ref, out_ref):
     for xh in range(2):
         for k, w_ref in enumerate((w0_ref, w1_ref, w2_ref, w3_ref)):
             for z in range(8):
@@ -167,7 +167,7 @@
     from_right = lax.ppermute(to_left, cols, left)
 
     near = along_zx.reshape(2, 8, 72, 128)
-    stages = [near] + [lax.ppermute(near, "y", [(n, n ^ k) for n in range(4)]) for k in (1, 3, 2)]
+    stages = [near] + [lax.ppermute(near, "y", [(n, n ^ k) for n in range(4)]) for k in (3, 1, 2)]
 
     place = jnp.stack([r * 4, c * 16, nr * 4, nc * 16]).astype(jnp.int32)
     bias = jnp.pad(position_bias, ((0, 0), (0, 128 - 49)), constant_values=-jnp.inf)

time: 53.3 us -> 53.3 us (level)
  no operation moved by 1% of the time
where the time goes in v7:
time: 53.3 us; the launch traced here: 53 us
  starting transfers between devices  29.4 us (55%)
  waiting for transfers between devices  12.8 us (24%)
  Pallas kernels  8.64 us (16%)
  other arithmetic  1.31 us (2%)
  local copies, waits for them, and re-layouts  0.77 us (1%)
    all_to_all x1, starting transfers between devices, shards(): along_zx = lax.all_to_all(packed, ('xh', 'z'), 0, 0, tiled=True)  10.1 us
    all_to_all x1, waiting for transfers between devices, shards(): along_zx = lax.all_to_all(packed, ('xh', 'z'), 0, 0, tiled=True)  6.01 us
    pallas_call x1, Pallas kernels, shards(): call(attention_kernel, side, 9, smem=(0,), flops=50000000000)  5.02 us
    ppermute x1, starting transfers between devices, shards(): from_right = lax.ppermute(to_left, cols, left)  4.11 us
    ppermute x3, starting transfers between devices, shards(): lax.ppermute(near, 'y', [(n, n ^ k) for n in range(4)])  3.69 us
    ppermute x1, starting transfers between devices, shards(): bot = lax.ppermute(to_up, rows, up).reshape(96, width)  3.32 us
    ppermute x1, waiting for transfers between devices, shards(): next_mixed = lax.ppermute(mixed, 'xl', swap)  3.1 us
    ppermute x1, starting transfers between devices, shards(): both_mixed = lax.ppermute(next_mixed, 'core', swap)  2.5 us
  transfers between devices with their start and end apart: 14, of which 6 were waited for; matrix products, arithmetic and copies ran while one was open for 0% of the time, Pallas kernels for 12%

profile of v7, /device:TPU:1, one launch (start us, length us, event | category | flops | bytes accessed | tf_op | source)
XLA Modules:
  0.0 53.0 jit_solution(12446704619064933821)
XLA Ops:
  0.0 1.2 %pad_maximum_fusion = (bf16[2,48,1536]{2,1,0:T(8,128)(2,1)S(1)}, bf16[2,48,1536]{2,1,0:T(8,128)(2,1)S(1)}) fusion(bf16[1,64,1536]{2,1,0:T(8,128)(2,1)} %bitcast.21, bf16[1,64,1536]{2,1,0:T(8,128)(2,1)} %bitcast.19), kind=kLoop, calls=%fused_computation.3 | loop fusion | flops 1179648 | bytes 983040 | tf_op jit(solution)/shard_map/stack | solution.py:160
  1.2 3.3 %collective-permute-start.1 = (bf16[2,48,1536]{2,1,0:T(8,128)(2,1)S(1)}, bf16[2,48,1536]{2,1,0:T(8,128)(2,1)S(1)}, u32[]{:S(2)}, u32[]{:S(2)}) collective-permute-start(bf16[2,48,1536]{2,1,0:T(8,128)(2,1)S(1)} %get-tuple-element.17.up_ref), channel_id=1, source_target_pairs={{0,248},{8,0},{16,8},{24,16},{32,24},{40,32},{48,40},{56,48},{64,5... | collective-permute-start | bytes 884744 | tf_op jit(solution)/shard_map/ppermute | solution.py:163
  4.5 0.0 collective-permute-start
  4.5 0.0 copy-start.2
  4.5 0.7 %copy-done.2 = bf16[192,48]{0,1:T(8,128)(2,1)S(1)} copy-done((bf16[192,48]{0,1:T(8,128)(2,1)S(1)}, bf16[192,48]{0,1:T(8,128)(2,1)}, u32[]{:S(2)}) %copy-start.2) | copy-done | bytes 18456
  5.2 0.8 %shard_map.57 = bf16[16,72,128]{2,1,0:T(8,128)(2,1)} custom-call(bf16[48,192]{1,0:T(8,128)(2,1)S(1)} %bitcast.23), custom_call_target="tpu_custom_call" | custom-call | tf_op jit(solution)/shard_map/pallas_call | solution.py:157
  6.0 10.1 %all-to-all-start = ((bf16[16,72,128]{2,1,0:T(8,128)(2,1)}), bf16[16,72,128]{2,1,0:T(8,128)(2,1)S(1)}, u32[]{:S(2)}, u32[]{:S(2)}) async-start(bf16[16,72,128]{2,1,0:T(8,128)(2,1)} %shard_map.57), calls=%async_computation | async-start | bytes 589824 | tf_op jit(solution)/shard_map/all_to_all | solution.py:158
  16.1 0.0 collective-permute-done.1
  16.1 0.0 collective-permute-done
  16.1 0.0 copy-start.4
  16.2 0.0 copy-start
  16.2 0.0 copy-start.1
  16.2 0.0 copy-start.3
  16.2 0.3 shard_map.55
  16.5 1.4 %collective-permute-start.2 = (bf16[64,1536]{1,0:T(8,128)(2,1)S(1)}, bf16[64,1536]{1,0:T(8,128)(2,1)S(1)}, u32[]{:S(2)}, u32[]{:S(2)}) collective-permute-start(bf16[64,1536]{1,0:T(8,128)(2,1)S(1)} %get-tuple-element.11), channel_id=1, source_target_pairs={{0,1},{1,2},{2,3},{3,4},{4,5},{5,6},{6,7},{7,0},{8,9},{9,10},{10,1... | collective-permute-start | bytes 589832 | tf_op jit(solution)/shard_map/ppermute | solution.py:166
  17.9 4.1 %collective-permute-start.3 = (bf16[64,1536]{1,0:T(8,128)(2,1)S(1)}, bf16[64,1536]{1,0:T(8,128)(2,1)S(1)}, u32[]{:S(2)}, u32[]{:S(2)}) collective-permute-start(bf16[64,1536]{1,0:T(8,128)(2,1)S(1)} %get-tuple-element.12), channel_id=1, source_target_pairs={{0,7},{1,0},{2,1},{3,2},{4,3},{5,4},{6,5},{7,6},{8,15},{9,8},{10,9... | collective-permute-start | bytes 589832 | tf_op jit(solution)/shard_map/ppermute | solution.py:167
  22.0 0.0 copy-done.4
  22.0 0.1 pad_add_fusion.1.place_ref
  22.1 6.0 %all-to-all-done = bf16[16,72,128]{2,1,0:T(8,128)(2,1)S(1)} async-done(((bf16[16,72,128]{2,1,0:T(8,128)(2,1)}), bf16[16,72,128]{2,1,0:T(8,128)(2,1)S(1)}, u32[]{:S(2)}, u32[]{:S(2)}) %all-to-all-start) | async-done | bytes 294944 | tf_op jit(solution)/shard_map/all_to_all | solution.py:158
  28.1 2.9 %collective-permute-start.9 = (bf16[2,8,72,128]{3,2,1,0:T(8,128)(2,1)S(1)}, bf16[2,8,72,128]{3,2,1,0:T(8,128)(2,1)S(1)}, u32[]{:S(2)}, u32[]{:S(2)}) collective-permute-start(bf16[2,8,72,128]{3,2,1,0:T(8,128)(2,1)S(1)} %bitcast.15), channel_id=1, source_target_pairs={{0,2},{1,3},{2,0},{3,1},{4,6},{5,7},{6,4},{7,5},{8,10},{9,11},{10,... | collective-permute-start | bytes 884744 | tf_op jit(solution)/shard_map/ppermute | solution.py:170
  31.0 0.4 collective-permute-start.8
  31.4 0.4 collective-permute-start.7
  31.8 0.0 collective-permute-done.2.left_ref
  31.8 0.0 collective-permute-done.3.right_ref
  31.8 0.0 copy-done
  31.8 0.0 copy-done.1
  31.8 0.0 copy-done.3
  31.8 5.0 %shard_map.56.a_ref = bf16[64,1536]{1,0:T(8,128)(2,1)S(1)} custom-call(s32[4]{0:T(128)S(1)} %pad_add_fusion.1.place_ref, bf16[64,1536]{1,0:T(8,128)(2,1)S(1)} %bitcast.28, bf16[64,1536]{1,0:T(8,128)(2,1)S(1)} %bitcast.20, bf16[64,1536]{1,0:T(8,128)(2,1)S(1)} %bitcast.22, bf16[96,1536]{1,0:T(8,128)(2,1)S(1)} %bitcast.27, bf16[96,1536]{1,0:T(8,128)(2,1)S(1)} %bitcast.25, ...), custom_call_target="tpu_custom_call" | custom-call | flops 49999998976 | bytes 4194304 | tf_op jit(solution)/shard_map/pallas_call | solution.py:174
  36.8 1.0 %collective-permute-start.4 = (bf16[64,1536]{1,0:T(8,128)(2,1)S(1)}, bf16[64,1536]{1,0:T(8,128)(2,1)S(1)}, u32[]{:S(2)}, u32[]{:S(2)}) collective-permute-start(bf16[64,1536]{1,0:T(8,128)(2,1)S(1)} %shard_map.56.a_ref), channel_id=1, source_target_pairs={{0,16},{16,0},{1,17},{17,1},{2,18},{18,2},{3,19},{19,3},{4,20},{20... | collective-permute-start | bytes 589832 | tf_op jit(solution)/shard_map/ppermute | solution.py:178
  37.8 0.8 %collective-permute-start.5 = (bf16[64,1536]{1,0:T(8,128)(2,1)S(1)}, bf16[64,1536]{1,0:T(8,128)(2,1)S(1)}, u32[]{:S(2)}, u32[]{:S(2)}) collective-permute-start(bf16[64,1536]{1,0:T(8,128)(2,1)S(1)} %shard_map.56.a_ref), channel_id=1, source_target_pairs={{0,8},{8,0},{1,9},{9,1},{2,10},{10,2},{3,11},{11,3},{4,12},{12,4},... | collective-permute-start | bytes 589832 | tf_op jit(solution)/shard_map/ppermute | solution.py:179
  38.6 3.1 %collective-permute-done.4.b_ref = bf16[64,1536]{1,0:T(8,128)(2,1)S(1)} collective-permute-done((bf16[64,1536]{1,0:T(8,128)(2,1)S(1)}, bf16[64,1536]{1,0:T(8,128)(2,1)S(1)}, u32[]{:S(2)}, u32[]{:S(2)}) %collective-permute-start.4) | collective-permute-done | bytes 196640 | tf_op jit(solution)/shard_map/ppermute | solution.py:178
  41.7 2.5 %collective-permute-start.6 = (bf16[64,1536]{1,0:T(8,128)(2,1)S(1)}, bf16[64,1536]{1,0:T(8,128)(2,1)S(1)}, u32[]{:S(2)}, u32[]{:S(2)}) collective-permute-start(bf16[64,1536]{1,0:T(8,128)(2,1)S(1)} %collective-permute-done.4.b_ref), channel_id=1, source_target_pairs={{0,8},{8,0},{1,9},{9,1},{2,10},{10,2},{3,11},{11,3},{4,12},{12,4},... | collective-permute-start | bytes 589832 | tf_op jit(solution)/shard_map/ppermute | solution.py:180
  44.2 0.0 collective-permute-done.9.w2_ref
  44.2 0.0 collective-permute-done.8.w1_ref
  44.2 0.5 collective-permute-done.7.w3_ref
  44.7 0.2 shard_map.58.w_ref
  44.9 0.0 collective-permute-done.5.c_ref
  45.0 0.3 collective-permute-done.6.d_ref
  45.3 0.9 %shard_map.59 = (bf16[64,384]{1,0:T(8,128)(2,1)S(1)}, bf16[64,384]{1,0:T(8,128)(2,1)S(1)}, bf16[64,384]{1,0:T(8,128)(2,1)S(1)}, bf16[64,384]{1,0:T(8,128)(2,1)S(1)}) custom-call(s32[1]{0:T(128)} %bitcast.2.y_ref, bf16[64,1536]{1,0:T(8,128)(2,1)S(1)} %shard_map.56.a_ref, bf16[64,1536]{1,0:T(8,128)(2,1)S(1)} %collective-permute-done.4.b_ref, ...), custom_call_target="tpu_custom_call" | custom-call | tf_op jit(solution)/shard_map/pallas_call | solution.py:184
  46.2 0.7 %collective-permute-start.10 = (bf16[64,384]{1,0:T(8,128)(2,1)S(1)}, bf16[64,384]{1,0:T(8,128)(2,1)S(1)}, u32[]{:S(2)}, u32[]{:S(2)}) collective-permute-start(bf16[64,384]{1,0:T(8,128)(2,1)S(1)} %get-tuple-element.14), channel_id=1, source_target_pairs={{0,8},{8,0},{1,9},{9,1},{2,10},{10,2},{3,11},{11,3},{4,12},{12,4},... | collective-permute-start | bytes 147464 | tf_op jit(solution)/shard_map/ppermute | solution.py:187
  46.9 0.9 %collective-permute-start.11 = (bf16[64,384]{1,0:T(8,128)(2,1)S(1)}, bf16[64,384]{1,0:T(8,128)(2,1)S(1)}, u32[]{:S(2)}, u32[]{:S(2)}) collective-permute-start(bf16[64,384]{1,0:T(8,128)(2,1)S(1)} %get-tuple-element.15), channel_id=1, source_target_pairs={{0,16},{16,0},{1,17},{17,1},{2,18},{18,2},{3,19},{19,3},{4,20},{20... | collective-permute-start | bytes 147464 | tf_op jit(solution)/shard_map/ppermute | solution.py:188
  47.8 0.8 %collective-permute-start.12 = (bf16[64,384]{1,0:T(8,128)(2,1)S(1)}, bf16[64,384]{1,0:T(8,128)(2,1)S(1)}, u32[]{:S(2)}, u32[]{:S(2)}) collective-permute-start(bf16[64,384]{1,0:T(8,128)(2,1)S(1)} %get-tuple-element.16), channel_id=1, source_target_pairs={{0,24},{8,16},{16,8},{24,0},{1,25},{9,17},{17,9},{25,1},{2,26},{10... | collective-permute-start | bytes 147464 | tf_op jit(solution)/shard_map/ppermute | solution.py:189
  48.6 0.1 pad_add_fusion.at_ref
  48.7 0.0 collective-permute-done.10.core_ref
  48.7 1.1 %collective-permute-done.11.chip_ref = bf16[64,384]{1,0:T(8,128)(2,1)S(1)} collective-permute-done((bf16[64,384]{1,0:T(8,128)(2,1)S(1)}, bf16[64,384]{1,0:T(8,128)(2,1)S(1)}, u32[]{:S(2)}, u32[]{:S(2)}) %collective-permute-start.11) | collective-permute-done | bytes 49184 | tf_op jit(solution)/shard_map/ppermute | solution.py:188
  49.9 1.7 %collective-permute-done.12.both_ref = bf16[64,384]{1,0:T(8,128)(2,1)S(1)} collective-permute-done((bf16[64,384]{1,0:T(8,128)(2,1)S(1)}, bf16[64,384]{1,0:T(8,128)(2,1)S(1)}, u32[]{:S(2)}, u32[]{:S(2)}) %collective-permute-start.12) | collective-permute-done | bytes 49184 | tf_op jit(solution)/shard_map/ppermute | solution.py:189
  51.6 1.5 %shard_map.60 = bf16[64,1536]{1,0:T(8,128)(2,1)} custom-call(s32[2]{0:T(128)S(1)} %pad_add_fusion.at_ref, bf16[64,384]{1,0:T(8,128)(2,1)S(1)} %get-tuple-element.13.keep_ref, bf16[64,384]{1,0:T(8,128)(2,1)S(1)} %collective-permute-done.10.core_ref, bf16[64,384]{1,0:T(8,128)(2,1)S(1)} %collective-permute-done.11.chip_ref, ...), custom_call_target="tpu_custom_call" | custom-call | tf_op jit(solution)/shard_map/pallas_call | solution.py:191
  (2 shorter events, 0.0 us)
Async XLA Ops:
  1.2 15.0 %collective-permute-start.1 = (bf16[2,48,1536]{2,1,0:T(8,128)(2,1)S(1)}, bf16[2,48,1536]{2,1,0:T(8,128)(2,1)S(1)}, u32[]{:S(2)}, u32[]{:S(2)}) collective-permute-start(bf16[2,48,1536]{2,1,0:T(8,128)(2,1)S(1)} %get-tuple-element.17.up_ref), channel_id=1, source_target_pairs={{0,248},{8,0},{16,8},{24,16},{32,24},{40,32},{48,40},{56,48},{64,5... | collective-permute-start | bytes 884744 | tf_op jit(solution)/shard_map/ppermute | solution.py:163
  4.5 11.6 %collective-permute-start = (bf16[2,48,1536]{2,1,0:T(8,128)(2,1)S(1)}, bf16[2,48,1536]{2,1,0:T(8,128)(2,1)S(1)}, u32[]{:S(2)}, u32[]{:S(2)}) collective-permute-start(bf16[2,48,1536]{2,1,0:T(8,128)(2,1)S(1)} %get-tuple-element.18.down_ref), channel_id=1, source_target_pairs={{0,8},{8,16},{16,24},{24,32},{32,40},{40,48},{48,56},{56,64},{64,7... | collective-permute-start | bytes 884744 | tf_op jit(solution)/shard_map/ppermute | solution.py:162
  4.5 0.7 %copy-start.2 = (bf16[192,48]{0,1:T(8,128)(2,1)S(1)}, bf16[192,48]{0,1:T(8,128)(2,1)}, u32[]{:S(2)}) copy-start(bf16[192,48]{0,1:T(8,128)(2,1)} %param.9) | copy-start | bytes 55300
  6.0 22.0 %all-to-all-start = ((bf16[16,72,128]{2,1,0:T(8,128)(2,1)}), bf16[16,72,128]{2,1,0:T(8,128)(2,1)S(1)}, u32[]{:S(2)}, u32[]{:S(2)}) async-start(bf16[16,72,128]{2,1,0:T(8,128)(2,1)} %shard_map.57), calls=%async_computation | async-start | bytes 589824 | tf_op jit(solution)/shard_map/all_to_all | solution.py:158
  16.1 5.8 %copy-start.4 = (f32[24,49]{1,0:T(8,128)S(1)}, f32[24,49]{1,0:T(8,128)}, u32[]{:S(2)}) copy-start(f32[24,49]{1,0:T(8,128)} %param.8) | copy-start | bytes 14116
  16.2 15.6 %copy-start = (bf16[1,4,16,1536]{3,2,1,0:T(8,128)(2,1)S(1)}, bf16[1,4,16,1536]{3,2,1,0:T(8,128)(2,1)}, u32[]{:S(2)}) copy-start(bf16[1,4,16,1536]{3,2,1,0:T(8,128)(2,1)} %param.6) | copy-start | bytes 589828
  16.2 15.6 %copy-start.1 = (bf16[1,4,16,1536]{3,2,1,0:T(8,128)(2,1)S(1)}, bf16[1,4,16,1536]{3,2,1,0:T(8,128)(2,1)}, u32[]{:S(2)}) copy-start(bf16[1,4,16,1536]{3,2,1,0:T(8,128)(2,1)} %param.7) | copy-start | bytes 589828
  16.2 15.6 %copy-start.3 = (bf16[1,4,16,1536]{3,2,1,0:T(8,128)(2,1)S(1)}, bf16[1,4,16,1536]{3,2,1,0:T(8,128)(2,1)}, u32[]{:S(2)}) copy-start(bf16[1,4,16,1536]{3,2,1,0:T(8,128)(2,1)} %param.5) | copy-start | bytes 589828
  16.5 15.3 %collective-permute-start.2 = (bf16[64,1536]{1,0:T(8,128)(2,1)S(1)}, bf16[64,1536]{1,0:T(8,128)(2,1)S(1)}, u32[]{:S(2)}, u32[]{:S(2)}) collective-permute-start(bf16[64,1536]{1,0:T(8,128)(2,1)S(1)} %get-tuple-element.11), channel_id=1, source_target_pairs={{0,1},{1,2},{2,3},{3,4},{4,5},{5,6},{6,7},{7,0},{8,9},{9,10},{10,1... | collective-permute-start | bytes 589832 | tf_op jit(solution)/shard_map/ppermute | solution.py:166
  17.9 13.9 %collective-permute-start.3 = (bf16[64,1536]{1,0:T(8,128)(2,1)S(1)}, bf16[64,1536]{1,0:T(8,128)(2,1)S(1)}, u32[]{:S(2)}, u32[]{:S(2)}) collective-permute-start(bf16[64,1536]{1,0:T(8,128)(2,1)S(1)} %get-tuple-element.12), channel_id=1, source_target_pairs={{0,7},{1,0},{2,1},{3,2},{4,3},{5,4},{6,5},{7,6},{8,15},{9,8},{10,9... | collective-permute-start | bytes 589832 | tf_op jit(solution)/shard_map/ppermute | solution.py:167
  28.1 16.2 %collective-permute-start.9 = (bf16[2,8,72,128]{3,2,1,0:T(8,128)(2,1)S(1)}, bf16[2,8,72,128]{3,2,1,0:T(8,128)(2,1)S(1)}, u32[]{:S(2)}, u32[]{:S(2)}) collective-permute-start(bf16[2,8,72,128]{3,2,1,0:T(8,128)(2,1)S(1)} %bitcast.15), channel_id=1, source_target_pairs={{0,2},{1,3},{2,0},{3,1},{4,6},{5,7},{6,4},{7,5},{8,10},{9,11},{10,... | collective-permute-start | bytes 884744 | tf_op jit(solution)/shard_map/ppermute | solution.py:170
  31.0 13.2 %collective-permute-start.8 = (bf16[2,8,72,128]{3,2,1,0:T(8,128)(2,1)S(1)}, bf16[2,8,72,128]{3,2,1,0:T(8,128)(2,1)S(1)}, u32[]{:S(2)}, u32[]{:S(2)}) collective-permute-start(bf16[2,8,72,128]{3,2,1,0:T(8,128)(2,1)S(1)} %bitcast.16), channel_id=1, source_target_pairs={{0,1},{1,0},{2,3},{3,2},{4,5},{5,4},{6,7},{7,6},{8,9},{9,8},{10,11... | collective-permute-start | bytes 884744 | tf_op jit(solution)/shard_map/ppermute | solution.py:170
  31.4 13.3 %collective-permute-start.7 = (bf16[2,8,72,128]{3,2,1,0:T(8,128)(2,1)S(1)}, bf16[2,8,72,128]{3,2,1,0:T(8,128)(2,1)S(1)}, u32[]{:S(2)}, u32[]{:S(2)}) collective-permute-start(bf16[2,8,72,128]{3,2,1,0:T(8,128)(2,1)S(1)} %bitcast.17), channel_id=1, source_target_pairs={{0,3},{1,2},{2,1},{3,0},{4,7},{5,6},{6,5},{7,4},{8,11},{9,10},{10,... | collective-permute-start | bytes 884744 | tf_op jit(solution)/shard_map/ppermute | solution.py:170
  36.8 4.9 %collective-permute-start.4 = (bf16[64,1536]{1,0:T(8,128)(2,1)S(1)}, bf16[64,1536]{1,0:T(8,128)(2,1)S(1)}, u32[]{:S(2)}, u32[]{:S(2)}) collective-permute-start(bf16[64,1536]{1,0:T(8,128)(2,1)S(1)} %shard_map.56.a_ref), channel_id=1, source_target_pairs={{0,16},{16,0},{1,17},{17,1},{2,18},{18,2},{3,19},{19,3},{4,20},{20... | collective-permute-start | bytes 589832 | tf_op jit(solution)/shard_map/ppermute | solution.py:178
  37.8 7.1 %collective-permute-start.5 = (bf16[64,1536]{1,0:T(8,128)(2,1)S(1)}, bf16[64,1536]{1,0:T(8,128)(2,1)S(1)}, u32[]{:S(2)}, u32[]{:S(2)}) collective-permute-start(bf16[64,1536]{1,0:T(8,128)(2,1)S(1)} %shard_map.56.a_ref), channel_id=1, source_target_pairs={{0,8},{8,0},{1,9},{9,1},{2,10},{10,2},{3,11},{11,3},{4,12},{12,4},... | collective-permute-start | bytes 589832 | tf_op jit(solution)/shard_map/ppermute | solution.py:179
  41.7 3.6 %collective-permute-start.6 = (bf16[64,1536]{1,0:T(8,128)(2,1)S(1)}, bf16[64,1536]{1,0:T(8,128)(2,1)S(1)}, u32[]{:S(2)}, u32[]{:S(2)}) collective-permute-start(bf16[64,1536]{1,0:T(8,128)(2,1)S(1)} %collective-permute-done.4.b_ref), channel_id=1, source_target_pairs={{0,8},{8,0},{1,9},{9,1},{2,10},{10,2},{3,11},{11,3},{4,12},{12,4},... | collective-permute-start | bytes 589832 | tf_op jit(solution)/shard_map/ppermute | solution.py:180
  46.2 2.5 %collective-permute-start.10 = (bf16[64,384]{1,0:T(8,128)(2,1)S(1)}, bf16[64,384]{1,0:T(8,128)(2,1)S(1)}, u32[]{:S(2)}, u32[]{:S(2)}) collective-permute-start(bf16[64,384]{1,0:T(8,128)(2,1)S(1)} %get-tuple-element.14), channel_id=1, source_target_pairs={{0,8},{8,0},{1,9},{9,1},{2,10},{10,2},{3,11},{11,3},{4,12},{12,4},... | collective-permute-start | bytes 147464 | tf_op jit(solution)/shard_map/ppermute | solution.py:187
  46.9 3.0 %collective-permute-start.11 = (bf16[64,384]{1,0:T(8,128)(2,1)S(1)}, bf16[64,384]{1,0:T(8,128)(2,1)S(1)}, u32[]{:S(2)}, u32[]{:S(2)}) collective-permute-start(bf16[64,384]{1,0:T(8,128)(2,1)S(1)} %get-tuple-element.15), channel_id=1, source_target_pairs={{0,16},{16,0},{1,17},{17,1},{2,18},{18,2},{3,19},{19,3},{4,20},{20... | collective-permute-start | bytes 147464 | tf_op jit(solution)/shard_map/ppermute | solution.py:188
  47.8 3.7 %collective-permute-start.12 = (bf16[64,384]{1,0:T(8,128)(2,1)S(1)}, bf16[64,384]{1,0:T(8,128)(2,1)S(1)}, u32[]{:S(2)}, u32[]{:S(2)}) collective-permute-start(bf16[64,384]{1,0:T(8,128)(2,1)S(1)} %get-tuple-element.16), channel_id=1, source_target_pairs={{0,24},{8,16},{16,8},{24,0},{1,25},{9,17},{17,9},{25,1},{2,26},{10... | collective-permute-start | bytes 147464 | tf_op jit(solution)/shard_map/ppermute | solution.py:189
